TPU v7x, 256 devices: a whole 4x4x8 slice. The times are simulated.
256 devices in a mesh: lon: 32 (over x, y, z_lo), lat: 4 (over z_hi), grp: 2 (over core).
Axes of the slice: x: 4, y: 4, z: 8 (z_hi: 4, z_lo: 2; z = z_hi * 2 + z_lo), core: 2. Of those that a mesh axis runs over, the one named last changes fastest.
Arguments:
- thermal_anomaly: float32 [12, 512, 2048], P(None, ('lon', 'grp'), 'lat'), may hold values from -6 to 6
- saltiness_anomaly: float32 [12, 512, 2048], P(None, ('lon', 'grp'), 'lat'), may hold values from -6 to 6
- zonal_flow_speed: float32 [12, 512, 2048], P(None, ('lon', 'grp'), 'lat'), may hold values from -3 to 3
- meridional_flow_speed: float32 [12, 512, 2048], P(None, ('lon', 'grp'), 'lat'), may hold values from -3 to 3
- water_indicator: int32 [512, 2048], P(('lon', 'grp'), 'lat'), may hold values from 0 to 1
- kernel_factors: float32 [64, 3, 3, 48], replicated, may hold values from -0.3125 to 0.3125
- hidden_pointwise_factors: float32 [64, 64], replicated, may hold values from -0.75 to 0.75
- final_pointwise_factors: float32 [48, 64], replicated, may hold values from -0.75 to 0.75
Outputs:
- temperature_out: float32 [12, 512, 2048], P(None, ('lon', 'grp'), 'lat')
- salinity_out: float32 [12, 512, 2048], P(None, ('lon', 'grp'), 'lat')
- conv_out: float32 [64, 3, 3, 48], replicated
- mix_out: float32 [64, 64], replicated
- out_out: float32 [48, 64], replicated
All inputs are finite; a program needn't handle non-finite values.
Results may differ from a plain program's by a relative error of at most 0.0003.
Values sent between devices are 32-bit elements; how exact they have to be, the bound alone decides.
No kernel may reach another device: no remote copies, remote signals or barrier semaphores. Data moves between devices by JAX's collectives and lax.ppermute only.
A program may use at most 64 MiB of HBM per device.

v0:
```python
import jax
import jax.numpy as jnp
from jax import lax
from jax.sharding import PartitionSpec as P

time_step = 0.2
diffusivity = 0.5
learn_rate = 200.0
highest = lax.Precision.HIGHEST


def with_halo(block, sides, width):
    for axis, dim in sides:
        count = lax.axis_size(axis)
        forward = [(i, i + 1) for i in range(count - 1)]
        forward.append((count - 1, 0))
        backward = [(target, source) for source, target in forward]
        low = lax.ppermute(
            lax.slice_in_dim(block, block.shape[dim] - width, None, axis=dim), axis, forward
        )
        high = lax.ppermute(lax.slice_in_dim(block, 0, width, axis=dim), axis, backward)
        block = jnp.concatenate([low, block, high], axis=dim)
    return block


def clear_rim(padded, width):
    lat_index = lax.axis_index("lat")
    lat_last = lax.axis_size("lat") - 1
    columns = jnp.arange(padded.shape[-1])
    low_rim = (columns < width) & (lat_index == 0)
    high_rim = (columns >= padded.shape[-1] - width) & (lat_index == lat_last)
    return jnp.where(low_rim | high_rim, jnp.zeros((), padded.dtype), padded)


def detailed_haloed_field(stacked):
    return clear_rim(with_halo(stacked, ((("lon", "grp"), 1), ("lat", 2)), 1), 1)


def average_to_blocks(field):
    array_extent = field.shape
    return field.reshape(
        array_extent[:-2] + (array_extent[-2] // 4, 4, array_extent[-1] // 4, 4)
    ).mean(axis=(-3, -1))


def upsample_blocks(field):
    return jnp.repeat(jnp.repeat(field, 4, axis=-2), 4, axis=-1)


def scalar_step_update(
    tracer, haloed_scalar, padded_eastward, padded_northward, padded_land_mask, forcing
):
    west_side = haloed_scalar[..., :-1, 1:-1]
    east_side = haloed_scalar[..., 1:, 1:-1]
    east_flux = (
        padded_land_mask[:-1, 1:-1]
        * padded_land_mask[1:, 1:-1]
        * (
            0.25
            * (padded_eastward[..., :-1, 1:-1] + padded_eastward[..., 1:, 1:-1])
            * (west_side + east_side)
            - diffusivity * (east_side - west_side)
        )
    )
    south_side = haloed_scalar[..., 1:-1, :-1]
    north_side = haloed_scalar[..., 1:-1, 1:]
    north_flux = (
        padded_land_mask[1:-1, :-1]
        * padded_land_mask[1:-1, 1:]
        * (
            0.25
            * (padded_northward[..., 1:-1, :-1] + padded_northward[..., 1:-1, 1:])
            * (south_side + north_side)
            - diffusivity * (north_side - south_side)
        )
    )
    tendency = (
        forcing
        - (east_flux[..., 1:, :] - east_flux[..., :-1, :])
        - (north_flux[..., 1:] - north_flux[..., :-1])
    )
    return tracer + time_step * padded_land_mask[1:-1, 1:-1] * tendency


def patches(padded, rows, columns):
    pieces = [
        padded[:, offset_x : offset_x + rows, offset_y : offset_y + columns]
        for offset_x in range(3)
        for offset_y in range(3)
    ]
    return jnp.stack(pieces, 0).reshape(9 * padded.shape[0], rows * columns)


def network(present_kernel_result, present_hidden_result, present_final_result, patch_rows):
    flat_conv = present_kernel_result.reshape(present_kernel_result.shape[0], -1)
    hidden_one = jnp.tanh(jnp.dot(flat_conv, patch_rows, precision=highest))
    hidden_two = jnp.tanh(jnp.dot(present_hidden_result, hidden_one, precision=highest))
    predicted = jnp.dot(present_final_result, hidden_two, precision=highest)
    return (hidden_one, hidden_two, predicted)


def subgrid_closure_term(haloed_prediction, vertical_slabs):
    parallel_divergence = haloed_prediction[:, 2:, 1:-1] - haloed_prediction[:, :-2, 1:-1]
    meridional_divergence = haloed_prediction[:, 1:-1, 2:] - haloed_prediction[:, 1:-1, :-2]
    thermal_source_term = -0.5 * (
        parallel_divergence[:vertical_slabs]
        + meridional_divergence[vertical_slabs : 2 * vertical_slabs]
    )
    salinity_source_term = -0.5 * (
        parallel_divergence[2 * vertical_slabs : 3 * vertical_slabs]
        + meridional_divergence[3 * vertical_slabs :]
    )
    return (thermal_source_term, salinity_source_term)


def shards(
    thermal_anomaly,
    saltiness_anomaly,
    zonal_flow_speed,
    meridional_flow_speed,
    water_indicator,
    kernel_factors,
    hidden_pointwise_factors,
    final_pointwise_factors,
):
    vertical_slabs = thermal_anomaly.shape[0]
    mask_field = water_indicator.astype(jnp.float32)
    static_pad = detailed_haloed_field(
        jnp.concatenate([zonal_flow_speed, meridional_flow_speed, mask_field[None]], 0)
    )
    padded_eastward = static_pad[:vertical_slabs]
    padded_northward = static_pad[vertical_slabs : 2 * vertical_slabs]
    padded_land_mask = static_pad[2 * vertical_slabs]
    ocean_weight = average_to_blocks(mask_field)
    ocean_area = lax.psum(jnp.sum(ocean_weight), ("lon", "lat", "grp"))
    blocky_zonal_flow = average_to_blocks(zonal_flow_speed)
    blocky_meridional_flow = average_to_blocks(meridional_flow_speed)
    coarse_rows, coarse_columns = ocean_weight.shape
    present_kernel_result, present_hidden_result, present_final_result = (
        kernel_factors,
        hidden_pointwise_factors,
        final_pointwise_factors,
    )
    channels_out = final_pointwise_factors.shape[0]
    for turn_index in range(2):
        blocky_heat_field = average_to_blocks(thermal_anomaly)
        blocky_salinity_sum = average_to_blocks(saltiness_anomaly)
        network_features = jnp.concatenate(
            [blocky_heat_field, blocky_salinity_sum, blocky_zonal_flow, blocky_meridional_flow], 0
        )
        target = jnp.concatenate(
            [
                average_to_blocks(zonal_flow_speed * thermal_anomaly)
                - blocky_zonal_flow * blocky_heat_field,
                average_to_blocks(meridional_flow_speed * thermal_anomaly)
                - blocky_meridional_flow * blocky_heat_field,
                average_to_blocks(zonal_flow_speed * saltiness_anomaly)
                - blocky_zonal_flow * blocky_salinity_sum,
                average_to_blocks(meridional_flow_speed * saltiness_anomaly)
                - blocky_meridional_flow * blocky_salinity_sum,
            ],
            0,
        )
        input_pad = clear_rim(with_halo(network_features, ((("lon", "grp"), 1), ("lat", 2)), 1), 1)
        rows, columns = (coarse_rows, coarse_columns)
        patch_rows = patches(input_pad, rows, columns)
        hidden_one, hidden_two, predicted = network(
            present_kernel_result, present_hidden_result, present_final_result, patch_rows
        )
        reformed_values = predicted.reshape(channels_out, rows, columns)
        haloed_prediction = clear_rim(
            with_halo(reformed_values, ((("lon", "grp"), 1), ("lat", 2)), 1), 1
        )
        thermal_source_term, salinity_source_term = subgrid_closure_term(
            haloed_prediction, vertical_slabs
        )
        haloed_scalar = detailed_haloed_field(
            jnp.concatenate([thermal_anomaly, saltiness_anomaly], 0)
        )
        thermal_anomaly = scalar_step_update(
            thermal_anomaly,
            haloed_scalar[:vertical_slabs],
            padded_eastward,
            padded_northward,
            padded_land_mask,
            upsample_blocks(thermal_source_term),
        )
        saltiness_anomaly = scalar_step_update(
            saltiness_anomaly,
            haloed_scalar[vertical_slabs:],
            padded_eastward,
            padded_northward,
            padded_land_mask,
            upsample_blocks(salinity_source_term),
        )
        loss_scale = 2.0 / (channels_out * ocean_area)
        misfit = predicted - target.reshape(channels_out, -1)
        back_out = loss_scale * ocean_weight.reshape(-1) * misfit
        grad_out = jnp.dot(back_out, hidden_two.T, precision=highest)
        back_two = jnp.dot(present_final_result.T, back_out, precision=highest) * (
            1.0 - hidden_two * hidden_two
        )
        grad_mix = jnp.dot(back_two, hidden_one.T, precision=highest)
        back_one = jnp.dot(present_hidden_result.T, back_two, precision=highest) * (
            1.0 - hidden_one * hidden_one
        )
        grad_conv = jnp.dot(back_one, patch_rows.T, precision=highest).reshape(
            present_kernel_result.shape
        )
        grad_conv, grad_mix, grad_out = lax.psum(
            (grad_conv, grad_mix, grad_out), ("lon", "lat", "grp")
        )
        present_kernel_result = present_kernel_result - learn_rate * grad_conv
        present_hidden_result = present_hidden_result - learn_rate * grad_mix
        present_final_result = present_final_result - learn_rate * grad_out
    return (
        thermal_anomaly,
        saltiness_anomaly,
        present_kernel_result,
        present_hidden_result,
        present_final_result,
    )


def solution(mesh):
    placed = (
        P(None, ("lon", "grp"), "lat"),
        P(None, ("lon", "grp"), "lat"),
        P(None, ("lon", "grp"), "lat"),
        P(None, ("lon", "grp"), "lat"),
        P(("lon", "grp"), "lat"),
        P(),
        P(),
        P(),
    )
    return jax.shard_map(
        shards,
        mesh=mesh,
        in_specs=placed,
        out_specs=(P(None, ("lon", "grp"), "lat"), P(None, ("lon", "grp"), "lat"), P(), P(), P()),
        check_vma=False,
    )
```

profile of v0, /device:TPU:1, one launch (start us, length us, event | category | flops | bytes accessed | tf_op | source)
XLA Modules:
  0.0 799.0 jit_solution(6274394843490103715)
XLA Ops:
  14.0 3.1 collective-permute-start.4
  20.3 4.4 collective-permute-start.13
  26.7 84.9 %psum.49 = f32[]{:T(128)} all-reduce(f32[]{:T(128)} %multiply_reduce_fusion), channel_id=1, replica_groups=mesh['lon'=32,'lat'=4,'grp'=2] {'lon','lat','grp'}, use_global_device_ids=true, to_apply=%region_6.7 | all-reduce | flops 1 | bytes 8 | tf_op jit(solution)/shard_map/psum | solution.py:135
  114.2 3.7 collective-permute-start.7
  122.6 1.8 collective-permute-start.1
  131.0 2.7 collective-permute-start.15
  133.9 9.6 %collective-permute-done.14 = f32[24,10,1]{2,1,0:T(8,128)S(1)} collective-permute-done((f32[24,10,1]{2,1,0:T(8,128)S(1)}, f32[24,10,1]{2,1,0:T(8,128)S(1)}, u32[]{:S(2)}, u32[]{:S(2)}) %collective-permute-start.14) | collective-permute-done | bytes 992 | tf_op jit(solution)/shard_map/ppermute | solution.py:18
  143.5 1.8 collective-permute-start.11
  151.6 2.9 collective-permute-start.3
  160.1 1.8 maximum_select_fusion
  181.2 4.5 collective-permute-start.17
  187.1 6.0 collective-permute-start.25
  193.1 2.7 collective-permute-start.18
  196.8 78.4 %all-reduce.1 = (f32[64,64]{1,0:T(8,128)S(1)}, f32[48,64]{1,0:T(8,128)}) all-reduce(f32[64,64]{1,0:T(8,128)S(1)} %fusion.73, f32[48,64]{1,0:T(8,128)S(1)} %fusion.52), channel_id=1, replica_groups=mesh['lon'=32,'lat'=4,'grp'=2] {'lon','lat','grp'}, use_global_device_ids=true, to_apply=%region_12.13 | all-reduce | flops 7168 | bytes 57344 | tf_op jit(solution)/shard_map/psum | solution.py:210
  277.3 3.6 collective-permute-start.27
  282.4 2.7 collective-permute-done.26
  285.1 3.9 collective-permute-done.27
  290.5 145.5 %all-reduce.5.cloned.1.call-done = f32[64,3,3,48]{0,3,2,1:T(8,128)} async-done(((f32[64,3,3,48]{0,3,2,1:T(8,128)}), f32[64,3,3,48]{0,3,2,1:T(8,128)}) %all-reduce.5.cloned.1.call-update) | async-done | bytes 110608 | tf_op jit(solution)/shard_map/psum | solution.py:210
  440.5 2.4 collective-permute-done.21
  443.1 2.1 collective-permute-start.22
  445.2 1.8 collective-permute-start.23
  454.6 2.4 fusion.61
  461.9 82.4 %all-reduce = (f32[64,64]{1,0:T(8,128)S(1)}, f32[48,64]{1,0:T(8,128)S(1)}) all-reduce(f32[64,64]{1,0:T(8,128)S(1)} %fusion.76, f32[48,64]{1,0:T(8,128)S(1)} %fusion.48), channel_id=1, replica_groups=mesh['lon'=32,'lat'=4,'grp'=2] {'lon','lat','grp'}, use_global_device_ids=true, to_apply=%region_21.22 | all-reduce | flops 7168 | bytes 57344 | tf_op jit(solution)/shard_map/psum | solution.py:210
  546.8 243.5 %all-reduce.7.cloned.1.call-done = f32[64,3,3,48]{0,3,2,1:T(8,128)} async-done(((f32[64,3,3,48]{0,3,2,1:T(8,128)}), f32[64,3,3,48]{0,3,2,1:T(8,128)}) %all-reduce.7.cloned.1.call-update) | async-done | bytes 110608 | tf_op jit(solution)/shard_map/psum | solution.py:210
  (383 shorter events, 83.7 us)
Async XLA Ops:
  7.2 428.8 %all-reduce.5.cloned.1.call-start = ((), (), s32[]{:S(2)}) async-start(), calls=%async_computation | async-start | bytes 442368 | tf_op jit(solution)/shard_map/psum | solution.py:210
  14.0 99.5 %collective-permute-start.4 = (f32[48,1,128]{2,0,1:T(8,128)S(1)}, f32[48,1,128]{2,0,1:T(8,128)S(1)}, u32[]{:S(2)}, u32[]{:S(2)}) collective-permute-start(f32[48,1,128]{2,0,1:T(8,128)S(1)} %get-tuple-element.72), channel_id=1, source_target_pairs={{0,1},{1,8},{8,9},{9,16},{16,17},{17,24},{24,25},{25,32},{32,33},{... | collective-permute-start | bytes 73736 | tf_op jit(solution)/shard_map/ppermute | solution.py:18
  17.1 96.4 %collective-permute-start.5 = (f32[48,1,128]{2,0,1:T(8,128)S(1)}, f32[48,1,128]{2,0,1:T(8,128)S(1)}, u32[]{:S(2)}, u32[]{:S(2)}) collective-permute-start(f32[48,1,128]{2,0,1:T(8,128)S(1)} %get-tuple-element.73), channel_id=1, source_target_pairs={{1,0},{8,1},{9,8},{16,9},{17,16},{24,17},{25,24},{32,25},{33,32},{... | collective-permute-start | bytes 73736 | tf_op jit(solution)/shard_map/ppermute | solution.py:21
  19.2 109.4 %collective-permute-start.12 = (f32[24,1,512]{2,1,0:T(1,128)}, f32[24,1,512]{2,1,0:T(1,128)}, u32[]{:S(2)}, u32[]{:S(2)}) collective-permute-start(f32[24,1,512]{2,1,0:T(1,128)} %get-tuple-element.38), channel_id=1, source_target_pairs={{0,1},{1,8},{8,9},{9,16},{16,17},{17,24},{24,25},{25,32},{32,33},{... | collective-permute-start | bytes 147464 | tf_op jit(solution)/shard_map/ppermute | solution.py:18
  20.3 108.8 %collective-permute-start.13 = (f32[24,1,512]{2,1,0:T(1,128)}, f32[24,1,512]{2,1,0:T(1,128)}, u32[]{:S(2)}, u32[]{:S(2)}) collective-permute-start(f32[24,1,512]{2,1,0:T(1,128)} %get-tuple-element.39), channel_id=1, source_target_pairs={{1,0},{8,1},{9,8},{16,9},{17,16},{24,17},{25,24},{32,25},{33,32},{... | collective-permute-start | bytes 147464 | tf_op jit(solution)/shard_map/ppermute | solution.py:21
  25.5 123.4 %collective-permute-start = (f32[25,1,512]{2,1,0:T(1,128)}, f32[25,1,512]{2,1,0:T(1,128)}, u32[]{:S(2)}, u32[]{:S(2)}) collective-permute-start(f32[25,1,512]{2,1,0:T(1,128)} %get-tuple-element.32), channel_id=1, source_target_pairs={{0,1},{1,8},{8,9},{9,16},{16,17},{17,24},{24,25},{25,32},{32,33},{... | collective-permute-start | bytes 153608 | tf_op jit(solution)/shard_map/ppermute | solution.py:18
  114.2 8.3 %collective-permute-start.6 = (f32[48,4,1]{2,0,1:T(8,128)}, f32[48,4,1]{2,0,1:T(8,128)S(1)}, u32[]{:S(2)}, u32[]{:S(2)}) collective-permute-start(f32[48,4,1]{2,0,1:T(8,128)} %get-tuple-element.64), channel_id=1, source_target_pairs={{0,2},{2,4},{4,6},{6,0},{1,3},{3,5},{5,7},{7,1},{8,10},{10,12},{12... | collective-permute-start | bytes 2312 | tf_op jit(solution)/shard_map/ppermute | solution.py:18
  114.2 10.1 %collective-permute-start.7 = (f32[48,4,1]{2,0,1:T(8,128)S(1)}, f32[48,4,1]{2,0,1:T(8,128)}, u32[]{:S(2)}, u32[]{:S(2)}) collective-permute-start(f32[48,4,1]{2,0,1:T(8,128)S(1)} %get-tuple-element.65), channel_id=1, source_target_pairs={{2,0},{4,2},{6,4},{0,6},{3,1},{5,3},{7,5},{1,7},{10,8},{12,10},{14... | collective-permute-start | bytes 2312 | tf_op jit(solution)/shard_map/ppermute | solution.py:21
  122.6 26.3 %collective-permute-start.1 = (f32[25,1,512]{2,1,0:T(1,128)S(1)}, f32[25,1,512]{2,1,0:T(1,128)S(1)}, u32[]{:S(2)}, u32[]{:S(2)}) collective-permute-start(f32[25,1,512]{2,1,0:T(1,128)S(1)} %copy-done.70), channel_id=1, source_target_pairs={{1,0},{8,1},{9,8},{16,9},{17,16},{24,17},{25,24},{32,25},{33,32},{... | collective-permute-start | bytes 153608 | tf_op jit(solution)/shard_map/ppermute | solution.py:21
  130.1 13.4 %collective-permute-start.14 = (f32[24,10,1]{2,1,0:T(8,128)S(1)}, f32[24,10,1]{2,1,0:T(8,128)S(1)}, u32[]{:S(2)}, u32[]{:S(2)}) collective-permute-start(f32[24,10,1]{2,1,0:T(8,128)S(1)} %get-tuple-element.30), channel_id=1, source_target_pairs={{0,2},{2,4},{4,6},{6,0},{1,3},{3,5},{5,7},{7,1},{8,10},{10,12},{12... | collective-permute-start | bytes 2888 | tf_op jit(solution)/shard_map/ppermute | solution.py:18
  131.0 14.3 %collective-permute-start.15 = (f32[24,10,1]{2,1,0:T(8,128)S(1)}, f32[24,10,1]{2,1,0:T(8,128)S(1)}, u32[]{:S(2)}, u32[]{:S(2)}) collective-permute-start(f32[24,10,1]{2,1,0:T(8,128)S(1)} %get-tuple-element.31), channel_id=1, source_target_pairs={{2,0},{4,2},{6,4},{0,6},{3,1},{5,3},{7,5},{1,7},{10,8},{12,10},{14... | collective-permute-start | bytes 2888 | tf_op jit(solution)/shard_map/ppermute | solution.py:21
  133.8 13.0 %collective-permute-start.10 = (f32[48,4,1]{2,0,1:T(8,128)S(1)}, f32[48,4,1]{2,0,1:T(8,128)S(1)}, u32[]{:S(2)}, u32[]{:S(2)}) collective-permute-start(f32[48,4,1]{2,0,1:T(8,128)S(1)} %get-tuple-element.62), channel_id=1, source_target_pairs={{0,2},{2,4},{4,6},{6,0},{1,3},{3,5},{5,7},{7,1},{8,10},{10,12},{12... | collective-permute-start | bytes 2312 | tf_op jit(solution)/shard_map/ppermute | solution.py:18
  150.5 8.9 %collective-permute-start.2 = (f32[25,10,1]{2,1,0:T(8,128)}, f32[25,10,1]{2,1,0:T(8,128)}, u32[]{:S(2)}, u32[]{:S(2)}) collective-permute-start(f32[25,10,1]{2,1,0:T(8,128)} %get-tuple-element.26), channel_id=1, source_target_pairs={{0,2},{2,4},{4,6},{6,0},{1,3},{3,5},{5,7},{7,1},{8,10},{10,12},{12... | collective-permute-start | bytes 3008 | tf_op jit(solution)/shard_map/ppermute | solution.py:18
  151.6 8.5 %collective-permute-start.3 = (f32[25,10,1]{2,1,0:T(8,128)}, f32[25,10,1]{2,1,0:T(8,128)}, u32[]{:S(2)}, u32[]{:S(2)}) collective-permute-start(f32[25,10,1]{2,1,0:T(8,128)} %get-tuple-element.27), channel_id=1, source_target_pairs={{2,0},{4,2},{6,4},{0,6},{3,1},{5,3},{7,5},{1,7},{10,8},{12,10},{14... | collective-permute-start | bytes 3008 | tf_op jit(solution)/shard_map/ppermute | solution.py:21
  180.8 12.2 %collective-permute-start.16 = (f32[48,1,128]{2,0,1:T(8,128)S(1)}, f32[48,1,128]{2,0,1:T(8,128)S(1)}, u32[]{:S(2)}, u32[]{:S(2)}) collective-permute-start(f32[48,1,128]{2,0,1:T(8,128)S(1)} %get-tuple-element.68), channel_id=1, source_target_pairs={{0,1},{1,8},{8,9},{9,16},{16,17},{17,24},{24,25},{25,32},{32,33},{... | collective-permute-start | bytes 73736 | tf_op jit(solution)/shard_map/ppermute | solution.py:18
  181.2 11.8 %collective-permute-start.17 = (f32[48,1,128]{2,0,1:T(8,128)S(1)}, f32[48,1,128]{2,0,1:T(8,128)S(1)}, u32[]{:S(2)}, u32[]{:S(2)}) collective-permute-start(f32[48,1,128]{2,0,1:T(8,128)S(1)} %get-tuple-element.69), channel_id=1, source_target_pairs={{1,0},{8,1},{9,8},{16,9},{17,16},{24,17},{25,24},{32,25},{33,32},{... | collective-permute-start | bytes 73736 | tf_op jit(solution)/shard_map/ppermute | solution.py:21
  186.9 603.3 %all-reduce.7.cloned.1.call-start = ((), (), s32[]{:S(2)}) async-start(), calls=%async_computation.1 | async-start | bytes 442368 | tf_op jit(solution)/shard_map/psum | solution.py:210
  187.0 90.1 %collective-permute-start.24 = (f32[24,1,512]{2,1,0:T(1,128)S(1)}, f32[24,1,512]{2,1,0:T(1,128)S(1)}, u32[]{:S(2)}, u32[]{:S(2)}) collective-permute-start(f32[24,1,512]{2,1,0:T(1,128)S(1)} %get-tuple-element.36), channel_id=1, source_target_pairs={{0,1},{1,8},{8,9},{9,16},{16,17},{17,24},{24,25},{25,32},{32,33},{... | collective-permute-start | bytes 147464 | tf_op jit(solution)/shard_map/ppermute | solution.py:18
  187.1 90.0 %collective-permute-start.25 = (f32[24,1,512]{2,1,0:T(1,128)S(1)}, f32[24,1,512]{2,1,0:T(1,128)S(1)}, u32[]{:S(2)}, u32[]{:S(2)}) collective-permute-start(f32[24,1,512]{2,1,0:T(1,128)S(1)} %get-tuple-element.37), channel_id=1, source_target_pairs={{1,0},{8,1},{9,8},{16,9},{17,16},{24,17},{25,24},{32,25},{33,32},{... | collective-permute-start | bytes 147464 | tf_op jit(solution)/shard_map/ppermute | solution.py:21
  193.1 83.3 %collective-permute-start.18 = (f32[48,4,1]{2,0,1:T(8,128)S(1)}, f32[48,4,1]{2,0,1:T(8,128)S(1)}, u32[]{:S(2)}, u32[]{:S(2)}) collective-permute-start(f32[48,4,1]{2,0,1:T(8,128)S(1)} %get-tuple-element.58), channel_id=1, source_target_pairs={{0,2},{2,4},{4,6},{6,0},{1,3},{3,5},{5,7},{7,1},{8,10},{10,12},{12... | collective-permute-start | bytes 2312 | tf_op jit(solution)/shard_map/ppermute | solution.py:18
  195.9 80.6 %collective-permute-start.19 = (f32[48,4,1]{2,0,1:T(8,128)S(1)}, f32[48,4,1]{2,0,1:T(8,128)S(1)}, u32[]{:S(2)}, u32[]{:S(2)}) collective-permute-start(f32[48,4,1]{2,0,1:T(8,128)S(1)} %get-tuple-element.59), channel_id=1, source_target_pairs={{2,0},{4,2},{6,4},{0,6},{3,1},{5,3},{7,5},{1,7},{10,8},{12,10},{14... | collective-permute-start | bytes 2312 | tf_op jit(solution)/shard_map/ppermute | solution.py:21
  277.2 7.8 collective-permute-start.26
  277.3 11.6 %collective-permute-start.27 = (f32[24,10,1]{2,1,0:T(8,128)S(1)}, f32[24,10,1]{2,1,0:T(8,128)}, u32[]{:S(2)}, u32[]{:S(2)}) collective-permute-start(f32[24,10,1]{2,1,0:T(8,128)S(1)} %get-tuple-element.29), channel_id=1, source_target_pairs={{2,0},{4,2},{6,4},{0,6},{3,1},{5,3},{7,5},{1,7},{10,8},{12,10},{14... | collective-permute-start | bytes 2888 | tf_op jit(solution)/shard_map/ppermute | solution.py:21
  443.1 6.4 collective-permute-start.22
  (84 other events, 1970.9 us)
Sparse Core Ops, SparseCore 0:
  187.0 248.9 all-reduce.4
  546.3 243.9 all-reduce.6
where the time goes:
time: 808 us; the launch traced here: 799 us
  waiting for transfers between devices  413 us (51%)
  blocking collectives  246 us (30%)
  starting transfers between devices  48.3 us (6%)
  other arithmetic  34.8 us (4%)
  local copies, waits for them, and re-layouts  33.4 us (4%)
  between operations  16.7 us (2%)
    psum x2, waiting for transfers between devices, shards(): lax.psum((grad_conv, grad_mix, grad_out), ('lon', 'lat', 'grp'))  389 us
    psum x2, blocking collectives, shards(): lax.psum((grad_conv, grad_mix, grad_out), ('lon', 'lat', 'grp'))  161 us
    psum x1, blocking collectives, shards(): ocean_area = lax.psum(jnp.sum(ocean_weight), ('lon', 'lat', 'grp'))  84.9 us
    ppermute x14, starting transfers between devices, with_halo(): lax.ppermute(lax.slice_in_dim(block, 0, width, axis=dim), axis, backward)  36 us
  transfers between devices with their start and end apart: 30, of which 10 were waited for; matrix products, arithmetic and copies ran while one was open for 4% of the time, Pallas kernels for 0%

commit v1 on v0

v1 whole, which is shorter than its diff:
```python
import functools

import jax
import jax.numpy as jnp
from jax import lax
from jax.experimental import pallas as pl
from jax.experimental.pallas import tpu as pltpu
from jax.sharding import PartitionSpec as P

time_step = 0.2
diffusivity = 0.5
learn_rate = 200.0
highest = lax.Precision.HIGHEST
f32 = jnp.float32
bf16 = jnp.bfloat16

LEVELS = 12
CHANNELS = 4 * LEVELS
HIDDEN = 64
TAPS = 9 * CHANNELS
MIX_AT = 512
OUT_AT = 576
AREA_AT = 624
PACKED = 640
FINE = 512
COARSE = 128
VMEM_LIMIT = 48 * 1024 * 1024


def struct(*shape):
    return jax.ShapeDtypeStruct(shape, f32)


def call(kernel, outs, *args, scratch=(), smem=0, flops=0, bytes_accessed=0):
    specs = [pl.BlockSpec(memory_space=pltpu.SMEM)] * smem
    specs += [pl.BlockSpec(memory_space=pltpu.VMEM)] * (len(args) - smem)
    return pl.pallas_call(
        kernel,
        out_shape=outs,
        in_specs=specs,
        out_specs=[pl.BlockSpec(memory_space=pltpu.VMEM)] * len(outs),
        scratch_shapes=scratch,
        compiler_params=pltpu.CompilerParams(vmem_limit_bytes=VMEM_LIMIT),
        cost_estimate=pl.CostEstimate(
            flops=flops, bytes_accessed=bytes_accessed, transcendentals=0
        ),
    )(*args)


def exact_dot(value, selector):
    high = value.astype(bf16)
    rest = value - high.astype(f32)
    middle = rest.astype(bf16)
    low = (rest - middle.astype(f32)).astype(bf16)
    dot = functools.partial(jnp.dot, preferred_element_type=f32)
    return (dot(low, selector) + dot(middle, selector)) + dot(high, selector)


def pooling_matrix():
    fine = lax.broadcasted_iota(jnp.int32, (FINE, COARSE), 0) >> 2
    coarse = lax.broadcasted_iota(jnp.int32, (FINE, COARSE), 1)
    return jnp.where(fine == coarse, f32(1.0 / 16.0), f32(0.0)).astype(bf16)


def spreading_matrix():
    fine = lax.broadcasted_iota(jnp.int32, (COARSE, FINE), 1) >> 2
    coarse = lax.broadcasted_iota(jnp.int32, (COARSE, FINE), 0)
    return jnp.where(fine == coarse, f32(1.0), f32(0.0)).astype(bf16)


def lane_index(shape):
    return lax.broadcasted_iota(jnp.int32, shape, len(shape) - 1)


def fill_blocks(blocks, refs):
    for which, ref in enumerate(refs):
        for block in range(4):
            start = (4 * which + block) * 8 * LEVELS
            blocks[start : start + 8 * LEVELS, :] = ref[:, 128 * block : 128 * (block + 1)]


def longitude_row(blocks, which, block, lon):
    start = (4 * which + block) * 8 * LEVELS + lon
    return blocks[pl.ds(start, LEVELS, stride=8), :]


def coarsen(blocks, sums_ref, x_ref, target_ref, low_ref, high_ref):
    for row in range(2):
        for block in range(4):
            total = None
            for lon in range(4 * row, 4 * row + 4):
                t, s, u, v = (longitude_row(blocks, which, block, lon) for which in range(4))
                terms = (t, s, u, v, u * t, v * t, u * s, v * s)
                total = terms if total is None else [a + b for a, b in zip(total, terms)]
            for at, value in enumerate(total):
                start = 2 * CHANNELS * row + LEVELS * at
                sums_ref[start : start + LEVELS, 128 * block : 128 * (block + 1)] = value
    means = exact_dot(sums_ref[...], pooling_matrix())
    for row in range(2):
        x = means[2 * CHANNELS * row : 2 * CHANNELS * row + CHANNELS]
        products = means[2 * CHANNELS * row + CHANNELS : 2 * CHANNELS * (row + 1)]
        ct, cs, cu, cv = (x[LEVELS * k : LEVELS * (k + 1)] for k in range(4))
        x_ref[CHANNELS * row : CHANNELS * (row + 1), :] = x
        own = jnp.concatenate([cu * ct, cv * ct, cu * cs, cv * cs], 0)
        target_ref[CHANNELS * row : CHANNELS * (row + 1), :] = products - own
    turned = x_ref[...].T
    low_ref[...] = jnp.zeros(low_ref.shape, f32)
    high_ref[...] = jnp.zeros(high_ref.shape, f32)
    low_ref[0:1, 0 : 2 * CHANNELS] = turned[0:1]
    high_ref[0:1, 0 : 2 * CHANNELS] = turned[COARSE - 1 : COARSE]


def fine_edges(blocks, rows_of, mask_ref, columns_of, first_ref, last_ref, low_ref, high_ref):
    depth = first_ref.shape[0] // 4
    for lon, out in ((0, first_ref), (7, last_ref)):
        out[...] = jnp.zeros(out.shape, f32)
        for block in range(4):
            for which in range(rows_of):
                start = block * depth + which * LEVELS
                out[start : start + LEVELS, :] = longitude_row(blocks, which, block, lon)
            if mask_ref is not None:
                start = block * depth + rows_of * LEVELS
                out[start : start + 1, :] = mask_ref[lon : lon + 1, 128 * block : 128 * (block + 1)]
    low_ref[...] = jnp.zeros(low_ref.shape, f32)
    high_ref[...] = jnp.zeros(high_ref.shape, f32)
    for at, ref in enumerate(columns_of):
        size = ref.shape[0]
        low_ref[at : at + 1, 0:size] = ref[:, 0:128].T[0:1]
        high_ref[at : at + 1, 0:size] = ref[:, FINE - 128 : FINE].T[127:128]


def prepare_kernel(t, s, u, v, mask, x, target, weight, low, high, sums, blocks):
    fill_blocks(blocks, (t, s, u, v))
    coarsen(blocks, sums, x, target, low, high)
    m = mask[...].astype(f32)
    rows = jnp.concatenate(
        [jnp.sum(m[0:4], axis=0, keepdims=True), jnp.sum(m[4:8], axis=0, keepdims=True)]
        + [jnp.zeros((6, FINE), f32)],
        0,
    )
    weight[...] = jnp.dot(rows.astype(bf16), pooling_matrix(), preferred_element_type=f32)


def edges_kernel(t, s, u, v, mask, first, last, low, high, mask_values, blocks):
    mask_values[...] = mask[...].astype(f32)
    fill_blocks(blocks, (t, s, u))
    fine_edges(blocks, 3, mask_values, (t, s, v, mask_values), first, last, low, high)


def dot(a, b):
    return jnp.dot(a, b, precision=highest, preferred_element_type=f32)


def dot_nt(a, b):
    return lax.dot_general(
        a, b, (((1,), (1,)), ((), ())), precision=highest, preferred_element_type=f32
    )


def network_step(
    core, x, west, east, low, high, target, weight, packed, pred, pred_low, pred_high, own, other, taps, grads
):
    lanes = lane_index((CHANNELS, COARSE))
    corners = jnp.concatenate(
        [
            low[0:1, :],
            high[0:1, :],
            west[CHANNELS : CHANNELS + 1, :],
            west[CHANNELS + 8 : CHANNELS + 9, :],
            east[CHANNELS : CHANNELS + 1, :],
            east[CHANNELS + 8 : CHANNELS + 9, :],
            jnp.zeros((2, COARSE), f32),
        ],
        0,
    ).T
    rows = (
        (west[0:CHANNELS, :], CHANNELS, 2),
        (x[0:CHANNELS, :], 0, 0),
        (x[CHANNELS : 2 * CHANNELS, :], CHANNELS, 0),
        (east[0:CHANNELS, :], 0, 4),
    )
    for at, (value, start, column) in enumerate(rows):
        before = corners[start : start + CHANNELS, column : column + 1]
        after = corners[start : start + CHANNELS, column + 1 : column + 2]
        shifted = (
            jnp.where(lanes == 0, before, pltpu.roll(value, 1, 1)),
            value,
            jnp.where(lanes == COARSE - 1, after, pltpu.roll(value, COARSE - 1, 1)),
        )
        for row in range(2):
            tap = at - row
            if 0 <= tap < 3:
                for side in range(3):
                    begin = (3 * tap + side) * CHANNELS
                    taps[begin : begin + CHANNELS, COARSE * row : COARSE * (row + 1)] = shifted[side]
    kernel = packed[:, 0:TAPS]
    mix = packed[:, MIX_AT : MIX_AT + HIDDEN]
    out_turned = packed[:, OUT_AT : OUT_AT + CHANNELS]
    hidden_one = jnp.tanh(dot(kernel, taps[...]))
    hidden_two = jnp.tanh(dot(mix, hidden_one))
    predicted = dot(out_turned.T, hidden_two)
    pred[0:CHANNELS, :] = predicted[:, 0:COARSE]
    pred[CHANNELS : 2 * CHANNELS, :] = predicted[:, COARSE : 2 * COARSE]
    back_out = jnp.concatenate(
        [
            weight[row : row + 1, :]
            * (
                predicted[:, COARSE * row : COARSE * (row + 1)]
                - target[CHANNELS * row : CHANNELS * (row + 1), :]
            )
            for row in range(2)
        ],
        1,
    )
    back_two = dot(out_turned, back_out) * (1.0 - hidden_two * hidden_two)
    back_one = dot(mix.T, back_two) * (1.0 - hidden_one * hidden_one)
    grads[:, MIX_AT - 128 : PACKED] = jnp.zeros((HIDDEN, PACKED - MIX_AT + 128), f32)
    grads[:, 0:TAPS] = dot_nt(back_one, taps[...])
    grads[:, MIX_AT : MIX_AT + HIDDEN] = dot_nt(back_two, hidden_one)
    grads[:, OUT_AT : OUT_AT + CHANNELS] = dot_nt(hidden_two, back_out)
    area = jnp.sum(weight[0:2, :], axis=(0, 1), keepdims=True)
    grads[:, AREA_AT : AREA_AT + 1] = jnp.broadcast_to(area, (HIDDEN, 1))
    half = HIDDEN // 2
    own[...] = grads[pl.ds(pl.multiple_of(core[0] * half, half), half), :]
    other[...] = grads[pl.ds(pl.multiple_of((1 - core[0]) * half, half), half), :]
    turned = pred[...].T
    pred_low[...] = jnp.zeros(pred_low.shape, f32)
    pred_high[...] = jnp.zeros(pred_high.shape, f32)
    pred_low[0:1, 0 : 2 * CHANNELS] = turned[0:1]
    pred_high[0:1, 0 : 2 * CHANNELS] = turned[COARSE - 1 : COARSE]


def descended(core, packed, part, back):
    half = HIDDEN // 2
    mine, theirs = part[...], back[...]
    first = core[0] == 0
    total = jnp.concatenate(
        [jnp.where(first, mine, theirs), jnp.where(first, theirs, mine)], 0
    )
    area = total[0:1, AREA_AT : AREA_AT + 1]
    step = (learn_rate * 2.0 / CHANNELS) / area
    return packed[...] - step * total


def first_network_kernel(core, x, west, east, low, high, target, weight, packed, *rest):
    network_step(core, x, west, east, low, high, target, weight, packed, *rest)


def next_network_kernel(
    core, x, west, east, low, high, target, weight, packed, part, back, renewed, *rest
):
    renewed[...] = descended(core, packed, part, back)
    network_step(core, x, west, east, low, high, target, weight, renewed, *rest)


def last_kernel(core, packed, part, back, kernel, mix, out):
    renewed = descended(core, packed, part, back)
    kernel[...] = renewed[:, 0:TAPS]
    mix[...] = renewed[:, MIX_AT : MIX_AT + HIDDEN]
    out[...] = renewed[:, OUT_AT : OUT_AT + CHANNELS].T


def forcing(pred, west, east, low, high):
    before = (west[0:CHANNELS], pred[0:CHANNELS, :])
    after = (pred[CHANNELS : 2 * CHANNELS, :], east[0:CHANNELS])
    lanes = lane_index((CHANNELS, COARSE))
    pieces = []
    for row in range(2):
        value = pred[CHANNELS * row : CHANNELS * (row + 1), :]
        along = after[row] - before[row]
        south = jnp.where(lanes == 0, low[CHANNELS * row : CHANNELS * (row + 1)], pltpu.roll(value, 1, 1))
        north = jnp.where(
            lanes == COARSE - 1,
            high[CHANNELS * row : CHANNELS * (row + 1)],
            pltpu.roll(value, COARSE - 1, 1),
        )
        across = north - south
        for at in (0, 2 * LEVELS):
            pieces.append(-0.5 * (along[at : at + LEVELS] + across[at + LEVELS : at + 2 * LEVELS]))
            pieces.append(jnp.zeros((4, COARSE), f32))
    return exact_dot(jnp.concatenate(pieces, 0), spreading_matrix())


def advance(
    t, s, u, v, mask, pred, fixed_west, fixed_east, fixed_low, fixed_high, west, east, low, high, t_out, s_out
):
    m = mask[...].astype(f32)
    shape = (8, FINE)
    lanes = lane_index(shape)
    subs = lax.broadcasted_iota(jnp.int32, shape, 0)
    fixed_depth = 40
    depth = (west.shape[0] - CHANNELS) // 4

    def edge_row(ref, stride, at):
        return jnp.concatenate([ref[stride * k + at : stride * k + at + 1, :] for k in range(4)], 1)

    def neighbours_lon(value, row_west, row_east):
        return (
            jnp.where(subs == 0, row_west, pltpu.roll(value, 1, 0)),
            jnp.where(subs == 7, row_east, pltpu.roll(value, 7, 0)),
        )

    def neighbours_lat(value, column_low, column_high):
        return (
            jnp.where(lanes == 0, column_low, pltpu.roll(value, 1, 1)),
            jnp.where(lanes == FINE - 1, column_high, pltpu.roll(value, FINE - 1, 1)),
        )

    fixed_low_turned = fixed_low[0:8, :].T
    fixed_high_turned = fixed_high[0:8, :].T
    low_turned = jnp.concatenate([low[0:2, :], low[8:9, :], low[2:7, :]], 0).T
    high_turned = jnp.concatenate([high[0:2, :], high[8:9, :], high[2:7, :]], 0).T
    start = 4 * depth
    force = forcing(
        pred,
        west[start : start + CHANNELS, :],
        east[start : start + CHANNELS, :],
        low_turned[:, 2:3],
        high_turned[:, 2:3],
    )
    m_west, m_east = neighbours_lon(
        m, edge_row(fixed_west, fixed_depth, 3 * LEVELS), edge_row(fixed_east, fixed_depth, 3 * LEVELS)
    )
    m_low, m_high = neighbours_lat(m, fixed_low_turned[0:8, 3:4], fixed_high_turned[0:8, 3:4])
    open_west, open_east, open_low, open_high = m * m_west, m * m_east, m * m_low, m * m_high
    mix_west, mix_east = diffusivity * open_west, diffusivity * open_east
    mix_low, mix_high = diffusivity * open_low, diffusivity * open_high
    pace = time_step * m
    for level in range(LEVELS):
        at = slice(8 * level, 8 * (level + 1))
        u_here, v_here = u[at, :], v[at, :]
        u_west, u_east = neighbours_lon(
            u_here,
            edge_row(fixed_west, fixed_depth, 2 * LEVELS + level),
            edge_row(fixed_east, fixed_depth, 2 * LEVELS + level),
        )
        v_low, v_high = neighbours_lat(v_here, fixed_low_turned[at, 2:3], fixed_high_turned[at, 2:3])
        speed_west = 0.25 * (u_here + u_west) * open_west
        speed_east = 0.25 * (u_here + u_east) * open_east
        speed_low = 0.25 * (v_here + v_low) * open_low
        speed_high = 0.25 * (v_here + v_high) * open_high
        for which, (q_ref, out) in enumerate(((t, t_out), (s, s_out))):
            q = q_ref[at, :]
            q_west, q_east = neighbours_lon(
                q,
                edge_row(west, depth, LEVELS * which + level),
                edge_row(east, depth, LEVELS * which + level),
            )
            q_low, q_high = neighbours_lat(
                q, low_turned[at, which : which + 1], high_turned[at, which : which + 1]
            )
            flux_east = speed_east * (q + q_east) - mix_east * (q_east - q)
            flux_west = speed_west * (q_west + q) - mix_west * (q - q_west)
            flux_high = speed_high * (q + q_high) - mix_high * (q_high - q)
            flux_low = speed_low * (q_low + q) - mix_low * (q - q_low)
            row = 16 * which + level
            push = jnp.where(subs < 4, force[row : row + 1], force[32 + row : 33 + row])
            out[at, :] = q + pace * (push - (flux_east - flux_west) - (flux_high - flux_low))


def first_advance_kernel(*refs):
    ins, outs = refs[:10], refs[10:]
    t, s, u, v, mask, pred, west, east, low, high = ins
    t_out, s_out, x, target, low_out, high_out, first, last, fine_low, fine_high, sums, blocks = outs
    advance(t, s, u, v, mask, pred, west, east, low, high, west, east, low, high, t_out, s_out)
    fill_blocks(blocks, (t_out, s_out, u, v))
    coarsen(blocks, sums, x, target, low_out, high_out)
    fine_edges(blocks, 2, None, (t_out, s_out), first, last, fine_low, fine_high)


def next_advance_kernel(*refs):
    advance(*refs)


def ring(axis, step):
    count = 1
    for name in axis:
        count *= lax.axis_size(name)
    return [(i, (i + step) % count) for i in range(count)]


def exchange_lon(first, last):
    axis = ("lon", "grp")
    return lax.ppermute(last, axis, ring(axis, 1)), lax.ppermute(first, axis, ring(axis, -1))


def exchange_lat(low, high):
    count = lax.axis_size("lat")
    up = [(i, i + 1) for i in range(count - 1)]
    down = [(i + 1, i) for i in range(count - 1)]
    return lax.ppermute(high, "lat", up), lax.ppermute(low, "lat", down)


def flipped(axis, mask):
    return [(i, i ^ mask) for i in range(lax.axis_size(axis))]


def exchanged_sum(value, axis, masks):
    parts = [lax.ppermute(value, axis, flipped(axis, mask)) for mask in masks]
    if len(parts) == 1:
        return value + parts[0]
    return (value + parts[0]) + (parts[1] + parts[2])


def sum_over_devices(own, other):
    part = own + lax.ppermute(other, "grp", flipped("grp", 1))
    part = exchanged_sum(part, "lon", (1,))
    low = 2
    while low < lax.axis_size("lon"):
        part = exchanged_sum(part, "lon", (low, 2 * low, 3 * low))
        low *= 4
    part = exchanged_sum(part, "lat", (1, 2, 3))
    return part, lax.ppermute(part, "grp", flipped("grp", 1))


def shards(
    thermal_anomaly,
    saltiness_anomaly,
    zonal_flow_speed,
    meridional_flow_speed,
    water_indicator,
    kernel_factors,
    hidden_pointwise_factors,
    final_pointwise_factors,
):
    fields = tuple(
        value.reshape(8 * LEVELS, FINE)
        for value in (thermal_anomaly, saltiness_anomaly, zonal_flow_speed, meridional_flow_speed)
    )
    core = lax.axis_index("grp").astype(jnp.int32).reshape(1)
    packed = jnp.concatenate(
        [
            kernel_factors.reshape(HIDDEN, TAPS),
            jnp.zeros((HIDDEN, MIX_AT - TAPS), f32),
            hidden_pointwise_factors,
            final_pointwise_factors.T,
            jnp.zeros((HIDDEN, PACKED - AREA_AT), f32),
        ],
        1,
    )
    blocks = pltpu.VMEM((16 * 8 * LEVELS, 128), f32)
    sums = [pltpu.VMEM((4 * CHANNELS, FINE), f32), blocks]
    wide = struct(2 * CHANNELS, COARSE)
    tile = struct(8, 128)
    half = struct(HIDDEN // 2, PACKED)
    field = struct(8 * LEVELS, FINE)

    def input_halo(x, low, high):
        south, north = exchange_lat(low, high)
        first, last = (
            jnp.concatenate([x[CHANNELS * row : CHANNELS * (row + 1)], south, north], 0)
            for row in range(2)
        )
        west, east = exchange_lon(first, last)
        return west, east, south, north

    network_outs = [wide, tile, tile, half, half]
    network_scratch = [pltpu.VMEM((TAPS, 2 * COARSE), f32), pltpu.VMEM((HIDDEN, PACKED), f32)]

    def state_halo(pred, pred_low, pred_high, first, last, low, high):
        west, east = exchange_lon(
            jnp.concatenate([first, pred[0:CHANNELS]], 0),
            jnp.concatenate([last, pred[CHANNELS : 2 * CHANNELS]], 0),
        )
        south, north = exchange_lat(
            jnp.concatenate([low, pred_low], 0), jnp.concatenate([high, pred_high], 0)
        )
        return west, east, south, north

    x, target, weight, low, high = call(
        prepare_kernel, [wide, wide, tile, tile, tile], *fields, water_indicator, scratch=sums
    )
    edge = struct(160, 128)
    first, last, fine_low, fine_high = call(
        edges_kernel,
        [edge, edge, tile, tile],
        *fields,
        water_indicator,
        scratch=[pltpu.VMEM((8, FINE), f32), blocks],
    )
    west, east, south, north = input_halo(x, low, high)
    pred, pred_low, pred_high, own, other = call(
        first_network_kernel,
        network_outs,
        core, x, west, east, south, north, target, weight, packed,
        scratch=network_scratch,
        smem=1,
    )
    part, back = sum_over_devices(own, other)
    fixed = state_halo(pred, pred_low, pred_high, first, last, fine_low, fine_high)
    edge = struct(96, 128)
    t, s, x, target, low, high, first, last, fine_low, fine_high = call(
        first_advance_kernel,
        [field, field, wide, wide, tile, tile, edge, edge, tile, tile],
        *fields, water_indicator, pred, *fixed,
        scratch=sums,
    )
    west, east, south, north = input_halo(x, low, high)
    packed, pred, pred_low, pred_high, own, other = call(
        next_network_kernel,
        [struct(HIDDEN, PACKED)] + network_outs,
        core, x, west, east, south, north, target, weight, packed, part, back,
        scratch=network_scratch,
        smem=1,
    )
    part, back = sum_over_devices(own, other)
    moving = state_halo(pred, pred_low, pred_high, first, last, fine_low, fine_high)
    t, s = call(
        next_advance_kernel,
        [field, field],
        t, s, *fields[2:], water_indicator, pred, *fixed, *moving,
    )
    kernel, mix, out = call(
        last_kernel,
        [struct(HIDDEN, TAPS), struct(HIDDEN, HIDDEN), struct(CHANNELS, HIDDEN)],
        core, packed, part, back,
        smem=1,
    )
    return (
        t.reshape(thermal_anomaly.shape),
        s.reshape(thermal_anomaly.shape),
        kernel.reshape(kernel_factors.shape),
        mix,
        out,
    )


def solution(mesh):
    field = P(None, ("lon", "grp"), "lat")
    return jax.shard_map(
        shards,
        mesh=mesh,
        in_specs=(field, field, field, field, P(("lon", "grp"), "lat"), P(), P(), P()),
        out_specs=(field, field, P(), P(), P()),
        check_vma=False,
    )
```

time: 808 us -> 135 us (0.17); the launches traced: 799 us -> 135 us
  waiting for transfers between devices: 413 us -> 30.2 us
  blocking collectives: 246 us -> 0 us
  starting transfers between devices: 48.3 us -> 87 us
  other arithmetic: 34.8 us -> 0.22 us
  local copies, waits for them, and re-layouts: 33.4 us -> 6.99 us
  between operations: 16.7 us -> 1.11 us
  Pallas kernels: 0 us -> 9.41 us
    psum x2 -> x0, waiting for transfers between devices: 389 us -> none  [shards(): lax.psum((grad_conv, grad_mix, grad_out), ('lon', 'lat', 'grp'))]
    psum x3 -> x0, blocking collectives: 246 us -> none  [the longest x2 161 us: shards(): lax.psum((grad_conv, grad_mix, grad_out), ('lon', 'lat', 'grp'))]
    ppermute x28 -> x40, starting transfers between devices: 48.2 us -> 87 us  [the longest x20 25.6 us: exchanged_sum(): parts = [lax.ppermute(value, axis, flipped(axis, mask)) for mask in masks]]
    reduce_sum x16 -> x0, other arithmetic: 9.53 us -> none  [the longest x15 8.92 us: average_to_blocks(): return field.reshape(array_extent[:-2] + (array_extent[-2] // 4, 4, array...]
    pallas_call x0 -> x7, Pallas kernels: none -> 9.41 us  [call(): pl.pallas_call(kernel, out_shape=outs, in_specs=specs, out_specs=[pl.Bloc...]
    mul x15 -> x0, other arithmetic: 9.16 us -> none  [the longest x2 3.16 us: shards(): meridional_flow_speed * thermal_anomaly]
    mul x12 -> x0, local copies, waits for them, and re-layouts: 8.34 us -> none  [the longest x2 2.25 us: shards(): zonal_flow_speed * thermal_anomaly]
    ppermute x28 -> x40, waiting for transfers between devices: 23.8 us -> 30.2 us  [the longest x20 19.1 us: exchanged_sum(): parts = [lax.ppermute(value, axis, flipped(axis, mask)) for mask in masks]]
  transfers between devices with their start and end apart: 30 -> 40, of which waited for: 10 -> 13; matrix products, arithmetic and copies ran while one was open for 4% -> 0% of each run, Pallas kernels for 0% -> 3%
where the time goes in v1:
time: 135 us
  starting transfers between devices  87 us (64%)
  waiting for transfers between devices  30.2 us (22%)
  Pallas kernels  9.41 us (7%)
  local copies, waits for them, and re-layouts  6.99 us (5%)
    ppermute x20, starting transfers between devices, exchanged_sum(): parts = [lax.ppermute(value, axis, flipped(axis, mask)) for mask in masks]  25.6 us
    ppermute x8, starting transfers between devices, exchange_lat(): return (lax.ppermute(high, 'lat', up), lax.ppermute(low, 'lat', down))  24.5 us
    ppermute x20, waiting for transfers between devices, exchanged_sum(): parts = [lax.ppermute(value, axis, flipped(axis, mask)) for mask in masks]  19.1 us
    ppermute x2, starting transfers between devices, sum_over_devices(): part = own + lax.ppermute(other, 'grp', flipped('grp', 1))  11.4 us
    ppermute x2, starting transfers between devices, sum_over_devices(): return (part, lax.ppermute(part, 'grp', flipped('grp', 1)))  10.1 us
    ppermute x4, starting transfers between devices, exchange_lon(): lax.ppermute(first, axis, ring(axis, -1))  9.44 us
    pallas_call x7, Pallas kernels, call(): pl.pallas_call(kernel, out_shape=outs, in_specs=specs, out_specs=[pl.Bloc...  9.41 us
    ppermute x8, waiting for transfers between devices, exchange_lat(): return (lax.ppermute(high, 'lat', up), lax.ppermute(low, 'lat', down))  6.57 us
  transfers between devices with their start and end apart: 40, of which 13 were waited for; matrix products, arithmetic and copies ran while one was open for 0% of the time, Pallas kernels for 3%

profile of v1, /device:TPU:1, one launch (start us, length us, event | category | flops | bytes accessed | tf_op | source)
XLA Modules:
  0.0 134.9 jit_solution(11587610127995896598)
XLA Ops:
  5.7 5.7 %collective-permute-start = (f32[8,128]{1,0:T(8,128)S(1)}, f32[8,128]{1,0:T(8,128)S(1)}, u32[]{:S(2)}, u32[]{:S(2)}) collective-permute-start(f32[8,128]{1,0:T(8,128)S(1)} %get-tuple-element.41), channel_id=1, source_target_pairs={{0,2},{2,4},{4,6},{1,3},{3,5},{5,7},{8,10},{10,12},{12,14},{9,11},... | collective-permute-start | bytes 12296 | tf_op jit(solution)/shard_map/ppermute | solution.py:391
  12.7 5.8 %collective-permute-done.1.high = f32[8,128]{1,0:T(8,128)S(1)} collective-permute-done((f32[8,128]{1,0:T(8,128)S(1)}, f32[8,128]{1,0:T(8,128)S(1)}, u32[]{:S(2)}, u32[]{:S(2)}) %collective-permute-start.1) | collective-permute-done | bytes 4128 | tf_op jit(solution)/shard_map/ppermute | solution.py:391
  27.2 6.9 %collective-permute-start.12 = (f32[32,640]{1,0:T(8,128)S(1)}, f32[32,640]{1,0:T(8,128)S(1)}, u32[]{:S(2)}, u32[]{:S(2)}) collective-permute-start(f32[32,640]{1,0:T(8,128)S(1)} %get-tuple-element.59), channel_id=1, source_target_pairs={{0,1},{1,0},{2,3},{3,2},{4,5},{5,4},{6,7},{7,6},{8,9},{9,8},{10,11... | collective-permute-start | bytes 245768 | tf_op jit(solution)/shard_map/ppermute | solution.py:406
  35.5 6.1 %collective-permute-start.6 = (f32[16,128]{1,0:T(8,128)S(1)}, f32[16,128]{1,0:T(8,128)S(1)}, u32[]{:S(2)}, u32[]{:S(2)}) collective-permute-start(f32[16,128]{1,0:T(8,128)S(1)} %pad_maximum_fusion.12), channel_id=1, source_target_pairs={{0,2},{2,4},{4,6},{1,3},{3,5},{5,7},{8,10},{10,12},{12,14},{9,11},... | collective-permute-start | bytes 24584 | tf_op jit(solution)/shard_map/ppermute | solution.py:391
  41.7 3.7 %collective-permute-done.13 = f32[32,640]{1,0:T(8,128)S(1)} collective-permute-done((f32[32,640]{1,0:T(8,128)S(1)}, f32[32,640]{1,0:T(8,128)S(1)}, u32[]{:S(2)}, u32[]{:S(2)}) %collective-permute-start.13) | collective-permute-done | bytes 81952 | tf_op jit(solution)/shard_map/ppermute | solution.py:399
  45.6 3.1 %collective-permute-start.14 = (f32[32,640]{1,0:T(8,128)S(1)}, f32[32,640]{1,0:T(8,128)S(1)}, u32[]{:S(2)}, u32[]{:S(2)}) collective-permute-start(f32[32,640]{1,0:T(8,128)S(1)} %add.67), channel_id=1, source_target_pairs={{0,16},{8,24},{16,0},{24,8},{32,48},{40,56},{48,32},{56,40},{64,80... | collective-permute-start | bytes 245768 | tf_op jit(solution)/shard_map/ppermute | solution.py:399
  48.8 2.5 %collective-permute-done.16 = f32[32,640]{1,0:T(8,128)S(1)} collective-permute-done((f32[32,640]{1,0:T(8,128)S(1)}, f32[32,640]{1,0:T(8,128)S(1)}, u32[]{:S(2)}, u32[]{:S(2)}) %collective-permute-start.16) | collective-permute-done | bytes 81952 | tf_op jit(solution)/shard_map/ppermute | solution.py:399
  54.0 3.1 %collective-permute-start.17 = (f32[32,640]{1,0:T(8,128)S(1)}, f32[32,640]{1,0:T(8,128)S(1)}, u32[]{:S(2)}, u32[]{:S(2)}) collective-permute-start(f32[32,640]{1,0:T(8,128)S(1)} %add_add_fusion.5), channel_id=1, source_target_pairs={{0,64},{8,72},{16,80},{24,88},{32,96},{40,104},{48,112},{56,120},{... | collective-permute-start | bytes 245768 | tf_op jit(solution)/shard_map/ppermute | solution.py:399
  58.8 5.2 %collective-permute-start.8 = (f32[8,128]{1,0:T(8,128)S(1)}, f32[8,128]{1,0:T(8,128)S(1)}, u32[]{:S(2)}, u32[]{:S(2)}) collective-permute-start(f32[8,128]{1,0:T(8,128)S(1)} %get-tuple-element.55), channel_id=1, source_target_pairs={{0,2},{2,4},{4,6},{1,3},{3,5},{5,7},{8,10},{10,12},{12,14},{9,11},... | collective-permute-start | bytes 12296 | tf_op jit(solution)/shard_map/ppermute | solution.py:391
  66.4 5.3 %collective-permute-start.21 = (f32[32,640]{1,0:T(8,128)S(1)}, f32[32,640]{1,0:T(8,128)S(1)}, u32[]{:S(2)}, u32[]{:S(2)}) collective-permute-start(f32[32,640]{1,0:T(8,128)S(1)} %add_add_fusion.4), channel_id=1, source_target_pairs={{0,4},{2,6},{4,0},{6,2},{1,5},{3,7},{5,1},{7,3},{8,12},{10,14},{12... | collective-permute-start | bytes 245768 | tf_op jit(solution)/shard_map/ppermute | solution.py:399
  73.6 4.5 %collective-permute-done.20 = f32[32,640]{1,0:T(8,128)S(1)} collective-permute-done((f32[32,640]{1,0:T(8,128)S(1)}, f32[32,640]{1,0:T(8,128)S(1)}, u32[]{:S(2)}, u32[]{:S(2)}) %collective-permute-start.20) | collective-permute-done | bytes 81952 | tf_op jit(solution)/shard_map/ppermute | solution.py:399
  78.1 6.2 %collective-permute-start.23 = (f32[32,640]{1,0:T(8,128)S(1)}, f32[32,640]{1,0:T(8,128)S(1)}, u32[]{:S(2)}, u32[]{:S(2)}) collective-permute-start(f32[32,640]{1,0:T(8,128)S(1)} %add_add_fusion.3.part), channel_id=1, source_target_pairs={{0,1},{1,0},{2,3},{3,2},{4,5},{5,4},{6,7},{7,6},{8,9},{9,8},{10,11... | collective-permute-start | bytes 245768 | tf_op jit(solution)/shard_map/ppermute | solution.py:413
  87.7 2.2 %shard_map.123 = (f32[64,640]{1,0:T(8,128)S(1)}, f32[96,128]{1,0:T(8,128)S(1)}, f32[8,128]{1,0:T(8,128)S(1)}, f32[8,128]{1,0:T(8,128)S(1)}, f32[32,640]{1,0:T(8,128)S(1)}, /*index=5*/f32[32,640]{1,0:T(8,128)S(1)}) custom-call(s32[1]{0:T(128)} %bitcast.4.core, f32[96,128]{1,0:T(8,128)S(1)} %get-tuple-element.54.x, ...), custom_call_target="tpu_custom_call" | custom-call | tf_op jit(solution)/shard_map/pallas_call | solution.py:37
  89.9 4.4 %collective-permute-start.28 = (f32[32,640]{1,0:T(8,128)S(1)}, f32[32,640]{1,0:T(8,128)S(1)}, u32[]{:S(2)}, u32[]{:S(2)}) collective-permute-start(f32[32,640]{1,0:T(8,128)S(1)} %get-tuple-element.71), channel_id=1, source_target_pairs={{0,1},{1,0},{2,3},{3,2},{4,5},{5,4},{6,7},{7,6},{8,9},{9,8},{10,11... | collective-permute-start | bytes 245768 | tf_op jit(solution)/shard_map/ppermute | solution.py:406
  96.7 2.3 %collective-permute-done.29 = f32[32,640]{1,0:T(8,128)S(1)} collective-permute-done((f32[32,640]{1,0:T(8,128)S(1)}, f32[32,640]{1,0:T(8,128)S(1)}, u32[]{:S(2)}, u32[]{:S(2)}) %collective-permute-start.29) | collective-permute-done | bytes 81952 | tf_op jit(solution)/shard_map/ppermute | solution.py:399
  99.2 3.1 %collective-permute-start.30 = (f32[32,640]{1,0:T(8,128)S(1)}, f32[32,640]{1,0:T(8,128)S(1)}, u32[]{:S(2)}, u32[]{:S(2)}) collective-permute-start(f32[32,640]{1,0:T(8,128)S(1)} %add.78), channel_id=1, source_target_pairs={{0,16},{8,24},{16,0},{24,8},{32,48},{40,56},{48,32},{56,40},{64,80... | collective-permute-start | bytes 245768 | tf_op jit(solution)/shard_map/ppermute | solution.py:399
  102.4 2.5 %collective-permute-done.32 = f32[32,640]{1,0:T(8,128)S(1)} collective-permute-done((f32[32,640]{1,0:T(8,128)S(1)}, f32[32,640]{1,0:T(8,128)S(1)}, u32[]{:S(2)}, u32[]{:S(2)}) %collective-permute-start.32) | collective-permute-done | bytes 81952 | tf_op jit(solution)/shard_map/ppermute | solution.py:399
  106.2 2.6 %collective-permute-start.33 = (f32[32,640]{1,0:T(8,128)S(1)}, f32[32,640]{1,0:T(8,128)S(1)}, u32[]{:S(2)}, u32[]{:S(2)}) collective-permute-start(f32[32,640]{1,0:T(8,128)S(1)} %add_add_fusion.2), channel_id=1, source_target_pairs={{0,64},{8,72},{16,80},{24,88},{32,96},{40,104},{48,112},{56,120},{... | collective-permute-start | bytes 245768 | tf_op jit(solution)/shard_map/ppermute | solution.py:399
  108.7 3.2 %collective-permute-start.24 = (f32[144,128]{1,0:T(8,128)S(1)}, f32[144,128]{1,0:T(8,128)S(1)}, u32[]{:S(2)}, u32[]{:S(2)}) collective-permute-start(f32[144,128]{1,0:T(8,128)S(1)} %pad_maximum_fusion.2), channel_id=1, source_target_pairs={{0,1},{1,8},{8,9},{9,16},{16,17},{17,24},{24,25},{25,32},{32,33},{... | collective-permute-start | bytes 221192 | tf_op jit(solution)/shard_map/ppermute | solution.py:384
  112.0 2.5 %collective-permute-start.38 = (f32[32,640]{1,0:T(8,128)S(1)}, f32[32,640]{1,0:T(8,128)S(1)}, u32[]{:S(2)}, u32[]{:S(2)}) collective-permute-start(f32[32,640]{1,0:T(8,128)S(1)} %add_add_fusion.1), channel_id=1, source_target_pairs={{0,6},{2,4},{4,2},{6,0},{1,7},{3,5},{5,3},{7,1},{8,14},{10,12},{12... | collective-permute-start | bytes 245768 | tf_op jit(solution)/shard_map/ppermute | solution.py:399
  114.5 2.6 %collective-permute-start.37 = (f32[32,640]{1,0:T(8,128)S(1)}, f32[32,640]{1,0:T(8,128)S(1)}, u32[]{:S(2)}, u32[]{:S(2)}) collective-permute-start(f32[32,640]{1,0:T(8,128)S(1)} %add_add_fusion.1), channel_id=1, source_target_pairs={{0,4},{2,6},{4,0},{6,2},{1,5},{3,7},{5,1},{7,3},{8,12},{10,14},{12... | collective-permute-start | bytes 245768 | tf_op jit(solution)/shard_map/ppermute | solution.py:399
  117.7 5.4 %collective-permute-start.25 = (f32[144,128]{1,0:T(8,128)S(1)}, f32[144,128]{1,0:T(8,128)S(1)}, u32[]{:S(2)}, u32[]{:S(2)}) collective-permute-start(f32[144,128]{1,0:T(8,128)S(1)} %pad_maximum_fusion.3), channel_id=1, source_target_pairs={{0,249},{1,0},{8,1},{9,8},{16,9},{17,16},{24,17},{25,24},{32,25},{... | collective-permute-start | bytes 221192 | tf_op jit(solution)/shard_map/ppermute | solution.py:384
  124.4 3.9 %collective-permute-start.39 = (f32[32,640]{1,0:T(8,128)S(1)}, f32[32,640]{1,0:T(8,128)S(1)}, u32[]{:S(2)}, u32[]{:S(2)}) collective-permute-start(f32[32,640]{1,0:T(8,128)S(1)} %add_add_fusion.part), channel_id=1, source_target_pairs={{0,1},{1,0},{2,3},{3,2},{4,5},{5,4},{6,7},{7,6},{8,9},{9,8},{10,11... | collective-permute-start | bytes 245768 | tf_op jit(solution)/shard_map/ppermute | solution.py:413
  128.4 2.4 %collective-permute-start.26 = (f32[16,128]{1,0:T(8,128)S(1)}, f32[16,128]{1,0:T(8,128)S(1)}, u32[]{:S(2)}, u32[]{:S(2)}) collective-permute-start(f32[16,128]{1,0:T(8,128)S(1)} %pad_maximum_fusion.14), channel_id=1, source_target_pairs={{0,2},{2,4},{4,6},{1,3},{3,5},{5,7},{8,10},{10,12},{12,14},{9,11},... | collective-permute-start | bytes 24584 | tf_op jit(solution)/shard_map/ppermute | solution.py:391
  (119 shorter events, 38.5 us)
Async XLA Ops:
  5.7 7.1 %collective-permute-start = (f32[8,128]{1,0:T(8,128)S(1)}, f32[8,128]{1,0:T(8,128)S(1)}, u32[]{:S(2)}, u32[]{:S(2)}) collective-permute-start(f32[8,128]{1,0:T(8,128)S(1)} %get-tuple-element.41), channel_id=1, source_target_pairs={{0,2},{2,4},{4,6},{1,3},{3,5},{5,7},{8,10},{10,12},{12,14},{9,11},... | collective-permute-start | bytes 12296 | tf_op jit(solution)/shard_map/ppermute | solution.py:391
  11.4 7.1 %collective-permute-start.1 = (f32[8,128]{1,0:T(8,128)S(1)}, f32[8,128]{1,0:T(8,128)S(1)}, u32[]{:S(2)}, u32[]{:S(2)}) collective-permute-start(f32[8,128]{1,0:T(8,128)S(1)} %get-tuple-element.42), channel_id=1, source_target_pairs={{2,0},{4,2},{6,4},{3,1},{5,3},{7,5},{10,8},{12,10},{14,12},{11,9},... | collective-permute-start | bytes 12296 | tf_op jit(solution)/shard_map/ppermute | solution.py:391
  27.2 14.4 %collective-permute-start.12 = (f32[32,640]{1,0:T(8,128)S(1)}, f32[32,640]{1,0:T(8,128)S(1)}, u32[]{:S(2)}, u32[]{:S(2)}) collective-permute-start(f32[32,640]{1,0:T(8,128)S(1)} %get-tuple-element.59), channel_id=1, source_target_pairs={{0,1},{1,0},{2,3},{3,2},{4,5},{5,4},{6,7},{7,6},{8,9},{9,8},{10,11... | collective-permute-start | bytes 245768 | tf_op jit(solution)/shard_map/ppermute | solution.py:406
  34.2 19.7 %collective-permute-start.7 = (f32[16,128]{1,0:T(8,128)S(1)}, f32[16,128]{1,0:T(8,128)S(1)}, u32[]{:S(2)}, u32[]{:S(2)}) collective-permute-start(f32[16,128]{1,0:T(8,128)S(1)} %pad_maximum_fusion.13), channel_id=1, source_target_pairs={{2,0},{4,2},{6,4},{3,1},{5,3},{7,5},{10,8},{12,10},{14,12},{11,9},... | collective-permute-start | bytes 24584 | tf_op jit(solution)/shard_map/ppermute | solution.py:391
  35.5 18.5 %collective-permute-start.6 = (f32[16,128]{1,0:T(8,128)S(1)}, f32[16,128]{1,0:T(8,128)S(1)}, u32[]{:S(2)}, u32[]{:S(2)}) collective-permute-start(f32[16,128]{1,0:T(8,128)S(1)} %pad_maximum_fusion.12), channel_id=1, source_target_pairs={{0,2},{2,4},{4,6},{1,3},{3,5},{5,7},{8,10},{10,12},{12,14},{9,11},... | collective-permute-start | bytes 24584 | tf_op jit(solution)/shard_map/ppermute | solution.py:391
  45.5 7.8 %collective-permute-start.15 = (f32[32,640]{1,0:T(8,128)S(1)}, f32[32,640]{1,0:T(8,128)S(1)}, u32[]{:S(2)}, u32[]{:S(2)}) collective-permute-start(f32[32,640]{1,0:T(8,128)S(1)} %add.67), channel_id=1, source_target_pairs={{0,32},{8,40},{16,48},{24,56},{32,0},{40,8},{48,16},{56,24},{64,96... | collective-permute-start | bytes 245768 | tf_op jit(solution)/shard_map/ppermute | solution.py:399
  45.6 8.1 %collective-permute-start.14 = (f32[32,640]{1,0:T(8,128)S(1)}, f32[32,640]{1,0:T(8,128)S(1)}, u32[]{:S(2)}, u32[]{:S(2)}) collective-permute-start(f32[32,640]{1,0:T(8,128)S(1)} %add.67), channel_id=1, source_target_pairs={{0,16},{8,24},{16,0},{24,8},{32,48},{40,56},{48,32},{56,40},{64,80... | collective-permute-start | bytes 245768 | tf_op jit(solution)/shard_map/ppermute | solution.py:399
  53.8 11.5 %collective-permute-start.19 = (f32[32,640]{1,0:T(8,128)S(1)}, f32[32,640]{1,0:T(8,128)S(1)}, u32[]{:S(2)}, u32[]{:S(2)}) collective-permute-start(f32[32,640]{1,0:T(8,128)S(1)} %add_add_fusion.5), channel_id=1, source_target_pairs={{0,192},{8,200},{16,208},{24,216},{32,224},{40,232},{48,240},{56,2... | collective-permute-start | bytes 245768 | tf_op jit(solution)/shard_map/ppermute | solution.py:399
  53.9 11.4 %collective-permute-start.18 = (f32[32,640]{1,0:T(8,128)S(1)}, f32[32,640]{1,0:T(8,128)S(1)}, u32[]{:S(2)}, u32[]{:S(2)}) collective-permute-start(f32[32,640]{1,0:T(8,128)S(1)} %add_add_fusion.5), channel_id=1, source_target_pairs={{0,128},{8,136},{16,144},{24,152},{32,160},{40,168},{48,176},{56,1... | collective-permute-start | bytes 245768 | tf_op jit(solution)/shard_map/ppermute | solution.py:399
  54.0 11.3 %collective-permute-start.17 = (f32[32,640]{1,0:T(8,128)S(1)}, f32[32,640]{1,0:T(8,128)S(1)}, u32[]{:S(2)}, u32[]{:S(2)}) collective-permute-start(f32[32,640]{1,0:T(8,128)S(1)} %add_add_fusion.5), channel_id=1, source_target_pairs={{0,64},{8,72},{16,80},{24,88},{32,96},{40,104},{48,112},{56,120},{... | collective-permute-start | bytes 245768 | tf_op jit(solution)/shard_map/ppermute | solution.py:399
  58.8 25.5 %collective-permute-start.8 = (f32[8,128]{1,0:T(8,128)S(1)}, f32[8,128]{1,0:T(8,128)S(1)}, u32[]{:S(2)}, u32[]{:S(2)}) collective-permute-start(f32[8,128]{1,0:T(8,128)S(1)} %get-tuple-element.55), channel_id=1, source_target_pairs={{0,2},{2,4},{4,6},{1,3},{3,5},{5,7},{8,10},{10,12},{12,14},{9,11},... | collective-permute-start | bytes 12296 | tf_op jit(solution)/shard_map/ppermute | solution.py:391
  64.0 20.3 %collective-permute-start.9 = (f32[8,128]{1,0:T(8,128)S(1)}, f32[8,128]{1,0:T(8,128)S(1)}, u32[]{:S(2)}, u32[]{:S(2)}) collective-permute-start(f32[8,128]{1,0:T(8,128)S(1)} %get-tuple-element.56), channel_id=1, source_target_pairs={{2,0},{4,2},{6,4},{3,1},{5,3},{7,5},{10,8},{12,10},{14,12},{11,9},... | collective-permute-start | bytes 12296 | tf_op jit(solution)/shard_map/ppermute | solution.py:391
  65.3 6.4 %collective-permute-start.22 = (f32[32,640]{1,0:T(8,128)S(1)}, f32[32,640]{1,0:T(8,128)S(1)}, u32[]{:S(2)}, u32[]{:S(2)}) collective-permute-start(f32[32,640]{1,0:T(8,128)S(1)} %add_add_fusion.4), channel_id=1, source_target_pairs={{0,6},{2,4},{4,2},{6,0},{1,7},{3,5},{5,3},{7,1},{8,14},{10,12},{12... | collective-permute-start | bytes 245768 | tf_op jit(solution)/shard_map/ppermute | solution.py:399
  66.4 7.2 %collective-permute-start.21 = (f32[32,640]{1,0:T(8,128)S(1)}, f32[32,640]{1,0:T(8,128)S(1)}, u32[]{:S(2)}, u32[]{:S(2)}) collective-permute-start(f32[32,640]{1,0:T(8,128)S(1)} %add_add_fusion.4), channel_id=1, source_target_pairs={{0,4},{2,6},{4,0},{6,2},{1,5},{3,7},{5,1},{7,3},{8,12},{10,14},{12... | collective-permute-start | bytes 245768 | tf_op jit(solution)/shard_map/ppermute | solution.py:399
  71.7 6.4 %collective-permute-start.20 = (f32[32,640]{1,0:T(8,128)S(1)}, f32[32,640]{1,0:T(8,128)S(1)}, u32[]{:S(2)}, u32[]{:S(2)}) collective-permute-start(f32[32,640]{1,0:T(8,128)S(1)} %add_add_fusion.4), channel_id=1, source_target_pairs={{0,2},{2,0},{4,6},{6,4},{1,3},{3,1},{5,7},{7,5},{8,10},{10,8},{12,... | collective-permute-start | bytes 245768 | tf_op jit(solution)/shard_map/ppermute | solution.py:399
  78.1 9.6 %collective-permute-start.23 = (f32[32,640]{1,0:T(8,128)S(1)}, f32[32,640]{1,0:T(8,128)S(1)}, u32[]{:S(2)}, u32[]{:S(2)}) collective-permute-start(f32[32,640]{1,0:T(8,128)S(1)} %add_add_fusion.3.part), channel_id=1, source_target_pairs={{0,1},{1,0},{2,3},{3,2},{4,5},{5,4},{6,7},{7,6},{8,9},{9,8},{10,11... | collective-permute-start | bytes 245768 | tf_op jit(solution)/shard_map/ppermute | solution.py:413
  95.4 35.4 %collective-permute-start.27 = (f32[16,128]{1,0:T(8,128)S(1)}, f32[16,128]{1,0:T(8,128)S(1)}, u32[]{:S(2)}, u32[]{:S(2)}) collective-permute-start(f32[16,128]{1,0:T(8,128)S(1)} %pad_maximum_fusion.15), channel_id=1, source_target_pairs={{2,0},{4,2},{6,4},{3,1},{5,3},{7,5},{10,8},{12,10},{14,12},{11,9},... | collective-permute-start | bytes 24584 | tf_op jit(solution)/shard_map/ppermute | solution.py:391
  105.4 6.6 %collective-permute-start.35 = (f32[32,640]{1,0:T(8,128)S(1)}, f32[32,640]{1,0:T(8,128)S(1)}, u32[]{:S(2)}, u32[]{:S(2)}) collective-permute-start(f32[32,640]{1,0:T(8,128)S(1)} %add_add_fusion.2), channel_id=1, source_target_pairs={{0,192},{8,200},{16,208},{24,216},{32,224},{40,232},{48,240},{56,2... | collective-permute-start | bytes 245768 | tf_op jit(solution)/shard_map/ppermute | solution.py:399
  105.5 6.5 %collective-permute-start.34 = (f32[32,640]{1,0:T(8,128)S(1)}, f32[32,640]{1,0:T(8,128)S(1)}, u32[]{:S(2)}, u32[]{:S(2)}) collective-permute-start(f32[32,640]{1,0:T(8,128)S(1)} %add_add_fusion.2), channel_id=1, source_target_pairs={{0,128},{8,136},{16,144},{24,152},{32,160},{40,168},{48,176},{56,1... | collective-permute-start | bytes 245768 | tf_op jit(solution)/shard_map/ppermute | solution.py:399
  108.7 22.8 %collective-permute-start.24 = (f32[144,128]{1,0:T(8,128)S(1)}, f32[144,128]{1,0:T(8,128)S(1)}, u32[]{:S(2)}, u32[]{:S(2)}) collective-permute-start(f32[144,128]{1,0:T(8,128)S(1)} %pad_maximum_fusion.2), channel_id=1, source_target_pairs={{0,1},{1,8},{8,9},{9,16},{16,17},{17,24},{24,25},{25,32},{32,33},{... | collective-permute-start | bytes 221192 | tf_op jit(solution)/shard_map/ppermute | solution.py:384
  114.5 8.7 %collective-permute-start.37 = (f32[32,640]{1,0:T(8,128)S(1)}, f32[32,640]{1,0:T(8,128)S(1)}, u32[]{:S(2)}, u32[]{:S(2)}) collective-permute-start(f32[32,640]{1,0:T(8,128)S(1)} %add_add_fusion.1), channel_id=1, source_target_pairs={{0,4},{2,6},{4,0},{6,2},{1,5},{3,7},{5,1},{7,3},{8,12},{10,14},{12... | collective-permute-start | bytes 245768 | tf_op jit(solution)/shard_map/ppermute | solution.py:399
  117.1 7.3 %collective-permute-start.36 = (f32[32,640]{1,0:T(8,128)S(1)}, f32[32,640]{1,0:T(8,128)S(1)}, u32[]{:S(2)}, u32[]{:S(2)}) collective-permute-start(f32[32,640]{1,0:T(8,128)S(1)} %add_add_fusion.1), channel_id=1, source_target_pairs={{0,2},{2,0},{4,6},{6,4},{1,3},{3,1},{5,7},{7,5},{8,10},{10,8},{12,... | collective-permute-start | bytes 245768 | tf_op jit(solution)/shard_map/ppermute | solution.py:399
  117.7 13.8 %collective-permute-start.25 = (f32[144,128]{1,0:T(8,128)S(1)}, f32[144,128]{1,0:T(8,128)S(1)}, u32[]{:S(2)}, u32[]{:S(2)}) collective-permute-start(f32[144,128]{1,0:T(8,128)S(1)} %pad_maximum_fusion.3), channel_id=1, source_target_pairs={{0,249},{1,0},{8,1},{9,8},{16,9},{17,16},{24,17},{25,24},{32,25},{... | collective-permute-start | bytes 221192 | tf_op jit(solution)/shard_map/ppermute | solution.py:384
  124.4 8.8 %collective-permute-start.39 = (f32[32,640]{1,0:T(8,128)S(1)}, f32[32,640]{1,0:T(8,128)S(1)}, u32[]{:S(2)}, u32[]{:S(2)}) collective-permute-start(f32[32,640]{1,0:T(8,128)S(1)} %add_add_fusion.part), channel_id=1, source_target_pairs={{0,1},{1,0},{2,3},{3,2},{4,5},{5,4},{6,7},{7,6},{8,9},{9,8},{10,11... | collective-permute-start | bytes 245768 | tf_op jit(solution)/shard_map/ppermute | solution.py:413
  (29 other events, 128.5 us)

commit v2 on v1

v2 whole, which is shorter than its diff:
```python
import functools

import jax
import jax.numpy as jnp
from jax import lax
from jax.experimental import pallas as pl
from jax.experimental.pallas import tpu as pltpu
from jax.sharding import PartitionSpec as P

time_step = 0.2
diffusivity = 0.5
learn_rate = 200.0
highest = lax.Precision.HIGHEST
f32 = jnp.float32
bf16 = jnp.bfloat16

LEVELS = 12
CHANNELS = 4 * LEVELS
HIDDEN = 64
TAPS = 9 * CHANNELS
MIX_AT = 512
OUT_AT = 576
AREA_AT = 624
PACKED = 640
COLUMNS_AT = 96
EDGE_AT = 112
FINE = 512
COARSE = 128
VMEM_LIMIT = 48 * 1024 * 1024


def struct(*shape):
    return jax.ShapeDtypeStruct(shape, f32)


def call(kernel, outs, *args, scratch=(), smem=0, remote=0, flops=0, bytes_accessed=0):
    specs = [pl.BlockSpec(memory_space=pltpu.SMEM)] * smem
    specs += [pl.BlockSpec(memory_space=pl.ANY)] * remote
    specs += [pl.BlockSpec(memory_space=pltpu.VMEM)] * (len(args) - smem - remote)
    return pl.pallas_call(
        kernel,
        out_shape=outs,
        in_specs=specs,
        out_specs=[pl.BlockSpec(memory_space=pltpu.VMEM)] * len(outs),
        scratch_shapes=scratch,
        compiler_params=pltpu.CompilerParams(vmem_limit_bytes=VMEM_LIMIT),
        cost_estimate=pl.CostEstimate(
            flops=flops, bytes_accessed=bytes_accessed, transcendentals=0
        ),
    )(*args)


def exact_dot(value, selector):
    high = value.astype(bf16)
    rest = value - high.astype(f32)
    middle = rest.astype(bf16)
    low = (rest - middle.astype(f32)).astype(bf16)
    dot = functools.partial(jnp.dot, preferred_element_type=f32)
    return (dot(low, selector) + dot(middle, selector)) + dot(high, selector)


def pooling_matrix():
    fine = lax.broadcasted_iota(jnp.int32, (FINE, COARSE), 0) >> 2
    coarse = lax.broadcasted_iota(jnp.int32, (FINE, COARSE), 1)
    return jnp.where(fine == coarse, f32(1.0 / 16.0), f32(0.0)).astype(bf16)


def spreading_matrix():
    fine = lax.broadcasted_iota(jnp.int32, (COARSE, FINE), 1) >> 2
    coarse = lax.broadcasted_iota(jnp.int32, (COARSE, FINE), 0)
    return jnp.where(fine == coarse, f32(1.0), f32(0.0)).astype(bf16)


def lane_index(shape):
    return lax.broadcasted_iota(jnp.int32, shape, len(shape) - 1)


def block_rows(which, block):
    start = (4 * which + block) * 8 * LEVELS
    return slice(start, start + 8 * LEVELS)


def fill_blocks(blocks, refs):
    for which, ref in enumerate(refs):
        for block in range(4):
            blocks[block_rows(which, block), :] = ref[:, 128 * block : 128 * (block + 1)]


def fetch(pairs, semaphore):
    copies = [
        pltpu.make_async_copy(source, target, semaphore.at[at])
        for at, (source, target) in enumerate(pairs)
    ]
    for copy in copies:
        copy.start()
    return copies


def longitude_row(blocks, which, block, lon):
    return blocks[pl.ds(block_rows(which, block).start + lon, LEVELS, stride=8), :]


def coarsen(blocks, sums_ref, x_ref, target_ref):
    for row in range(2):
        for block in range(4):
            total = None
            for lon in range(4 * row, 4 * row + 4):
                t, s, u, v = (longitude_row(blocks, which, block, lon) for which in range(4))
                terms = (t, s, u, v, u * t, v * t, u * s, v * s)
                total = terms if total is None else [a + b for a, b in zip(total, terms)]
            for at, value in enumerate(total):
                start = 2 * CHANNELS * row + LEVELS * at
                sums_ref[start : start + LEVELS, 128 * block : 128 * (block + 1)] = value
    means = exact_dot(sums_ref[...], pooling_matrix())
    for row in range(2):
        x = means[2 * CHANNELS * row : 2 * CHANNELS * row + CHANNELS]
        products = means[2 * CHANNELS * row + CHANNELS : 2 * CHANNELS * (row + 1)]
        ct, cs, cu, cv = (x[LEVELS * k : LEVELS * (k + 1)] for k in range(4))
        x_ref[CHANNELS * row : CHANNELS * (row + 1), :] = x
        own = jnp.concatenate([cu * ct, cv * ct, cu * cs, cv * cs], 0)
        target_ref[CHANNELS * row : CHANNELS * (row + 1), :] = products - own


def fill_edges(blocks, fields, column_fields, mask_ref, x_ref, first_ref, last_ref, low_ref, high_ref):
    depth = (first_ref.shape[0] - EDGE_AT) // 4
    for lon, out in ((0, first_ref), (7, last_ref)):
        out[0:COLUMNS_AT, :] = x_ref[...]
        out[COLUMNS_AT:, :] = jnp.zeros((out.shape[0] - COLUMNS_AT, COARSE), f32)
        for block in range(4):
            start = EDGE_AT + block * depth
            for which in range(fields):
                at = start + which * LEVELS
                out[at : at + LEVELS, :] = longitude_row(blocks, which, block, lon)
            if mask_ref is not None:
                at = start + fields * LEVELS
                out[at : at + 1, :] = mask_ref[lon : lon + 1, 128 * block : 128 * (block + 1)]
    turned = x_ref[...].T
    for out, block, column, inner in ((low_ref, 0, 0, 1), (high_ref, 3, 127, 126)):
        out[...] = jnp.zeros(out.shape, f32)
        for at, which in enumerate(column_fields):
            out[at : at + 1, 0 : 8 * LEVELS] = blocks[block_rows(which, block), :].T[column : column + 1]
        if mask_ref is not None:
            here = mask_ref[:, 128 * block : 128 * (block + 1)]
            out[3:4, 0:8] = here.T[column : column + 1]
        out[4:5, 0 : 2 * CHANNELS] = turned[column : column + 1]
        out[5:6, 0 : 2 * CHANNELS] = turned[inner : inner + 1]


def prepare_kernel(
    t, s, u, v, mask, x, target, weight, first, last, low, high, sums, blocks, mask_here, mask_values, semaphore
):
    pairs = [(mask, mask_here)]
    for which, ref in enumerate((t, s, u, v)):
        for block in range(4):
            pairs.append((ref.at[:, pl.ds(128 * block, 128)], blocks.at[block_rows(which, block), :]))
    copies = fetch(pairs, semaphore)
    for copy in copies:
        copy.wait()
    m = mask_here[...].astype(f32)
    mask_values[...] = m
    coarsen(blocks, sums, x, target)
    fill_edges(blocks, 3, (0, 1, 3), mask_values, x, first, last, low, high)
    rows = jnp.concatenate(
        [jnp.sum(m[0:4], axis=0, keepdims=True), jnp.sum(m[4:8], axis=0, keepdims=True)]
        + [jnp.zeros((6, FINE), f32)],
        0,
    )
    weight[...] = jnp.dot(rows.astype(bf16), pooling_matrix(), preferred_element_type=f32)


def dot(a, b):
    return jnp.dot(a, b, precision=highest, preferred_element_type=f32)


def dot_nt(a, b):
    return lax.dot_general(
        a, b, (((1,), (1,)), ((), ())), precision=highest, preferred_element_type=f32
    )


def column_matrix(low, high, west, east):
    rows = []
    for at in (4, 5):
        for ref, start in ((low, 0), (high, 0)):
            rows.append(ref[start + at : start + at + 1, :])
        for ref in (west, east):
            for start in (COLUMNS_AT, COLUMNS_AT + 8):
                rows.append(ref[start + at : start + at + 1, :])
    rows.append(jnp.zeros((4, COARSE), f32))
    return jnp.concatenate(rows, 0).T


def shifted_rows(value, before, after):
    lanes = lane_index((CHANNELS, COARSE))
    return (
        jnp.where(lanes == 0, before, pltpu.roll(value, 1, 1)),
        value,
        jnp.where(lanes == COARSE - 1, after, pltpu.roll(value, COARSE - 1, 1)),
    )


def coarse_rows(x, west, east):
    return (
        (west[0:CHANNELS, :], 0, 2),
        (west[CHANNELS : 2 * CHANNELS, :], CHANNELS, 2),
        (x[0:CHANNELS, :], 0, 0),
        (x[CHANNELS : 2 * CHANNELS, :], CHANNELS, 0),
        (east[0:CHANNELS, :], 0, 4),
        (east[CHANNELS : 2 * CHANNELS, :], CHANNELS, 4),
    )


def fill_taps(taps, rows, columns, centres):
    for at, (value, start, pair) in enumerate(rows):
        if not any(abs(at - centre) <= 1 for centre in centres):
            continue
        channels = slice(start, start + CHANNELS)
        shifted = shifted_rows(
            value, columns[channels, pair : pair + 1], columns[channels, pair + 1 : pair + 2]
        )
        for place, centre in enumerate(centres):
            tap = at - centre + 1
            if 0 <= tap < 3:
                for side in range(3):
                    begin = (3 * tap + side) * CHANNELS
                    taps[begin : begin + CHANNELS, COARSE * place : COARSE * (place + 1)] = shifted[side]


def fill_side_taps(taps, rows, columns, start_lane):
    lanes = lane_index((CHANNELS, COARSE))
    for tap in range(3):
        for side in range(3):
            out = jnp.zeros((CHANNELS, COARSE), f32)
            for row in range(2):
                value, start, pair = rows[row + tap + 1]
                channels = slice(start, start + CHANNELS)
                low = (
                    columns[channels, 6 + pair : 7 + pair],
                    columns[channels, pair : pair + 1],
                    value[:, 0:1],
                )[side]
                high = (
                    value[:, COARSE - 1 : COARSE],
                    columns[channels, pair + 1 : pair + 2],
                    columns[channels, 7 + pair : 8 + pair],
                )[side]
                out = jnp.where(lanes == row, low, out)
                out = jnp.where(lanes == 2 + row, high, out)
            begin = (3 * tap + side) * CHANNELS
            taps[begin : begin + CHANNELS, start_lane : start_lane + COARSE] = out


def network_step(
    core, x, west, east, low, high, target, weight, packed, pred, own, other, taps, grads
):
    columns = column_matrix(low, high, west, east)
    fill_taps(taps, coarse_rows(x, west, east), columns, (2, 3))
    kernel = packed[:, 0:TAPS]
    mix = packed[:, MIX_AT : MIX_AT + HIDDEN]
    out_turned = packed[:, OUT_AT : OUT_AT + CHANNELS]
    hidden_one = jnp.tanh(dot(kernel, taps[...]))
    hidden_two = jnp.tanh(dot(mix, hidden_one))
    predicted = dot(out_turned.T, hidden_two)
    pred[0:CHANNELS, :] = predicted[:, 0:COARSE]
    pred[CHANNELS : 2 * CHANNELS, :] = predicted[:, COARSE : 2 * COARSE]
    back_out = jnp.concatenate(
        [
            weight[row : row + 1, :]
            * (
                predicted[:, COARSE * row : COARSE * (row + 1)]
                - target[CHANNELS * row : CHANNELS * (row + 1), :]
            )
            for row in range(2)
        ],
        1,
    )
    back_two = dot(out_turned, back_out) * (1.0 - hidden_two * hidden_two)
    back_one = dot(mix.T, back_two) * (1.0 - hidden_one * hidden_one)
    grads[:, MIX_AT - 128 : PACKED] = jnp.zeros((HIDDEN, PACKED - MIX_AT + 128), f32)
    grads[:, 0:TAPS] = dot_nt(back_one, taps[...])
    grads[:, MIX_AT : MIX_AT + HIDDEN] = dot_nt(back_two, hidden_one)
    grads[:, OUT_AT : OUT_AT + CHANNELS] = dot_nt(hidden_two, back_out)
    area = jnp.sum(weight[0:2, :], axis=(0, 1), keepdims=True)
    grads[:, AREA_AT : AREA_AT + 1] = jnp.broadcast_to(area, (HIDDEN, 1))
    half = HIDDEN // 2
    own[...] = grads[pl.ds(pl.multiple_of(core[0] * half, half), half), :]
    other[...] = grads[pl.ds(pl.multiple_of((1 - core[0]) * half, half), half), :]


def descended(core, packed, part, back):
    half = HIDDEN // 2
    mine, theirs = part[...], back[...]
    first = core[0] == 0
    total = jnp.concatenate(
        [jnp.where(first, mine, theirs), jnp.where(first, theirs, mine)], 0
    )
    area = total[0:1, AREA_AT : AREA_AT + 1]
    step = (learn_rate * 2.0 / CHANNELS) / area
    return packed[...] - step * total


def first_network_kernel(core, x, west, east, low, high, target, weight, packed, *rest):
    network_step(core, x, west, east, low, high, target, weight, packed, *rest)


def next_network_kernel(
    core, x, west, east, low, high, target, weight, packed, part, back, renewed, *rest
):
    renewed[...] = descended(core, packed, part, back)
    network_step(core, x, west, east, low, high, target, weight, renewed, *rest)


def last_kernel(core, packed, part, back, kernel, mix, out):
    renewed = descended(core, packed, part, back)
    kernel[...] = renewed[:, 0:TAPS]
    mix[...] = renewed[:, MIX_AT : MIX_AT + HIDDEN]
    out[...] = renewed[:, OUT_AT : OUT_AT + CHANNELS].T


def forcing(place, x, pred, packed, west, east, low, high, taps):
    rows = coarse_rows(x, west, east)
    columns = column_matrix(low, high, west, east)
    fill_taps(taps, rows, columns, (1, 4))
    fill_side_taps(taps, rows, columns, 2 * COARSE)
    hidden = jnp.tanh(dot(packed[:, 0:TAPS], taps[...]))
    hidden = jnp.tanh(dot(packed[:, MIX_AT : MIX_AT + HIDDEN], hidden))
    beside = dot(packed[:, OUT_AT : OUT_AT + CHANNELS].T, hidden)
    sides = beside[:, 2 * COARSE :]
    sides_low = jnp.where(place[1] == 0, 0.0, sides)
    sides_high = jnp.where(place[2] == 0, 0.0, sides)
    before = (beside[:, 0:COARSE], pred[0:CHANNELS, :])
    after = (pred[CHANNELS : 2 * CHANNELS, :], beside[:, COARSE : 2 * COARSE])
    pieces = []
    for row in range(2):
        value = pred[CHANNELS * row : CHANNELS * (row + 1), :]
        along = after[row] - before[row]
        south, _, north = shifted_rows(value, sides_low[:, row : row + 1], sides_high[:, 2 + row : 3 + row])
        across = north - south
        for at in (0, 2 * LEVELS):
            pieces.append(-0.5 * (along[at : at + LEVELS] + across[at + LEVELS : at + 2 * LEVELS]))
            pieces.append(jnp.zeros((4, COARSE), f32))
    return exact_dot(jnp.concatenate(pieces, 0), spreading_matrix())


def advance(t, s, u, v, mask, force, fixed, moving, t_out, s_out):
    fixed_west, fixed_east, fixed_low, fixed_high = fixed
    west, east, low, high = moving
    m = mask[...].astype(f32)
    shape = (8, FINE)
    lanes = lane_index(shape)
    subs = lax.broadcasted_iota(jnp.int32, shape, 0)

    def edge_row(ref, at):
        depth = (ref.shape[0] - EDGE_AT) // 4
        starts = [EDGE_AT + depth * block + at for block in range(4)]
        return jnp.concatenate([ref[start : start + 1, :] for start in starts], 1)

    def neighbours_lon(value, row_west, row_east):
        return (
            jnp.where(subs == 0, row_west, pltpu.roll(value, 1, 0)),
            jnp.where(subs == 7, row_east, pltpu.roll(value, 7, 0)),
        )

    def neighbours_lat(value, column_low, column_high):
        return (
            jnp.where(lanes == 0, column_low, pltpu.roll(value, 1, 1)),
            jnp.where(lanes == FINE - 1, column_high, pltpu.roll(value, FINE - 1, 1)),
        )

    fixed_low_turned = fixed_low[...].T
    fixed_high_turned = fixed_high[...].T
    low_turned = low[...].T
    high_turned = high[...].T
    m_west, m_east = neighbours_lon(
        m, edge_row(fixed_west, 3 * LEVELS), edge_row(fixed_east, 3 * LEVELS)
    )
    m_low, m_high = neighbours_lat(m, fixed_low_turned[0:8, 3:4], fixed_high_turned[0:8, 3:4])
    open_west, open_east, open_low, open_high = m * m_west, m * m_east, m * m_low, m * m_high
    mix_west, mix_east = diffusivity * open_west, diffusivity * open_east
    mix_low, mix_high = diffusivity * open_low, diffusivity * open_high
    pace = time_step * m
    for level in range(LEVELS):
        at = slice(8 * level, 8 * (level + 1))
        u_here, v_here = u[at, :], v[at, :]
        u_west, u_east = neighbours_lon(
            u_here, edge_row(fixed_west, 2 * LEVELS + level), edge_row(fixed_east, 2 * LEVELS + level)
        )
        v_low, v_high = neighbours_lat(v_here, fixed_low_turned[at, 2:3], fixed_high_turned[at, 2:3])
        speed_west = 0.25 * (u_here + u_west) * open_west
        speed_east = 0.25 * (u_here + u_east) * open_east
        speed_low = 0.25 * (v_here + v_low) * open_low
        speed_high = 0.25 * (v_here + v_high) * open_high
        for which, (q_ref, out) in enumerate(((t, t_out), (s, s_out))):
            q = q_ref[at, :]
            q_west, q_east = neighbours_lon(
                q, edge_row(west, LEVELS * which + level), edge_row(east, LEVELS * which + level)
            )
            q_low, q_high = neighbours_lat(
                q, low_turned[at, which : which + 1], high_turned[at, which : which + 1]
            )
            flux_east = speed_east * (q + q_east) - mix_east * (q_east - q)
            flux_west = speed_west * (q_west + q) - mix_west * (q - q_west)
            flux_high = speed_high * (q + q_high) - mix_high * (q_high - q)
            flux_low = speed_low * (q_low + q) - mix_low * (q - q_low)
            row = 16 * which + level
            push = jnp.where(subs < 4, force[row : row + 1], force[32 + row : 33 + row])
            out[at, :] = q + pace * (push - (flux_east - flux_west) - (flux_high - flux_low))


def first_advance_kernel(place, *refs):
    t, s, u, v, mask, x, pred, packed, west, east, low, high = refs[:12]
    t_out, s_out, x_out, target, first, last, low_out, high_out = refs[12:20]
    sums, blocks, taps, t_here, s_here, u_here, v_here, semaphore = refs[20:]
    here = (t_here, s_here, u_here, v_here)
    copies = fetch(list(zip((t, s, u, v), here)), semaphore)
    halo = (west, east, low, high)
    force = forcing(place, x, pred, packed, *halo, taps)
    for copy in copies:
        copy.wait()
    advance(*here, mask, force, halo, halo, t_out, s_out)
    fill_blocks(blocks, (t_out, s_out, u_here, v_here))
    coarsen(blocks, sums, x_out, target)
    fill_edges(blocks, 2, (0, 1), None, x_out, first, last, low_out, high_out)


def next_advance_kernel(place, *refs):
    t, s, u, v, mask, x, pred, packed = refs[:8]
    fixed, moving, (t_out, s_out, taps) = refs[8:12], refs[12:16], refs[16:]
    force = forcing(place, x, pred, packed, *moving, taps)
    advance(t, s, u, v, mask, force, fixed, moving, t_out, s_out)


def ring(axis, step):
    count = 1
    for name in axis:
        count *= lax.axis_size(name)
    return [(i, (i + step) % count) for i in range(count)]


def exchange_lon(first, last):
    axis = ("lon", "grp")
    return lax.ppermute(last, axis, ring(axis, 1)), lax.ppermute(first, axis, ring(axis, -1))


def exchange_lat(low, high):
    count = lax.axis_size("lat")
    up = [(i, i + 1) for i in range(count - 1)]
    down = [(i + 1, i) for i in range(count - 1)]
    return lax.ppermute(high, "lat", up), lax.ppermute(low, "lat", down)


def flipped(axis, mask):
    return [(i, i ^ mask) for i in range(lax.axis_size(axis))]


def exchanged_sum(value, axis, masks):
    parts = [lax.ppermute(value, axis, flipped(axis, mask)) for mask in masks]
    if len(parts) == 1:
        return value + parts[0]
    return (value + parts[0]) + (parts[1] + parts[2])


def sum_over_devices(own, other):
    part = own + lax.ppermute(other, "grp", flipped("grp", 1))
    part = exchanged_sum(part, "lon", (1,))
    low = 2
    while low < lax.axis_size("lon"):
        part = exchanged_sum(part, "lon", (low, 2 * low, 3 * low))
        low *= 4
    part = exchanged_sum(part, ("lon", "lat"), (1, 6, 3))
    return part, lax.ppermute(part, "grp", flipped("grp", 1))


def shards(
    thermal_anomaly,
    saltiness_anomaly,
    zonal_flow_speed,
    meridional_flow_speed,
    water_indicator,
    kernel_factors,
    hidden_pointwise_factors,
    final_pointwise_factors,
):
    fields = tuple(
        value.reshape(8 * LEVELS, FINE)
        for value in (thermal_anomaly, saltiness_anomaly, zonal_flow_speed, meridional_flow_speed)
    )
    packed = jnp.concatenate(
        [
            kernel_factors.reshape(HIDDEN, TAPS),
            jnp.zeros((HIDDEN, MIX_AT - TAPS), f32),
            hidden_pointwise_factors,
            final_pointwise_factors.T,
            jnp.zeros((HIDDEN, PACKED - AREA_AT), f32),
        ],
        1,
    )
    blocks = pltpu.VMEM((16 * 8 * LEVELS, 128), f32)
    lat = lax.axis_index("lat")
    lat_last = lax.axis_size("lat") - 1
    place = jnp.stack(
        [lax.axis_index("grp"), (lat != 0).astype(jnp.int32), (lat != lat_last).astype(jnp.int32)]
    ).astype(jnp.int32)
    field_scratch = pltpu.VMEM((8 * LEVELS, FINE), f32)
    sums = [pltpu.VMEM((4 * CHANNELS, FINE), f32), pltpu.VMEM((16 * 8 * LEVELS, 128), f32)]
    wide = struct(2 * CHANNELS, COARSE)
    tile = struct(8, 128)
    half = struct(HIDDEN // 2, PACKED)
    field = struct(8 * LEVELS, FINE)
    network_outs = [wide, half, half]
    network_scratch = [pltpu.VMEM((TAPS, 2 * COARSE), f32), pltpu.VMEM((HIDDEN, PACKED), f32)]
    side_taps = pltpu.VMEM((TAPS, 3 * COARSE), f32)

    def halo(first, last, low, high):
        south, north = exchange_lat(low, high)
        columns = jnp.concatenate([south, north], 0)
        first = lax.dynamic_update_slice_in_dim(first, columns, COLUMNS_AT, 0)
        last = lax.dynamic_update_slice_in_dim(last, columns, COLUMNS_AT, 0)
        return *exchange_lon(first, last), south, north

    edge = struct(EDGE_AT + 160, 128)
    x, target, weight, *edges = call(
        prepare_kernel,
        [wide, wide, tile, edge, edge, tile, tile],
        *fields, water_indicator,
        scratch=sums
        + [
            pltpu.VMEM((8, FINE), jnp.int32),
            pltpu.VMEM((8, FINE), f32),
            pltpu.SemaphoreType.DMA((17,)),
        ],
        remote=5,
    )
    fixed = halo(*edges)
    pred, own, other = call(
        first_network_kernel,
        network_outs,
        place, x, *fixed, target, weight, packed,
        scratch=network_scratch,
        smem=1,
    )
    part, back = sum_over_devices(own, other)
    edge = struct(EDGE_AT + 96, 128)
    t, s, x, target, *edges = call(
        first_advance_kernel,
        [field, field, wide, wide, edge, edge, tile, tile],
        place, *fields, water_indicator, x, pred, packed, *fixed,
        scratch=sums + [side_taps] + [field_scratch] * 4 + [pltpu.SemaphoreType.DMA((4,))],
        smem=1,
        remote=4,
    )
    moving = halo(*edges)
    packed, pred, own, other = call(
        next_network_kernel,
        [struct(HIDDEN, PACKED)] + network_outs,
        place, x, *moving, target, weight, packed, part, back,
        scratch=network_scratch,
        smem=1,
    )
    part, back = sum_over_devices(own, other)
    t, s = call(
        next_advance_kernel,
        [field, field],
        place, t, s, *fields[2:], water_indicator, x, pred, packed, *fixed, *moving,
        scratch=[side_taps],
        smem=1,
    )
    kernel, mix, out = call(
        last_kernel,
        [struct(HIDDEN, TAPS), struct(HIDDEN, HIDDEN), struct(CHANNELS, HIDDEN)],
        place, packed, part, back,
        smem=1,
    )
    return (
        t.reshape(thermal_anomaly.shape),
        s.reshape(thermal_anomaly.shape),
        kernel.reshape(kernel_factors.shape),
        mix,
        out,
    )


def solution(mesh):
    field = P(None, ("lon", "grp"), "lat")
    return jax.shard_map(
        shards,
        mesh=mesh,
        in_specs=(field, field, field, field, P(("lon", "grp"), "lat"), P(), P(), P()),
        out_specs=(field, field, P(), P(), P()),
        check_vma=False,
    )
```

time: 135 us -> 123 us (0.911)
  starting transfers between devices: 87 us -> 63.3 us
  Pallas kernels: 9.41 us -> 15.8 us
  waiting for transfers between devices: 30.2 us -> 35.1 us
    ppermute x8 -> x4, starting transfers between devices: 24.5 us -> 13.8 us  [exchange_lat(): return (lax.ppermute(high, 'lat', up), lax.ppermute(low, 'lat', down))]
    pallas_call x7 -> x6, Pallas kernels: 9.41 us -> 15.8 us  [call(): pl.pallas_call(kernel, out_shape=outs, in_specs=specs, out_specs=[pl.Bloc...]
    ppermute x4 -> x2, starting transfers between devices: 6.01 us -> 1.07 us  [exchange_lon(): lax.ppermute(last, axis, ring(axis, 1))]
    ppermute x20, waiting for transfers between devices: 19.1 us -> 23.6 us  [exchanged_sum(): parts = [lax.ppermute(value, axis, flipped(axis, mask)) for mask in masks]]
    ppermute x4 -> x2, starting transfers between devices: 9.44 us -> 6.14 us  [exchange_lon(): lax.ppermute(first, axis, ring(axis, -1))]
    ppermute x20, starting transfers between devices: 25.6 us -> 23.8 us  [exchanged_sum(): parts = [lax.ppermute(value, axis, flipped(axis, mask)) for mask in masks]]
    ppermute x2, starting transfers between devices: 10.1 us -> 8.52 us  [sum_over_devices(): return (part, lax.ppermute(part, 'grp', flipped('grp', 1)))]
    ppermute x2, starting transfers between devices: 11.4 us -> 10 us  [sum_over_devices(): part = own + lax.ppermute(other, 'grp', flipped('grp', 1))]
  transfers between devices with their start and end apart: 40 -> 32, of which waited for: 13 -> 18; matrix products, arithmetic and copies ran while one was open for 0% -> 0% of each run, Pallas kernels for 3% -> 7%
where the time goes in v2:
time: 123 us; the launch traced here: 122 us
  starting transfers between devices  63.3 us (51%)
  waiting for transfers between devices  35.1 us (29%)
  Pallas kernels  15.8 us (13%)
  local copies, waits for them, and re-layouts  6.86 us (6%)
    ppermute x20, starting transfers between devices, exchanged_sum(): parts = [lax.ppermute(value, axis, flipped(axis, mask)) for mask in masks]  23.8 us
    ppermute x20, waiting for transfers between devices, exchanged_sum(): parts = [lax.ppermute(value, axis, flipped(axis, mask)) for mask in masks]  23.6 us
    pallas_call x6, Pallas kernels, call(): pl.pallas_call(kernel, out_shape=outs, in_specs=specs, out_specs=[pl.Bloc...  15.8 us
    ppermute x4, starting transfers between devices, exchange_lat(): return (lax.ppermute(high, 'lat', up), lax.ppermute(low, 'lat', down))  13.8 us
    ppermute x2, starting transfers between devices, sum_over_devices(): part = own + lax.ppermute(other, 'grp', flipped('grp', 1))  10 us
    ppermute x2, starting transfers between devices, sum_over_devices(): return (part, lax.ppermute(part, 'grp', flipped('grp', 1)))  8.52 us
    ppermute x2, starting transfers between devices, exchange_lon(): lax.ppermute(first, axis, ring(axis, -1))  6.14 us
    unnamed x29, local copies, waits for them, and re-layouts  5.81 us
  transfers between devices with their start and end apart: 32, of which 18 were waited for; matrix products, arithmetic and copies ran while one was open for 0% of the time, Pallas kernels for 7%

profile of v2, /device:TPU:1, one launch (start us, length us, event | category | flops | bytes accessed | tf_op | source)
XLA Modules:
  0.0 122.3 jit_solution(6968421383668632999)
XLA Ops:
  6.0 5.7 %collective-permute-start = (f32[8,128]{1,0:T(8,128)S(1)}, f32[8,128]{1,0:T(8,128)S(1)}, u32[]{:S(2)}, u32[]{:S(2)}) collective-permute-start(f32[8,128]{1,0:T(8,128)S(1)} %get-tuple-element.34), channel_id=1, source_target_pairs={{0,2},{2,4},{4,6},{1,3},{3,5},{5,7},{8,10},{10,12},{12,14},{9,11},... | collective-permute-start | bytes 12296 | tf_op jit(solution)/shard_map/ppermute | solution.py:449
  13.1 5.8 %collective-permute-done.1.high.refs_11_ = f32[8,128]{1,0:T(8,128)S(1)} collective-permute-done((f32[8,128]{1,0:T(8,128)S(1)}, f32[8,128]{1,0:T(8,128)S(1)}, u32[]{:S(2)}, u32[]{:S(2)}) %collective-permute-start.1) | collective-permute-done | bytes 4128 | tf_op jit(solution)/shard_map/ppermute | solution.py:449
  25.5 2.7 %shard_map.120 = (f32[96,128]{1,0:T(8,128)S(1)}, f32[32,640]{1,0:T(8,128)S(1)}, f32[32,640]{1,0:T(8,128)S(1)}) custom-call(s32[3]{0:T(128)S(1)} %pad_add_fusion.core.place, f32[96,128]{1,0:T(8,128)S(1)} %get-tuple-element.32.x.refs_5_, f32[272,128]{1,0:T(8,128)S(1)} %collective-permute-done.2.west.refs_8_, ...), custom_call_target="tpu_custom_call" | custom-call | tf_op jit(solution)/shard_map/pallas_call | solution.py:40
  28.3 7.9 %collective-permute-start.8 = (f32[32,640]{1,0:T(8,128)S(1)}, f32[32,640]{1,0:T(8,128)S(1)}, u32[]{:S(2)}, u32[]{:S(2)}) collective-permute-start(f32[32,640]{1,0:T(8,128)S(1)} %get-tuple-element.49), channel_id=1, source_target_pairs={{0,1},{1,0},{2,3},{3,2},{4,5},{5,4},{6,7},{7,6},{8,9},{9,8},{10,11... | collective-permute-start | bytes 245768 | tf_op jit(solution)/shard_map/ppermute | solution.py:464
  37.8 4.8 %shard_map.121 = (f32[96,512]{1,0:T(8,128)S(1)}, f32[96,512]{1,0:T(8,128)S(1)}, f32[96,128]{1,0:T(8,128)S(1)}, f32[96,128]{1,0:T(8,128)S(1)}, f32[208,128]{1,0:T...) custom-call(s32[3]{0:T(128)S(1)} %pad_add_fusion.core.place, ...), custom_call_target="tpu_custom_call" | custom-call | tf_op jit(solution)/shard_map/pallas_call | solution.py:40
  42.6 5.5 %collective-permute-start.4 = (f32[8,128]{1,0:T(8,128)S(1)}, f32[8,128]{1,0:T(8,128)S(1)}, u32[]{:S(2)}, u32[]{:S(2)}) collective-permute-start(f32[8,128]{1,0:T(8,128)S(1)} %get-tuple-element.44), channel_id=1, source_target_pairs={{0,2},{2,4},{4,6},{1,3},{3,5},{5,7},{8,10},{10,12},{12,14},{9,11},... | collective-permute-start | bytes 12296 | tf_op jit(solution)/shard_map/ppermute | solution.py:449
  49.7 3.1 %collective-permute-start.10 = (f32[32,640]{1,0:T(8,128)S(1)}, f32[32,640]{1,0:T(8,128)S(1)}, u32[]{:S(2)}, u32[]{:S(2)}) collective-permute-start(f32[32,640]{1,0:T(8,128)S(1)} %add.67), channel_id=1, source_target_pairs={{0,16},{8,24},{16,0},{24,8},{32,48},{40,56},{48,32},{56,40},{64,80... | collective-permute-start | bytes 245768 | tf_op jit(solution)/shard_map/ppermute | solution.py:457
  52.8 3.4 %collective-permute-done.12 = f32[32,640]{1,0:T(8,128)S(1)} collective-permute-done((f32[32,640]{1,0:T(8,128)S(1)}, f32[32,640]{1,0:T(8,128)S(1)}, u32[]{:S(2)}, u32[]{:S(2)}) %collective-permute-start.12) | collective-permute-done | bytes 81952 | tf_op jit(solution)/shard_map/ppermute | solution.py:457
  56.5 3.1 %collective-permute-start.13 = (f32[32,640]{1,0:T(8,128)S(1)}, f32[32,640]{1,0:T(8,128)S(1)}, u32[]{:S(2)}, u32[]{:S(2)}) collective-permute-start(f32[32,640]{1,0:T(8,128)S(1)} %add_add_fusion.5), channel_id=1, source_target_pairs={{0,64},{8,72},{16,80},{24,88},{32,96},{40,104},{48,112},{56,120},{... | collective-permute-start | bytes 245768 | tf_op jit(solution)/shard_map/ppermute | solution.py:457
  59.6 2.1 %collective-permute-done.15 = f32[32,640]{1,0:T(8,128)S(1)} collective-permute-done((f32[32,640]{1,0:T(8,128)S(1)}, f32[32,640]{1,0:T(8,128)S(1)}, u32[]{:S(2)}, u32[]{:S(2)}) %collective-permute-start.15) | collective-permute-done | bytes 81952 | tf_op jit(solution)/shard_map/ppermute | solution.py:457
  63.3 4.7 %collective-permute-start.17 = (f32[32,640]{1,0:T(8,128)S(1)}, f32[32,640]{1,0:T(8,128)S(1)}, u32[]{:S(2)}, u32[]{:S(2)}) collective-permute-start(f32[32,640]{1,0:T(8,128)S(1)} %add_add_fusion.4), channel_id=1, source_target_pairs={{0,12},{2,14},{4,8},{6,10},{8,4},{10,6},{12,0},{14,2},{16,28},{18,... | collective-permute-start | bytes 245768 | tf_op jit(solution)/shard_map/ppermute | solution.py:457
  68.0 4.3 %collective-permute-start.7 = (f32[208,128]{1,0:T(8,128)S(1)}, f32[208,128]{1,0:T(8,128)S(1)}, u32[]{:S(2)}, u32[]{:S(2)}) collective-permute-start(f32[208,128]{1,0:T(8,128)S(1)} %get-tuple-element.64), channel_id=1, source_target_pairs={{0,249},{1,0},{8,1},{9,8},{16,9},{17,16},{24,17},{25,24},{32,25},{... | collective-permute-start | bytes 319496 | tf_op jit(solution)/shard_map/ppermute | solution.py:442
  72.7 2.5 %collective-permute-done.16 = f32[32,640]{1,0:T(8,128)S(1)} collective-permute-done((f32[32,640]{1,0:T(8,128)S(1)}, f32[32,640]{1,0:T(8,128)S(1)}, u32[]{:S(2)}, u32[]{:S(2)}) %collective-permute-start.16) | collective-permute-done | bytes 81952 | tf_op jit(solution)/shard_map/ppermute | solution.py:457
  75.1 3.5 %collective-permute-start.19 = (f32[32,640]{1,0:T(8,128)S(1)}, f32[32,640]{1,0:T(8,128)S(1)}, u32[]{:S(2)}, u32[]{:S(2)}) collective-permute-start(f32[32,640]{1,0:T(8,128)S(1)} %add_add_fusion.3.part), channel_id=1, source_target_pairs={{0,1},{1,0},{2,3},{3,2},{4,5},{5,4},{6,7},{7,6},{8,9},{9,8},{10,11... | collective-permute-start | bytes 245768 | tf_op jit(solution)/shard_map/ppermute | solution.py:471
  79.5 2.7 %shard_map.122 = (f32[64,640]{1,0:T(8,128)S(1)}, f32[96,128]{1,0:T(8,128)S(1)}, f32[32,640]{1,0:T(8,128)S(1)}, f32[32,640]{1,0:T(8,128)S(1)}) custom-call(s32[3]{0:T(128)S(1)} %pad_add_fusion.core.place, f32[96,128]{1,0:T(8,128)S(1)} %get-tuple-element.42.x.refs_5_, f32[208,128]{1,0:T(8,128)S(1)} %collective-permute-done.6.west.refs_12_, ...), custom_call_target="tpu_custom_call" | custom-call | tf_op jit(solution)/shard_map/pallas_call | solution.py:40
  85.4 3.7 %collective-permute-done.21 = f32[32,640]{1,0:T(8,128)S(1)} collective-permute-done((f32[32,640]{1,0:T(8,128)S(1)}, f32[32,640]{1,0:T(8,128)S(1)}, u32[]{:S(2)}, u32[]{:S(2)}) %collective-permute-start.21) | collective-permute-done | bytes 81952 | tf_op jit(solution)/shard_map/ppermute | solution.py:457
  90.1 2.2 %collective-permute-start.22 = (f32[32,640]{1,0:T(8,128)S(1)}, f32[32,640]{1,0:T(8,128)S(1)}, u32[]{:S(2)}, u32[]{:S(2)}) collective-permute-start(f32[32,640]{1,0:T(8,128)S(1)} %add.78), channel_id=1, source_target_pairs={{0,16},{8,24},{16,0},{24,8},{32,48},{40,56},{48,32},{56,40},{64,80... | collective-permute-start | bytes 245768 | tf_op jit(solution)/shard_map/ppermute | solution.py:457
  92.4 2.5 %collective-permute-done.24 = f32[32,640]{1,0:T(8,128)S(1)} collective-permute-done((f32[32,640]{1,0:T(8,128)S(1)}, f32[32,640]{1,0:T(8,128)S(1)}, u32[]{:S(2)}, u32[]{:S(2)}) %collective-permute-start.24) | collective-permute-done | bytes 81952 | tf_op jit(solution)/shard_map/ppermute | solution.py:457
  98.8 2.1 %collective-permute-done.27 = f32[32,640]{1,0:T(8,128)S(1)} collective-permute-done((f32[32,640]{1,0:T(8,128)S(1)}, f32[32,640]{1,0:T(8,128)S(1)}, u32[]{:S(2)}, u32[]{:S(2)}) %collective-permute-start.27) | collective-permute-done | bytes 81952 | tf_op jit(solution)/shard_map/ppermute | solution.py:457
  102.5 3.4 %collective-permute-start.29 = (f32[32,640]{1,0:T(8,128)S(1)}, f32[32,640]{1,0:T(8,128)S(1)}, u32[]{:S(2)}, u32[]{:S(2)}) collective-permute-start(f32[32,640]{1,0:T(8,128)S(1)} %add_add_fusion.1), channel_id=1, source_target_pairs={{0,12},{2,14},{4,8},{6,10},{8,4},{10,6},{12,0},{14,2},{16,28},{18,... | collective-permute-start | bytes 245768 | tf_op jit(solution)/shard_map/ppermute | solution.py:457
  107.1 2.3 %collective-permute-done.29 = f32[32,640]{1,0:T(8,128)S(1)} collective-permute-done((f32[32,640]{1,0:T(8,128)S(1)}, f32[32,640]{1,0:T(8,128)S(1)}, u32[]{:S(2)}, u32[]{:S(2)}) %collective-permute-start.29) | collective-permute-done | bytes 81952 | tf_op jit(solution)/shard_map/ppermute | solution.py:457
  109.3 2.5 %collective-permute-done.28 = f32[32,640]{1,0:T(8,128)S(1)} collective-permute-done((f32[32,640]{1,0:T(8,128)S(1)}, f32[32,640]{1,0:T(8,128)S(1)}, u32[]{:S(2)}, u32[]{:S(2)}) %collective-permute-start.28) | collective-permute-done | bytes 81952 | tf_op jit(solution)/shard_map/ppermute | solution.py:457
  111.8 5.1 %collective-permute-start.31 = (f32[32,640]{1,0:T(8,128)S(1)}, f32[32,640]{1,0:T(8,128)S(1)}, u32[]{:S(2)}, u32[]{:S(2)}) collective-permute-start(f32[32,640]{1,0:T(8,128)S(1)} %add_add_fusion.part), channel_id=1, source_target_pairs={{0,1},{1,0},{2,3},{3,2},{4,5},{5,4},{6,7},{7,6},{8,9},{9,8},{10,11... | collective-permute-start | bytes 245768 | tf_op jit(solution)/shard_map/ppermute | solution.py:471
  116.9 3.2 %shard_map.123 = (f32[96,512]{1,0:T(8,128)}, f32[96,512]{1,0:T(8,128)}) custom-call(s32[3]{0:T(128)S(1)} %pad_add_fusion.core.place, f32[96,512]{1,0:T(8,128)S(1)} %get-tuple-element.40.refs_0_, f32[96,512]{1,0:T(8,128)S(1)} %get-tuple-element.41.refs_1_, f32[96,512]{1,0:T(8,128)S(1)} %bitcast.14, f32[96,512]{1,0:T(8,128)S(1)} %bitcast.17, ...), custom_call_target="tpu_custom_call" | custom-call | tf_op jit(solution)/shard_map/pallas_call | solution.py:40
  (95 shorter events, 32.6 us)
Async XLA Ops:
  6.0 7.0 %collective-permute-start = (f32[8,128]{1,0:T(8,128)S(1)}, f32[8,128]{1,0:T(8,128)S(1)}, u32[]{:S(2)}, u32[]{:S(2)}) collective-permute-start(f32[8,128]{1,0:T(8,128)S(1)} %get-tuple-element.34), channel_id=1, source_target_pairs={{0,2},{2,4},{4,6},{1,3},{3,5},{5,7},{8,10},{10,12},{12,14},{9,11},... | collective-permute-start | bytes 12296 | tf_op jit(solution)/shard_map/ppermute | solution.py:449
  11.8 7.1 %collective-permute-start.1 = (f32[8,128]{1,0:T(8,128)S(1)}, f32[8,128]{1,0:T(8,128)S(1)}, u32[]{:S(2)}, u32[]{:S(2)}) collective-permute-start(f32[8,128]{1,0:T(8,128)S(1)} %get-tuple-element.35), channel_id=1, source_target_pairs={{2,0},{4,2},{6,4},{3,1},{5,3},{7,5},{10,8},{12,10},{14,12},{11,9},... | collective-permute-start | bytes 12296 | tf_op jit(solution)/shard_map/ppermute | solution.py:449
  28.3 8.9 %collective-permute-start.8 = (f32[32,640]{1,0:T(8,128)S(1)}, f32[32,640]{1,0:T(8,128)S(1)}, u32[]{:S(2)}, u32[]{:S(2)}) collective-permute-start(f32[32,640]{1,0:T(8,128)S(1)} %get-tuple-element.49), channel_id=1, source_target_pairs={{0,1},{1,0},{2,3},{3,2},{4,5},{5,4},{6,7},{7,6},{8,9},{9,8},{10,11... | collective-permute-start | bytes 245768 | tf_op jit(solution)/shard_map/ppermute | solution.py:464
  37.1 12.3 %collective-permute-start.9 = (f32[32,640]{1,0:T(8,128)S(1)}, f32[32,640]{1,0:T(8,128)S(1)}, u32[]{:S(2)}, u32[]{:S(2)}) collective-permute-start(f32[32,640]{1,0:T(8,128)S(1)} %add.66), channel_id=1, source_target_pairs={{0,8},{8,0},{16,24},{24,16},{32,40},{40,32},{48,56},{56,48},{64,72... | collective-permute-start | bytes 245768 | tf_op jit(solution)/shard_map/ppermute | solution.py:457
  42.6 10.2 %collective-permute-start.4 = (f32[8,128]{1,0:T(8,128)S(1)}, f32[8,128]{1,0:T(8,128)S(1)}, u32[]{:S(2)}, u32[]{:S(2)}) collective-permute-start(f32[8,128]{1,0:T(8,128)S(1)} %get-tuple-element.44), channel_id=1, source_target_pairs={{0,2},{2,4},{4,6},{1,3},{3,5},{5,7},{8,10},{10,12},{12,14},{9,11},... | collective-permute-start | bytes 12296 | tf_op jit(solution)/shard_map/ppermute | solution.py:449
  48.1 11.5 %collective-permute-start.5 = (f32[8,128]{1,0:T(8,128)S(1)}, f32[8,128]{1,0:T(8,128)S(1)}, u32[]{:S(2)}, u32[]{:S(2)}) collective-permute-start(f32[8,128]{1,0:T(8,128)S(1)} %get-tuple-element.45), channel_id=1, source_target_pairs={{2,0},{4,2},{6,4},{3,1},{5,3},{7,5},{10,8},{12,10},{14,12},{11,9},... | collective-permute-start | bytes 12296 | tf_op jit(solution)/shard_map/ppermute | solution.py:449
  49.5 6.8 %collective-permute-start.12 = (f32[32,640]{1,0:T(8,128)S(1)}, f32[32,640]{1,0:T(8,128)S(1)}, u32[]{:S(2)}, u32[]{:S(2)}) collective-permute-start(f32[32,640]{1,0:T(8,128)S(1)} %add.67), channel_id=1, source_target_pairs={{0,48},{8,56},{16,32},{24,40},{32,16},{40,24},{48,0},{56,8},{64,11... | collective-permute-start | bytes 245768 | tf_op jit(solution)/shard_map/ppermute | solution.py:457
  49.6 6.7 %collective-permute-start.11 = (f32[32,640]{1,0:T(8,128)S(1)}, f32[32,640]{1,0:T(8,128)S(1)}, u32[]{:S(2)}, u32[]{:S(2)}) collective-permute-start(f32[32,640]{1,0:T(8,128)S(1)} %add.67), channel_id=1, source_target_pairs={{0,32},{8,40},{16,48},{24,56},{32,0},{40,8},{48,16},{56,24},{64,96... | collective-permute-start | bytes 245768 | tf_op jit(solution)/shard_map/ppermute | solution.py:457
  49.7 6.6 %collective-permute-start.10 = (f32[32,640]{1,0:T(8,128)S(1)}, f32[32,640]{1,0:T(8,128)S(1)}, u32[]{:S(2)}, u32[]{:S(2)}) collective-permute-start(f32[32,640]{1,0:T(8,128)S(1)} %add.67), channel_id=1, source_target_pairs={{0,16},{8,24},{16,0},{24,8},{32,48},{40,56},{48,32},{56,40},{64,80... | collective-permute-start | bytes 245768 | tf_op jit(solution)/shard_map/ppermute | solution.py:457
  56.2 5.5 %collective-permute-start.15 = (f32[32,640]{1,0:T(8,128)S(1)}, f32[32,640]{1,0:T(8,128)S(1)}, u32[]{:S(2)}, u32[]{:S(2)}) collective-permute-start(f32[32,640]{1,0:T(8,128)S(1)} %add_add_fusion.5), channel_id=1, source_target_pairs={{0,192},{8,200},{16,208},{24,216},{32,224},{40,232},{48,240},{56,2... | collective-permute-start | bytes 245768 | tf_op jit(solution)/shard_map/ppermute | solution.py:457
  56.3 5.4 %collective-permute-start.14 = (f32[32,640]{1,0:T(8,128)S(1)}, f32[32,640]{1,0:T(8,128)S(1)}, u32[]{:S(2)}, u32[]{:S(2)}) collective-permute-start(f32[32,640]{1,0:T(8,128)S(1)} %add_add_fusion.5), channel_id=1, source_target_pairs={{0,128},{8,136},{16,144},{24,152},{32,160},{40,168},{48,176},{56,1... | collective-permute-start | bytes 245768 | tf_op jit(solution)/shard_map/ppermute | solution.py:457
  56.5 6.1 %collective-permute-start.13 = (f32[32,640]{1,0:T(8,128)S(1)}, f32[32,640]{1,0:T(8,128)S(1)}, u32[]{:S(2)}, u32[]{:S(2)}) collective-permute-start(f32[32,640]{1,0:T(8,128)S(1)} %add_add_fusion.5), channel_id=1, source_target_pairs={{0,64},{8,72},{16,80},{24,88},{32,96},{40,104},{48,112},{56,120},{... | collective-permute-start | bytes 245768 | tf_op jit(solution)/shard_map/ppermute | solution.py:457
  62.6 10.0 %collective-permute-start.18 = (f32[32,640]{1,0:T(8,128)S(1)}, f32[32,640]{1,0:T(8,128)S(1)}, u32[]{:S(2)}, u32[]{:S(2)}) collective-permute-start(f32[32,640]{1,0:T(8,128)S(1)} %add_add_fusion.4), channel_id=1, source_target_pairs={{0,6},{2,4},{4,2},{6,0},{8,14},{10,12},{12,10},{14,8},{16,22},{18,... | collective-permute-start | bytes 245768 | tf_op jit(solution)/shard_map/ppermute | solution.py:457
  63.3 9.4 %collective-permute-start.17 = (f32[32,640]{1,0:T(8,128)S(1)}, f32[32,640]{1,0:T(8,128)S(1)}, u32[]{:S(2)}, u32[]{:S(2)}) collective-permute-start(f32[32,640]{1,0:T(8,128)S(1)} %add_add_fusion.4), channel_id=1, source_target_pairs={{0,12},{2,14},{4,8},{6,10},{8,4},{10,6},{12,0},{14,2},{16,28},{18,... | collective-permute-start | bytes 245768 | tf_op jit(solution)/shard_map/ppermute | solution.py:457
  68.0 7.2 %collective-permute-start.16 = (f32[32,640]{1,0:T(8,128)S(1)}, f32[32,640]{1,0:T(8,128)S(1)}, u32[]{:S(2)}, u32[]{:S(2)}) collective-permute-start(f32[32,640]{1,0:T(8,128)S(1)} %add_add_fusion.4), channel_id=1, source_target_pairs={{0,2},{2,0},{4,6},{6,4},{8,10},{10,8},{12,14},{14,12},{16,18},{18,... | collective-permute-start | bytes 245768 | tf_op jit(solution)/shard_map/ppermute | solution.py:457
  68.0 10.6 %collective-permute-start.7 = (f32[208,128]{1,0:T(8,128)S(1)}, f32[208,128]{1,0:T(8,128)S(1)}, u32[]{:S(2)}, u32[]{:S(2)}) collective-permute-start(f32[208,128]{1,0:T(8,128)S(1)} %get-tuple-element.64), channel_id=1, source_target_pairs={{0,249},{1,0},{8,1},{9,8},{16,9},{17,16},{24,17},{25,24},{32,25},{... | collective-permute-start | bytes 319496 | tf_op jit(solution)/shard_map/ppermute | solution.py:442
  72.3 6.3 %collective-permute-start.6 = (f32[208,128]{1,0:T(8,128)S(1)}, f32[208,128]{1,0:T(8,128)S(1)}, u32[]{:S(2)}, u32[]{:S(2)}) collective-permute-start(f32[208,128]{1,0:T(8,128)S(1)} %get-tuple-element.65), channel_id=1, source_target_pairs={{0,1},{1,8},{8,9},{9,16},{16,17},{17,24},{24,25},{25,32},{32,33},{... | collective-permute-start | bytes 319496 | tf_op jit(solution)/shard_map/ppermute | solution.py:442
  89.0 5.8 %collective-permute-start.24 = (f32[32,640]{1,0:T(8,128)S(1)}, f32[32,640]{1,0:T(8,128)S(1)}, u32[]{:S(2)}, u32[]{:S(2)}) collective-permute-start(f32[32,640]{1,0:T(8,128)S(1)} %add.78), channel_id=1, source_target_pairs={{0,48},{8,56},{16,32},{24,40},{32,16},{40,24},{48,0},{56,8},{64,11... | collective-permute-start | bytes 245768 | tf_op jit(solution)/shard_map/ppermute | solution.py:457
  89.2 5.7 %collective-permute-start.23 = (f32[32,640]{1,0:T(8,128)S(1)}, f32[32,640]{1,0:T(8,128)S(1)}, u32[]{:S(2)}, u32[]{:S(2)}) collective-permute-start(f32[32,640]{1,0:T(8,128)S(1)} %add.78), channel_id=1, source_target_pairs={{0,32},{8,40},{16,48},{24,56},{32,0},{40,8},{48,16},{56,24},{64,96... | collective-permute-start | bytes 245768 | tf_op jit(solution)/shard_map/ppermute | solution.py:457
  95.4 5.5 %collective-permute-start.27 = (f32[32,640]{1,0:T(8,128)S(1)}, f32[32,640]{1,0:T(8,128)S(1)}, u32[]{:S(2)}, u32[]{:S(2)}) collective-permute-start(f32[32,640]{1,0:T(8,128)S(1)} %add_add_fusion.2), channel_id=1, source_target_pairs={{0,192},{8,200},{16,208},{24,216},{32,224},{40,232},{48,240},{56,2... | collective-permute-start | bytes 245768 | tf_op jit(solution)/shard_map/ppermute | solution.py:457
  101.5 5.6 %collective-permute-start.30 = (f32[32,640]{1,0:T(8,128)S(1)}, f32[32,640]{1,0:T(8,128)S(1)}, u32[]{:S(2)}, u32[]{:S(2)}) collective-permute-start(f32[32,640]{1,0:T(8,128)S(1)} %add_add_fusion.1), channel_id=1, source_target_pairs={{0,6},{2,4},{4,2},{6,0},{8,14},{10,12},{12,10},{14,8},{16,22},{18,... | collective-permute-start | bytes 245768 | tf_op jit(solution)/shard_map/ppermute | solution.py:457
  102.5 6.9 %collective-permute-start.29 = (f32[32,640]{1,0:T(8,128)S(1)}, f32[32,640]{1,0:T(8,128)S(1)}, u32[]{:S(2)}, u32[]{:S(2)}) collective-permute-start(f32[32,640]{1,0:T(8,128)S(1)} %add_add_fusion.1), channel_id=1, source_target_pairs={{0,12},{2,14},{4,8},{6,10},{8,4},{10,6},{12,0},{14,2},{16,28},{18,... | collective-permute-start | bytes 245768 | tf_op jit(solution)/shard_map/ppermute | solution.py:457
  105.9 5.9 %collective-permute-start.28 = (f32[32,640]{1,0:T(8,128)S(1)}, f32[32,640]{1,0:T(8,128)S(1)}, u32[]{:S(2)}, u32[]{:S(2)}) collective-permute-start(f32[32,640]{1,0:T(8,128)S(1)} %add_add_fusion.1), channel_id=1, source_target_pairs={{0,2},{2,0},{4,6},{6,4},{8,10},{10,8},{12,14},{14,12},{16,18},{18,... | collective-permute-start | bytes 245768 | tf_op jit(solution)/shard_map/ppermute | solution.py:457
  111.8 8.2 %collective-permute-start.31 = (f32[32,640]{1,0:T(8,128)S(1)}, f32[32,640]{1,0:T(8,128)S(1)}, u32[]{:S(2)}, u32[]{:S(2)}) collective-permute-start(f32[32,640]{1,0:T(8,128)S(1)} %add_add_fusion.part), channel_id=1, source_target_pairs={{0,1},{1,0},{2,3},{3,2},{4,5},{5,4},{6,7},{7,6},{8,9},{9,8},{10,11... | collective-permute-start | bytes 245768 | tf_op jit(solution)/shard_map/ppermute | solution.py:471
  (21 other events, 105.1 us)

commit v3 on v2

--- a/solution.py
+++ b/solution.py
@@ -10,7 +10,6 @@
 time_step = 0.2
 diffusivity = 0.5
 learn_rate = 200.0
-highest = lax.Precision.HIGHEST
 f32 = jnp.float32
 bf16 = jnp.bfloat16
 
@@ -34,8 +33,13 @@
 
 
 def call(kernel, outs, *args, scratch=(), smem=0, remote=0, flops=0, bytes_accessed=0):
+    first, last = smem, smem + remote
+    args = [
+        pltpu.with_memory_space_constraint(arg, pltpu.HBM) if first <= at < last else arg
+        for at, arg in enumerate(args)
+    ]
     specs = [pl.BlockSpec(memory_space=pltpu.SMEM)] * smem
-    specs += [pl.BlockSpec(memory_space=pl.ANY)] * remote
+    specs += [pl.BlockSpec(memory_space=pltpu.HBM)] * remote
     specs += [pl.BlockSpec(memory_space=pltpu.VMEM)] * (len(args) - smem - remote)
     return pl.pallas_call(
         kernel,
@@ -121,33 +125,62 @@
         target_ref[CHANNELS * row : CHANNELS * (row + 1), :] = products - own
 
 
-def fill_edges(blocks, fields, column_fields, mask_ref, x_ref, first_ref, last_ref, low_ref, high_ref):
-    depth = (first_ref.shape[0] - EDGE_AT) // 4
-    for lon, out in ((0, first_ref), (7, last_ref)):
+class Either:
+    def __init__(self, flag, one, other):
+        self.flag, self.one, self.other, self.shape = flag, one, other, one.shape
+
+    def __getitem__(self, at):
+        return jnp.where(self.flag, self.one[at], self.other[at])
+
+
+def sides(place, inner, outer):
+    first = place[0] == 0
+    return Either(first, outer, inner), Either(first, inner, outer)
+
+
+def fill_edges(place, blocks, fields, column_fields, mask_ref, x_ref, inner_ref, outer_ref, near_ref, far_ref):
+    core_first = place[0] == 0
+    depth = (inner_ref.shape[0] - EDGE_AT) // 4
+    for out in (inner_ref, outer_ref):
         out[0:COLUMNS_AT, :] = x_ref[...]
         out[COLUMNS_AT:, :] = jnp.zeros((out.shape[0] - COLUMNS_AT, COARSE), f32)
-        for block in range(4):
-            start = EDGE_AT + block * depth
-            for which in range(fields):
-                at = start + which * LEVELS
-                out[at : at + LEVELS, :] = longitude_row(blocks, which, block, lon)
-            if mask_ref is not None:
-                at = start + fields * LEVELS
-                out[at : at + 1, :] = mask_ref[lon : lon + 1, 128 * block : 128 * (block + 1)]
-    turned = x_ref[...].T
-    for out, block, column, inner in ((low_ref, 0, 0, 1), (high_ref, 3, 127, 126)):
-        out[...] = jnp.zeros(out.shape, f32)
-        for at, which in enumerate(column_fields):
-            out[at : at + 1, 0 : 8 * LEVELS] = blocks[block_rows(which, block), :].T[column : column + 1]
+
+    def put(rows, first, last):
+        inner_ref[rows, :] = jnp.where(core_first, last, first)
+        outer_ref[rows, :] = jnp.where(core_first, first, last)
+
+    for block in range(4):
+        start = EDGE_AT + block * depth
+        for which in range(fields):
+            at = start + which * LEVELS
+            put(
+                slice(at, at + LEVELS),
+                longitude_row(blocks, which, block, 0),
+                longitude_row(blocks, which, block, 7),
+            )
         if mask_ref is not None:
-            here = mask_ref[:, 128 * block : 128 * (block + 1)]
-            out[3:4, 0:8] = here.T[column : column + 1]
-        out[4:5, 0 : 2 * CHANNELS] = turned[column : column + 1]
-        out[5:6, 0 : 2 * CHANNELS] = turned[inner : inner + 1]
+            at = start + fields * LEVELS
+            lanes = slice(128 * block, 128 * (block + 1))
+            put(slice(at, at + 1), mask_ref[0:1, lanes], mask_ref[7:8, lanes])
+    odd = place[3] == 1
+    near_ref[...] = jnp.zeros(near_ref.shape, f32)
+    far_ref[...] = jnp.zeros(far_ref.shape, f32)
+
+    def put_columns(at, low, high, low_column, high_column):
+        low, high = low.T[low_column : low_column + 1], high.T[high_column : high_column + 1]
+        near_ref[at : at + 1, 0 : low.shape[1]] = jnp.where(odd, low, high)
+        far_ref[at : at + 1, 0 : low.shape[1]] = jnp.where(odd, high, low)
+
+    for at, which in enumerate(column_fields):
+        put_columns(at, blocks[block_rows(which, 0), :], blocks[block_rows(which, 3), :], 0, 127)
+    if mask_ref is not None:
+        put_columns(3, mask_ref[:, 0:128], mask_ref[:, FINE - 128 : FINE], 0, 127)
+    put_columns(4, x_ref[...], x_ref[...], 0, COARSE - 1)
+    put_columns(5, x_ref[...], x_ref[...], 1, COARSE - 2)
 
 
 def prepare_kernel(
-    t, s, u, v, mask, x, target, weight, first, last, low, high, sums, blocks, mask_here, mask_values, semaphore
+    place, t, s, u, v, mask, x, target, weight, mask_values, inner, outer, near, far, sums, blocks, mask_here, semaphore
 ):
     pairs = [(mask, mask_here)]
     for which, ref in enumerate((t, s, u, v)):
@@ -159,7 +192,7 @@
     m = mask_here[...].astype(f32)
     mask_values[...] = m
     coarsen(blocks, sums, x, target)
-    fill_edges(blocks, 3, (0, 1, 3), mask_values, x, first, last, low, high)
+    fill_edges(place, blocks, 3, (0, 1, 3), mask_values, x, inner, outer, near, far)
     rows = jnp.concatenate(
         [jnp.sum(m[0:4], axis=0, keepdims=True), jnp.sum(m[4:8], axis=0, keepdims=True)]
         + [jnp.zeros((6, FINE), f32)],
@@ -168,14 +201,18 @@
     weight[...] = jnp.dot(rows.astype(bf16), pooling_matrix(), preferred_element_type=f32)
 
 
-def dot(a, b):
-    return jnp.dot(a, b, precision=highest, preferred_element_type=f32)
-
-
-def dot_nt(a, b):
-    return lax.dot_general(
-        a, b, (((1,), (1,)), ((), ())), precision=highest, preferred_element_type=f32
-    )
+def parts_of(value):
+    high = value.astype(bf16)
+    return high, (value - high.astype(f32)).astype(bf16)
+
+
+def dot_parts(a, b, contract):
+    (a_high, a_low), (b_high, b_low) = a, b
+    dims = (((1,), (contract,)), ((), ()))
+    dot = functools.partial(lax.dot_general, dimension_numbers=dims, preferred_element_type=f32)
+    rows = a_high.shape[0]
+    both = dot(jnp.concatenate([a_high, a_low], 0), b_high)
+    return both[:rows] + (both[rows:] + dot(a_high, b_low))
 
 
 def column_matrix(low, high, west, east):
@@ -215,15 +252,19 @@
         if not any(abs(at - centre) <= 1 for centre in centres):
             continue
         channels = slice(start, start + CHANNELS)
-        shifted = shifted_rows(
-            value, columns[channels, pair : pair + 1], columns[channels, pair + 1 : pair + 2]
-        )
+        shifted = [
+            parts_of(part)
+            for part in shifted_rows(
+                value, columns[channels, pair : pair + 1], columns[channels, pair + 1 : pair + 2]
+            )
+        ]
         for place, centre in enumerate(centres):
             tap = at - centre + 1
             if 0 <= tap < 3:
                 for side in range(3):
                     begin = (3 * tap + side) * CHANNELS
-                    taps[begin : begin + CHANNELS, COARSE * place : COARSE * (place + 1)] = shifted[side]
+                    for out, part in zip(taps, shifted[side]):
+                        out[begin : begin + CHANNELS, COARSE * place : COARSE * (place + 1)] = part
 
 
 def fill_side_taps(taps, rows, columns, start_lane):
@@ -247,72 +288,83 @@
                 out = jnp.where(lanes == row, low, out)
                 out = jnp.where(lanes == 2 + row, high, out)
             begin = (3 * tap + side) * CHANNELS
-            taps[begin : begin + CHANNELS, start_lane : start_lane + COARSE] = out
+            for ref, part in zip(taps, parts_of(out)):
+                ref[begin : begin + CHANNELS, start_lane : start_lane + COARSE] = part
 
 
 def network_step(
-    core, x, west, east, low, high, target, weight, packed, pred, own, other, taps, grads
+    place, x, inner, outer, low, high, target, weight, packed, pred, own, other, taps_high, taps_low, grads
 ):
+    west, east = sides(place, inner, outer)
     columns = column_matrix(low, high, west, east)
-    fill_taps(taps, coarse_rows(x, west, east), columns, (2, 3))
-    kernel = packed[:, 0:TAPS]
+    fill_taps((taps_high, taps_low), coarse_rows(x, west, east), columns, (2, 3))
+    taps = taps_high[...], taps_low[...]
+    kernel = parts_of(packed[:, 0:TAPS])
     mix = packed[:, MIX_AT : MIX_AT + HIDDEN]
     out_turned = packed[:, OUT_AT : OUT_AT + CHANNELS]
-    hidden_one = jnp.tanh(dot(kernel, taps[...]))
-    hidden_two = jnp.tanh(dot(mix, hidden_one))
-    predicted = dot(out_turned.T, hidden_two)
+    hidden_one = jnp.tanh(dot_parts(kernel, taps, 0))
+    one = parts_of(hidden_one)
+    hidden_two = jnp.tanh(dot_parts(parts_of(mix), one, 0))
+    two = parts_of(hidden_two)
+    predicted = dot_parts(parts_of(out_turned.T), two, 0)
     pred[0:CHANNELS, :] = predicted[:, 0:COARSE]
     pred[CHANNELS : 2 * CHANNELS, :] = predicted[:, COARSE : 2 * COARSE]
-    back_out = jnp.concatenate(
-        [
-            weight[row : row + 1, :]
-            * (
-                predicted[:, COARSE * row : COARSE * (row + 1)]
-                - target[CHANNELS * row : CHANNELS * (row + 1), :]
-            )
-            for row in range(2)
-        ],
-        1,
-    )
-    back_two = dot(out_turned, back_out) * (1.0 - hidden_two * hidden_two)
-    back_one = dot(mix.T, back_two) * (1.0 - hidden_one * hidden_one)
+    back_out = parts_of(
+        jnp.concatenate(
+            [
+                weight[row : row + 1, :]
+                * (
+                    predicted[:, COARSE * row : COARSE * (row + 1)]
+                    - target[CHANNELS * row : CHANNELS * (row + 1), :]
+                )
+                for row in range(2)
+            ],
+            1,
+        )
+    )
+    back_two = parts_of(
+        dot_parts(parts_of(out_turned), back_out, 0) * (1.0 - hidden_two * hidden_two)
+    )
+    back_one = parts_of(
+        dot_parts(parts_of(mix.T), back_two, 0) * (1.0 - hidden_one * hidden_one)
+    )
     grads[:, MIX_AT - 128 : PACKED] = jnp.zeros((HIDDEN, PACKED - MIX_AT + 128), f32)
-    grads[:, 0:TAPS] = dot_nt(back_one, taps[...])
-    grads[:, MIX_AT : MIX_AT + HIDDEN] = dot_nt(back_two, hidden_one)
-    grads[:, OUT_AT : OUT_AT + CHANNELS] = dot_nt(hidden_two, back_out)
+    grads[:, 0:TAPS] = dot_parts(back_one, taps, 1)
+    grads[:, MIX_AT : MIX_AT + HIDDEN] = dot_parts(back_two, one, 1)
+    grads[:, OUT_AT : OUT_AT + CHANNELS] = dot_parts(two, back_out, 1)
     area = jnp.sum(weight[0:2, :], axis=(0, 1), keepdims=True)
     grads[:, AREA_AT : AREA_AT + 1] = jnp.broadcast_to(area, (HIDDEN, 1))
     half = HIDDEN // 2
-    own[...] = grads[pl.ds(pl.multiple_of(core[0] * half, half), half), :]
-    other[...] = grads[pl.ds(pl.multiple_of((1 - core[0]) * half, half), half), :]
-
-
-def descended(core, packed, part, back):
+    for core, out in ((place[0], own), (1 - place[0], other)):
+        rows = pl.ds(pl.multiple_of(core * half, half), half)
+        for block in range(PACKED // 128):
+            out[half * block : half * (block + 1), :] = grads[rows, 128 * block : 128 * (block + 1)]
+
+
+def descended(place, packed, part, back):
     half = HIDDEN // 2
-    mine, theirs = part[...], back[...]
-    first = core[0] == 0
-    total = jnp.concatenate(
-        [jnp.where(first, mine, theirs), jnp.where(first, theirs, mine)], 0
-    )
-    area = total[0:1, AREA_AT : AREA_AT + 1]
+    first = place[0] == 0
+    blocks = []
+    for block in range(PACKED // 128):
+        mine, theirs = (ref[half * block : half * (block + 1), :] for ref in (part, back))
+        blocks.append(
+            jnp.concatenate([jnp.where(first, mine, theirs), jnp.where(first, theirs, mine)], 0)
+        )
+    area = blocks[AREA_AT // 128][0:1, AREA_AT % 128 : AREA_AT % 128 + 1]
     step = (learn_rate * 2.0 / CHANNELS) / area
-    return packed[...] - step * total
-
-
-def first_network_kernel(core, x, west, east, low, high, target, weight, packed, *rest):
-    network_step(core, x, west, east, low, high, target, weight, packed, *rest)
+    return packed[...] - step * jnp.concatenate(blocks, 1)
 
 
 def next_network_kernel(
-    core, x, west, east, low, high, target, weight, packed, part, back, renewed, *rest
+    place, x, inner, outer, low, high, target, weight, packed, part, back, renewed, *rest
 ):
-    renewed[...] = descended(core, packed, part, back)
-    network_step(core, x, west, east, low, high, target, weight, renewed, *rest)
-
-
-def last_kernel(core, packed, part, back, kernel, mix, out):
-    renewed = descended(core, packed, part, back)
-    kernel[...] = renewed[:, 0:TAPS]
+    renewed[...] = descended(place, packed, part, back)
+    network_step(place, x, inner, outer, low, high, target, weight, renewed, *rest)
+
+
+def last_kernel(place, packed, part, back, kernel, mix, out):
+    renewed = descended(place, packed, part, back)
+    kernel[...] = renewed[:, 0:TAPS].T
     mix[...] = renewed[:, MIX_AT : MIX_AT + HIDDEN]
     out[...] = renewed[:, OUT_AT : OUT_AT + CHANNELS].T
 
@@ -322,9 +374,14 @@
     columns = column_matrix(low, high, west, east)
     fill_taps(taps, rows, columns, (1, 4))
     fill_side_taps(taps, rows, columns, 2 * COARSE)
-    hidden = jnp.tanh(dot(packed[:, 0:TAPS], taps[...]))
-    hidden = jnp.tanh(dot(packed[:, MIX_AT : MIX_AT + HIDDEN], hidden))
-    beside = dot(packed[:, OUT_AT : OUT_AT + CHANNELS].T, hidden)
+    inputs = tuple(ref[...] for ref in taps)
+    hidden = jnp.tanh(dot_parts(parts_of(packed[:, 0:TAPS]), inputs, 0))
+    hidden = jnp.tanh(
+        dot_parts(parts_of(packed[:, MIX_AT : MIX_AT + HIDDEN]), parts_of(hidden), 0)
+    )
+    beside = dot_parts(
+        parts_of(packed[:, OUT_AT : OUT_AT + CHANNELS].T), parts_of(hidden), 0
+    )
     sides = beside[:, 2 * COARSE :]
     sides_low = jnp.where(place[1] == 0, 0.0, sides)
     sides_high = jnp.where(place[2] == 0, 0.0, sides)
@@ -345,7 +402,7 @@
 def advance(t, s, u, v, mask, force, fixed, moving, t_out, s_out):
     fixed_west, fixed_east, fixed_low, fixed_high = fixed
     west, east, low, high = moving
-    m = mask[...].astype(f32)
+    m = mask[...]
     shape = (8, FINE)
     lanes = lane_index(shape)
     subs = lax.broadcasted_iota(jnp.int32, shape, 0)
@@ -408,67 +465,85 @@
 
 
 def first_advance_kernel(place, *refs):
-    t, s, u, v, mask, x, pred, packed, west, east, low, high = refs[:12]
-    t_out, s_out, x_out, target, first, last, low_out, high_out = refs[12:20]
-    sums, blocks, taps, t_here, s_here, u_here, v_here, semaphore = refs[20:]
+    t, s, u, v, mask, x, pred, packed, inner, outer, low, high = refs[:12]
+    t_out, s_out, x_out, target, inner_out, outer_out, near, far = refs[12:20]
+    sums, blocks, *taps = refs[20:24]
+    t_here, s_here, u_here, v_here, semaphore = refs[24:]
     here = (t_here, s_here, u_here, v_here)
     copies = fetch(list(zip((t, s, u, v), here)), semaphore)
-    halo = (west, east, low, high)
+    halo = (*sides(place, inner, outer), low, high)
     force = forcing(place, x, pred, packed, *halo, taps)
     for copy in copies:
         copy.wait()
     advance(*here, mask, force, halo, halo, t_out, s_out)
     fill_blocks(blocks, (t_out, s_out, u_here, v_here))
     coarsen(blocks, sums, x_out, target)
-    fill_edges(blocks, 2, (0, 1), None, x_out, first, last, low_out, high_out)
+    fill_edges(place, blocks, 2, (0, 1), None, x_out, inner_out, outer_out, near, far)
 
 
 def next_advance_kernel(place, *refs):
     t, s, u, v, mask, x, pred, packed = refs[:8]
-    fixed, moving, (t_out, s_out, taps) = refs[8:12], refs[12:16], refs[16:]
+    fixed, moving, (t_out, s_out, *taps) = refs[8:12], refs[12:16], refs[16:]
+    fixed = (*sides(place, *fixed[:2]), *fixed[2:])
+    moving = (*sides(place, *moving[:2]), *moving[2:])
     force = forcing(place, x, pred, packed, *moving, taps)
     advance(t, s, u, v, mask, force, fixed, moving, t_out, s_out)
 
 
-def ring(axis, step):
-    count = 1
-    for name in axis:
-        count *= lax.axis_size(name)
-    return [(i, (i + step) % count) for i in range(count)]
-
-
-def exchange_lon(first, last):
+def swap_lon(inner, outer):
     axis = ("lon", "grp")
-    return lax.ppermute(last, axis, ring(axis, 1)), lax.ppermute(first, axis, ring(axis, -1))
-
-
-def exchange_lat(low, high):
-    count = lax.axis_size("lat")
-    up = [(i, i + 1) for i in range(count - 1)]
-    down = [(i + 1, i) for i in range(count - 1)]
-    return lax.ppermute(high, "lat", up), lax.ppermute(low, "lat", down)
+    count = lax.axis_size("lon") * lax.axis_size("grp")
+    chips = [(i, (i + (1 if i % 2 else -1)) % count) for i in range(count)]
+    outer = lax.ppermute(outer, axis, chips)
+    return lax.ppermute(inner, "grp", flipped("grp", 1)), outer
+
+
+def swap_lat(near, far):
+    last = lax.axis_size("lat") - 1
+    beyond = [(i, i ^ 3) for i in range(1, last)]
+    return lax.ppermute(near, "lat", flipped("lat", 1)), lax.ppermute(far, "lat", beyond)
+
+
+def south_north(near, far):
+    lat = lax.axis_index("lat")
+    odd = lat % 2 == 1
+    south, north = jnp.where(odd, near, far), jnp.where(odd, far, near)
+    south = jnp.where(lat == 0, 0.0, south)
+    return south, jnp.where(lat == lax.axis_size("lat") - 1, 0.0, north)
+
+
+def halo(inner, outer, near, far):
+    south, north = south_north(near, far)
+    columns = jnp.concatenate([south, north], 0)
+    inner = lax.dynamic_update_slice_in_dim(inner, columns, COLUMNS_AT, 0)
+    outer = lax.dynamic_update_slice_in_dim(outer, columns, COLUMNS_AT, 0)
+    return *swap_lon(inner, outer), south, north
 
 
 def flipped(axis, mask):
     return [(i, i ^ mask) for i in range(lax.axis_size(axis))]
 
 
-def exchanged_sum(value, axis, masks):
-    parts = [lax.ppermute(value, axis, flipped(axis, mask)) for mask in masks]
-    if len(parts) == 1:
-        return value + parts[0]
-    return (value + parts[0]) + (parts[1] + parts[2])
-
-
-def sum_over_devices(own, other):
+def from_chip(value, mask):
+    count = lax.axis_size("lon") * lax.axis_size("lat")
+    return lax.ppermute(value, ("lon", "lat"), [(i, i ^ mask) for i in range(count)])
+
+
+def sum_over_devices(own, other, beside):
+    rows = own.shape[0]
     part = own + lax.ppermute(other, "grp", flipped("grp", 1))
-    part = exchanged_sum(part, "lon", (1,))
-    low = 2
-    while low < lax.axis_size("lon"):
-        part = exchanged_sum(part, "lon", (low, 2 * low, 3 * low))
-        low *= 4
-    part = exchanged_sum(part, ("lon", "lat"), (1, 6, 3))
-    return part, lax.ppermute(part, "grp", flipped("grp", 1))
+    part = part + from_chip(part, 4)
+    part, riders, extra = beside(part)
+    near = from_chip(jnp.concatenate([part, *riders[:1]], 0), 1)
+    cross = from_chip(part, 6)
+    far = from_chip(jnp.concatenate([part, *riders[1:]], 0), 3)
+    part = (part + near[:rows]) + (cross + far[:rows])
+    extra = extra(near[rows:], far[rows:])
+    if lax.axis_size("lon") > 2:
+        for bit in (8, 32):
+            one, two, three = (from_chip(part, bit * step) for step in (1, 2, 3))
+            part = (part + one) + (two + three)
+    return part, lax.ppermute(part, "grp", flipped("grp", 1)), extra
 
 
 def shards(
@@ -499,57 +574,55 @@
     lat = lax.axis_index("lat")
     lat_last = lax.axis_size("lat") - 1
     place = jnp.stack(
-        [lax.axis_index("grp"), (lat != 0).astype(jnp.int32), (lat != lat_last).astype(jnp.int32)]
+        [lax.axis_index("grp"), (lat != 0).astype(jnp.int32), (lat != lat_last).astype(jnp.int32), lat % 2]
     ).astype(jnp.int32)
     field_scratch = pltpu.VMEM((8 * LEVELS, FINE), f32)
     sums = [pltpu.VMEM((4 * CHANNELS, FINE), f32), pltpu.VMEM((16 * 8 * LEVELS, 128), f32)]
     wide = struct(2 * CHANNELS, COARSE)
     tile = struct(8, 128)
-    half = struct(HIDDEN // 2, PACKED)
+    half = struct(HIDDEN // 2 * PACKED // 128, 128)
     field = struct(8 * LEVELS, FINE)
     network_outs = [wide, half, half]
-    network_scratch = [pltpu.VMEM((TAPS, 2 * COARSE), f32), pltpu.VMEM((HIDDEN, PACKED), f32)]
-    side_taps = pltpu.VMEM((TAPS, 3 * COARSE), f32)
-
-    def halo(first, last, low, high):
-        south, north = exchange_lat(low, high)
-        columns = jnp.concatenate([south, north], 0)
-        first = lax.dynamic_update_slice_in_dim(first, columns, COLUMNS_AT, 0)
-        last = lax.dynamic_update_slice_in_dim(last, columns, COLUMNS_AT, 0)
-        return *exchange_lon(first, last), south, north
+    network_scratch = [pltpu.VMEM((TAPS, 2 * COARSE), bf16)] * 2 + [pltpu.VMEM((HIDDEN, PACKED), f32)]
+    side_taps = [pltpu.VMEM((TAPS, 3 * COARSE), bf16)] * 2
 
     edge = struct(EDGE_AT + 160, 128)
-    x, target, weight, *edges = call(
+    x, target, weight, mask, *edges = call(
         prepare_kernel,
-        [wide, wide, tile, edge, edge, tile, tile],
-        *fields, water_indicator,
+        [wide, wide, tile, struct(8, FINE), edge, edge, tile, tile],
+        place, *fields, water_indicator,
         scratch=sums
         + [
             pltpu.VMEM((8, FINE), jnp.int32),
-            pltpu.VMEM((8, FINE), f32),
             pltpu.SemaphoreType.DMA((17,)),
         ],
+        smem=1,
         remote=5,
     )
-    fixed = halo(*edges)
+    fixed = halo(*edges[:2], *swap_lat(*edges[2:]))
     pred, own, other = call(
-        first_network_kernel,
+        network_step,
         network_outs,
         place, x, *fixed, target, weight, packed,
         scratch=network_scratch,
         smem=1,
     )
-    part, back = sum_over_devices(own, other)
     edge = struct(EDGE_AT + 96, 128)
-    t, s, x, target, *edges = call(
-        first_advance_kernel,
-        [field, field, wide, wide, edge, edge, tile, tile],
-        place, *fields, water_indicator, x, pred, packed, *fixed,
-        scratch=sums + [side_taps] + [field_scratch] * 4 + [pltpu.SemaphoreType.DMA((4,))],
-        smem=1,
-        remote=4,
-    )
-    moving = halo(*edges)
+
+    def first_advance(part):
+        t, s, x_next, target_next, *edges = call(
+            first_advance_kernel,
+            [field, field, wide, wide, edge, edge, tile, tile],
+            place, *fields, mask, x, pred, packed, *fixed,
+            scratch=sums + side_taps + [field_scratch] * 4 + [pltpu.SemaphoreType.DMA((4,))],
+            smem=1,
+            remote=4,
+        )
+        inner, outer, *riders = edges
+        state = t, s, x_next, target_next
+        return part, riders, lambda near, far: (*state, halo(inner, outer, near, far))
+
+    part, back, (t, s, x, target, moving) = sum_over_devices(own, other, first_advance)
     packed, pred, own, other = call(
         next_network_kernel,
         [struct(HIDDEN, PACKED)] + network_outs,
@@ -557,24 +630,29 @@
         scratch=network_scratch,
         smem=1,
     )
-    part, back = sum_over_devices(own, other)
-    t, s = call(
-        next_advance_kernel,
-        [field, field],
-        place, t, s, *fields[2:], water_indicator, x, pred, packed, *fixed, *moving,
-        scratch=[side_taps],
-        smem=1,
-    )
+
+    def next_advance(part):
+        fields_next = call(
+            next_advance_kernel,
+            [field, field],
+            place, t, s, *fields[2:], mask, x, pred, packed, *fixed, *moving,
+            scratch=side_taps,
+            smem=1,
+        )
+        part, *fields_next = lax.optimization_barrier((part, *fields_next))
+        return part, [], lambda near, far: fields_next
+
+    part, back, (t, s) = sum_over_devices(own, other, next_advance)
     kernel, mix, out = call(
         last_kernel,
-        [struct(HIDDEN, TAPS), struct(HIDDEN, HIDDEN), struct(CHANNELS, HIDDEN)],
+        [struct(TAPS, HIDDEN), struct(HIDDEN, HIDDEN), struct(CHANNELS, HIDDEN)],
         place, packed, part, back,
         smem=1,
     )
     return (
         t.reshape(thermal_anomaly.shape),
         s.reshape(thermal_anomaly.shape),
-        kernel.reshape(kernel_factors.shape),
+        kernel.T.reshape(kernel_factors.shape),
         mix,
         out,
     )

time: 123 us -> 106 us (0.86)
  starting transfers between devices: 63.3 us -> 56.6 us
  local copies, waits for them, and re-layouts: 6.86 us -> 1.66 us
  waiting for transfers between devices: 35.1 us -> 31 us
    ppermute x30 -> x28, starting transfers between devices: 53.3 us -> 47.1 us  [the longest x20 28.5 us: from_chip(): lax.ppermute(value, ('lon', 'lat'), [(i, i ^ mask) for i in range(count)])]
    unnamed x29 -> x11, local copies, waits for them, and re-layouts: 5.81 us -> 1.45 us
    ppermute x30 -> x28, waiting for transfers between devices: 33.3 us -> 29.1 us  [the longest x20 23.9 us: from_chip(): lax.ppermute(value, ('lon', 'lat'), [(i, i ^ mask) for i in range(count)])]
  transfers between devices with their start and end apart: 32 -> 30, of which waited for: 18 -> 18; matrix products, arithmetic and copies ran while one was open for 0% -> 0% of each run, Pallas kernels for 7% -> 7%
where the time goes in v3:
time: 106 us
  starting transfers between devices  56.6 us (53%)
  waiting for transfers between devices  31 us (29%)
  Pallas kernels  15.7 us (15%)
  local copies, waits for them, and re-layouts  1.66 us (2%)
    ppermute x20, starting transfers between devices, from_chip(): lax.ppermute(value, ('lon', 'lat'), [(i, i ^ mask) for i in range(count)])  28.5 us
    ppermute x20, waiting for transfers between devices, from_chip(): lax.ppermute(value, ('lon', 'lat'), [(i, i ^ mask) for i in range(count)])  23.9 us
    pallas_call x6, Pallas kernels, call(): pl.pallas_call(kernel, out_shape=outs, in_specs=specs, out_specs=[pl.Bloc...  15.7 us
    ppermute x2, starting transfers between devices, sum_over_devices(): part = own + lax.ppermute(other, 'grp', flipped('grp', 1))  9.45 us
    ppermute x2, starting transfers between devices, swap_lon(): return (lax.ppermute(inner, 'grp', flipped('grp', 1)), outer)  8 us
    ppermute x2, starting transfers between devices, sum_over_devices(): return (part, lax.ppermute(part, 'grp', flipped('grp', 1)), extra)  4.89 us
    ppermute x1, starting transfers between devices, swap_lat(): lax.ppermute(near, 'lat', flipped('lat', 1))  3.9 us
    ppermute x2, waiting for transfers between devices, swap_lon(): outer = lax.ppermute(outer, axis, chips)  3.71 us
  transfers between devices with their start and end apart: 30, of which 18 were waited for; matrix products, arithmetic and copies ran while one was open for 0% of the time, Pallas kernels for 7%

profile of v3, /device:TPU:1, one launch (start us, length us, event | category | flops | bytes accessed | tf_op | source)
XLA Modules:
  0.0 106.1 jit_solution(3589722767681369342)
XLA Ops:
  0.7 2.5 %shard_map.119 = (f32[96,128]{1,0:T(8,128)S(1)}, f32[96,128]{1,0:T(8,128)S(1)}, f32[8,128]{1,0:T(8,128)S(1)}, f32[8,512]{1,0:T(8,128)S(1)}, f32[272,128]{1,0:T(8...) custom-call(s32[4]{0:T(128)S(1)} %pad_add_fusion.place, f32[96,512]{1,0:T(8,128)} %bitcast.21, ...), custom_call_target="tpu_custom_call" | custom-call | tf_op jit(solution)/shard_map/pallas_call | solution.py:44
  3.2 3.9 %collective-permute-start = (f32[8,128]{1,0:T(8,128)S(1)}, f32[8,128]{1,0:T(8,128)S(1)}, u32[]{:S(2)}, u32[]{:S(2)}) collective-permute-start(f32[8,128]{1,0:T(8,128)S(1)} %get-tuple-element.39), channel_id=1, source_target_pairs={{0,2},{2,0},{4,6},{6,4},{1,3},{3,1},{5,7},{7,5},{8,10},{10,8},{12,... | collective-permute-start | bytes 12296 | tf_op jit(solution)/shard_map/ppermute | solution.py:504
  8.1 3.0 %collective-permute-start.2 = (f32[272,128]{1,0:T(8,128)S(1)}, f32[272,128]{1,0:T(8,128)S(1)}, u32[]{:S(2)}, u32[]{:S(2)}) collective-permute-start(f32[272,128]{1,0:T(8,128)S(1)} %get-tuple-element.74), channel_id=1, source_target_pairs={{0,1},{1,0},{2,3},{3,2},{4,5},{5,4},{6,7},{7,6},{8,9},{9,8},{10,11... | collective-permute-start | bytes 417800 | tf_op jit(solution)/shard_map/ppermute | solution.py:498
  13.1 3.1 %collective-permute-done.3.outer.refs_9_ = f32[272,128]{1,0:T(8,128)S(1)} collective-permute-done((f32[272,128]{1,0:T(8,128)S(1)}, f32[272,128]{1,0:T(8,128)S(1)}, u32[]{:S(2)}, u32[]{:S(2)}) %collective-permute-start.3) | collective-permute-done | bytes 139296 | tf_op jit(solution)/shard_map/ppermute | solution.py:497
  16.1 2.0 %shard_map.120 = (f32[96,128]{1,0:T(8,128)S(1)}, f32[160,128]{1,0:T(8,128)S(1)}, f32[160,128]{1,0:T(8,128)S(1)}) custom-call(s32[4]{0:T(128)S(1)} %pad_add_fusion.place, f32[96,128]{1,0:T(8,128)S(1)} %get-tuple-element.37.x.refs_5_, f32[272,128]{1,0:T(8,128)S(1)} %collective-permute-done.2.inner.refs_8_, ...), custom_call_target="tpu_custom_call" | custom-call | tf_op jit(solution)/shard_map/pallas_call | solution.py:44
  18.2 5.0 %collective-permute-start.4 = (f32[160,128]{1,0:T(8,128)S(1)}, f32[160,128]{1,0:T(8,128)S(1)}, u32[]{:S(2)}, u32[]{:S(2)}) collective-permute-start(f32[160,128]{1,0:T(8,128)S(1)} %get-tuple-element.48), channel_id=1, source_target_pairs={{0,1},{1,0},{2,3},{3,2},{4,5},{5,4},{6,7},{7,6},{8,9},{9,8},{10,11... | collective-permute-start | bytes 245768 | tf_op jit(solution)/shard_map/ppermute | solution.py:534
  24.2 4.5 %shard_map.121 = (f32[96,512]{1,0:T(8,128)S(1)}, f32[96,512]{1,0:T(8,128)S(1)}, f32[96,128]{1,0:T(8,128)S(1)}, f32[96,128]{1,0:T(8,128)S(1)}, f32[208,128]{1,0:T...) custom-call(s32[4]{0:T(128)S(1)} %pad_add_fusion.place, f32[96,512]{1,0:T(8,128)} %bitcast.22, ...), custom_call_target="tpu_custom_call" | custom-call | tf_op jit(solution)/shard_map/pallas_call | solution.py:44
  28.7 3.7 %collective-permute-start.7 = (f32[168,128]{1,0:T(8,128)S(1)}, f32[168,128]{1,0:T(8,128)S(1)}, u32[]{:S(2)}, u32[]{:S(2)}) collective-permute-start(f32[168,128]{1,0:T(8,128)S(1)} %get-tuple-element.70), channel_id=1, source_target_pairs={{0,6},{2,4},{4,2},{6,0},{8,14},{10,12},{12,10},{14,8},{16,22},{18,... | collective-permute-start | bytes 258056 | tf_op jit(solution)/shard_map/ppermute | solution.py:529
  32.5 5.6 %collective-permute-start.6 = (f32[168,128]{1,0:T(8,128)S(1)}, f32[168,128]{1,0:T(8,128)S(1)}, u32[]{:S(2)}, u32[]{:S(2)}) collective-permute-start(f32[168,128]{1,0:T(8,128)S(1)} %get-tuple-element.69), channel_id=1, source_target_pairs={{0,2},{2,0},{4,6},{6,4},{8,10},{10,8},{12,14},{14,12},{16,18},{18,... | collective-permute-start | bytes 258056 | tf_op jit(solution)/shard_map/ppermute | solution.py:529
  38.3 6.1 %collective-permute-done.10 = f32[160,128]{1,0:T(8,128)S(1)} collective-permute-done((f32[160,128]{1,0:T(8,128)S(1)}, f32[160,128]{1,0:T(8,128)S(1)}, u32[]{:S(2)}, u32[]{:S(2)}) %collective-permute-start.10) | collective-permute-done | bytes 81952 | tf_op jit(solution)/shard_map/ppermute | solution.py:529
  50.3 2.8 %collective-permute-start.15 = (f32[160,128]{1,0:T(8,128)S(1)}, f32[160,128]{1,0:T(8,128)S(1)}, u32[]{:S(2)}, u32[]{:S(2)}) collective-permute-start(f32[160,128]{1,0:T(8,128)S(1)} %add_add_fusion.4), channel_id=1, source_target_pairs={{0,128},{2,130},{4,132},{6,134},{8,136},{10,138},{12,140},{14,142}... | collective-permute-start | bytes 245768 | tf_op jit(solution)/shard_map/ppermute | solution.py:529
  54.9 5.0 %collective-permute-start.8 = (f32[208,128]{1,0:T(8,128)S(1)}, f32[208,128]{1,0:T(8,128)S(1)}, u32[]{:S(2)}, u32[]{:S(2)}) collective-permute-start(f32[208,128]{1,0:T(8,128)S(1)} %get-tuple-element.72), channel_id=1, source_target_pairs={{0,1},{1,0},{2,3},{3,2},{4,5},{5,4},{6,7},{7,6},{8,9},{9,8},{10,11... | collective-permute-start | bytes 319496 | tf_op jit(solution)/shard_map/ppermute | solution.py:498
  60.9 3.2 %collective-permute-start.17 = (f32[160,128]{1,0:T(8,128)S(1)}, f32[160,128]{1,0:T(8,128)S(1)}, u32[]{:S(2)}, u32[]{:S(2)}) collective-permute-start(f32[160,128]{1,0:T(8,128)S(1)} %add_add_fusion.3.part), channel_id=1, source_target_pairs={{0,1},{1,0},{2,3},{3,2},{4,5},{5,4},{6,7},{7,6},{8,9},{9,8},{10,11... | collective-permute-start | bytes 245768 | tf_op jit(solution)/shard_map/ppermute | solution.py:546
  65.0 2.0 %shard_map.122 = (f32[64,640]{1,0:T(8,128)S(1)}, f32[96,128]{1,0:T(8,128)S(1)}, f32[160,128]{1,0:T(8,128)S(1)}, f32[160,128]{1,0:T(8,128)S(1)}) custom-call(s32[4]{0:T(128)S(1)} %pad_add_fusion.place, f32[96,128]{1,0:T(8,128)S(1)} %get-tuple-element.45.x.refs_5_, f32[208,128]{1,0:T(8,128)S(1)} %collective-permute-done.8.inner.refs_12_, ...), custom_call_target="tpu_custom_call" | custom-call | tf_op jit(solution)/shard_map/pallas_call | solution.py:44
  67.0 4.4 %collective-permute-start.18 = (f32[160,128]{1,0:T(8,128)S(1)}, f32[160,128]{1,0:T(8,128)S(1)}, u32[]{:S(2)}, u32[]{:S(2)}) collective-permute-start(f32[160,128]{1,0:T(8,128)S(1)} %get-tuple-element.54), channel_id=1, source_target_pairs={{0,1},{1,0},{2,3},{3,2},{4,5},{5,4},{6,7},{7,6},{8,9},{9,8},{10,11... | collective-permute-start | bytes 245768 | tf_op jit(solution)/shard_map/ppermute | solution.py:534
  72.5 3.2 %shard_map.123 = (f32[96,512]{1,0:T(8,128)}, f32[96,512]{1,0:T(8,128)}) custom-call(s32[4]{0:T(128)S(1)} %pad_add_fusion.place, f32[96,512]{1,0:T(8,128)S(1)} %get-tuple-element.55.refs_0_, f32[96,512]{1,0:T(8,128)S(1)} %get-tuple-element.56.refs_1_, f32[96,512]{1,0:T(8,128)S(1)} %bitcast.17, f32[96,512]{1,0:T(8,128)S(1)} %bitcast.20, ...), custom_call_target="tpu_custom_call" | custom-call | tf_op jit(solution)/shard_map/pallas_call | solution.py:44
  76.2 3.3 %collective-permute-start.21 = (f32[160,128]{1,0:T(8,128)S(1)}, f32[160,128]{1,0:T(8,128)S(1)}, u32[]{:S(2)}, u32[]{:S(2)}) collective-permute-start(f32[160,128]{1,0:T(8,128)S(1)} %add.85), channel_id=1, source_target_pairs={{0,12},{2,14},{4,8},{6,10},{8,4},{10,6},{12,0},{14,2},{16,28},{18,... | collective-permute-start | bytes 245768 | tf_op jit(solution)/shard_map/ppermute | solution.py:529
  79.4 2.3 %collective-permute-start.20 = (f32[160,128]{1,0:T(8,128)S(1)}, f32[160,128]{1,0:T(8,128)S(1)}, u32[]{:S(2)}, u32[]{:S(2)}) collective-permute-start(f32[160,128]{1,0:T(8,128)S(1)} %add.85), channel_id=1, source_target_pairs={{0,2},{2,0},{4,6},{6,4},{8,10},{10,8},{12,14},{14,12},{16,18},{18,... | collective-permute-start | bytes 245768 | tf_op jit(solution)/shard_map/ppermute | solution.py:529
  81.7 2.7 %collective-permute-done.21 = f32[160,128]{1,0:T(8,128)S(1)} collective-permute-done((f32[160,128]{1,0:T(8,128)S(1)}, f32[160,128]{1,0:T(8,128)S(1)}, u32[]{:S(2)}, u32[]{:S(2)}) %collective-permute-start.21) | collective-permute-done | bytes 81952 | tf_op jit(solution)/shard_map/ppermute | solution.py:529
  88.2 2.2 %collective-permute-start.23 = (f32[160,128]{1,0:T(8,128)S(1)}, f32[160,128]{1,0:T(8,128)S(1)}, u32[]{:S(2)}, u32[]{:S(2)}) collective-permute-start(f32[160,128]{1,0:T(8,128)S(1)} %add_add_fusion.2), channel_id=1, source_target_pairs={{0,16},{2,18},{4,20},{6,22},{8,24},{10,26},{12,28},{14,30},{16,0},... | collective-permute-start | bytes 245768 | tf_op jit(solution)/shard_map/ppermute | solution.py:529
  90.4 2.3 %collective-permute-done.24 = f32[160,128]{1,0:T(8,128)S(1)} collective-permute-done((f32[160,128]{1,0:T(8,128)S(1)}, f32[160,128]{1,0:T(8,128)S(1)}, u32[]{:S(2)}, u32[]{:S(2)}) %collective-permute-start.24) | collective-permute-done | bytes 81952 | tf_op jit(solution)/shard_map/ppermute | solution.py:529
  92.6 2.1 %collective-permute-done.25 = f32[160,128]{1,0:T(8,128)S(1)} collective-permute-done((f32[160,128]{1,0:T(8,128)S(1)}, f32[160,128]{1,0:T(8,128)S(1)}, u32[]{:S(2)}, u32[]{:S(2)}) %collective-permute-start.25) | collective-permute-done | bytes 81952 | tf_op jit(solution)/shard_map/ppermute | solution.py:529
  97.7 2.0 %collective-permute-done.27 = f32[160,128]{1,0:T(8,128)S(1)} collective-permute-done((f32[160,128]{1,0:T(8,128)S(1)}, f32[160,128]{1,0:T(8,128)S(1)}, u32[]{:S(2)}, u32[]{:S(2)}) %collective-permute-start.27) | collective-permute-done | bytes 81952 | tf_op jit(solution)/shard_map/ppermute | solution.py:529
  99.6 2.2 %collective-permute-done.28 = f32[160,128]{1,0:T(8,128)S(1)} collective-permute-done((f32[160,128]{1,0:T(8,128)S(1)}, f32[160,128]{1,0:T(8,128)S(1)}, u32[]{:S(2)}, u32[]{:S(2)}) %collective-permute-start.28) | collective-permute-done | bytes 81952 | tf_op jit(solution)/shard_map/ppermute | solution.py:529
  (73 shorter events, 26.2 us)
Async XLA Ops:
  3.2 4.9 %collective-permute-start = (f32[8,128]{1,0:T(8,128)S(1)}, f32[8,128]{1,0:T(8,128)S(1)}, u32[]{:S(2)}, u32[]{:S(2)}) collective-permute-start(f32[8,128]{1,0:T(8,128)S(1)} %get-tuple-element.39), channel_id=1, source_target_pairs={{0,2},{2,0},{4,6},{6,4},{1,3},{3,1},{5,7},{7,5},{8,10},{10,8},{12,... | collective-permute-start | bytes 12296 | tf_op jit(solution)/shard_map/ppermute | solution.py:504
  8.1 4.9 %collective-permute-start.2 = (f32[272,128]{1,0:T(8,128)S(1)}, f32[272,128]{1,0:T(8,128)S(1)}, u32[]{:S(2)}, u32[]{:S(2)}) collective-permute-start(f32[272,128]{1,0:T(8,128)S(1)} %get-tuple-element.74), channel_id=1, source_target_pairs={{0,1},{1,0},{2,3},{3,2},{4,5},{5,4},{6,7},{7,6},{8,9},{9,8},{10,11... | collective-permute-start | bytes 417800 | tf_op jit(solution)/shard_map/ppermute | solution.py:498
  11.1 5.0 %collective-permute-start.3 = (f32[272,128]{1,0:T(8,128)S(1)}, f32[272,128]{1,0:T(8,128)S(1)}, u32[]{:S(2)}, u32[]{:S(2)}) collective-permute-start(f32[272,128]{1,0:T(8,128)S(1)} %get-tuple-element.73), channel_id=1, source_target_pairs={{0,249},{1,8},{8,1},{9,16},{16,9},{17,24},{24,17},{25,32},{32,25},... | collective-permute-start | bytes 417800 | tf_op jit(solution)/shard_map/ppermute | solution.py:497
  18.2 5.9 %collective-permute-start.4 = (f32[160,128]{1,0:T(8,128)S(1)}, f32[160,128]{1,0:T(8,128)S(1)}, u32[]{:S(2)}, u32[]{:S(2)}) collective-permute-start(f32[160,128]{1,0:T(8,128)S(1)} %get-tuple-element.48), channel_id=1, source_target_pairs={{0,1},{1,0},{2,3},{3,2},{4,5},{5,4},{6,7},{7,6},{8,9},{9,8},{10,11... | collective-permute-start | bytes 245768 | tf_op jit(solution)/shard_map/ppermute | solution.py:534
  24.1 4.6 %collective-permute-start.5 = (f32[160,128]{1,0:T(8,128)S(1)}, f32[160,128]{1,0:T(8,128)S(1)}, u32[]{:S(2)}, u32[]{:S(2)}) collective-permute-start(f32[160,128]{1,0:T(8,128)S(1)} %add.73), channel_id=1, source_target_pairs={{0,8},{2,10},{4,12},{6,14},{8,0},{10,2},{12,4},{14,6},{16,24},{18,... | collective-permute-start | bytes 245768 | tf_op jit(solution)/shard_map/ppermute | solution.py:529
  28.7 15.6 %collective-permute-start.7 = (f32[168,128]{1,0:T(8,128)S(1)}, f32[168,128]{1,0:T(8,128)S(1)}, u32[]{:S(2)}, u32[]{:S(2)}) collective-permute-start(f32[168,128]{1,0:T(8,128)S(1)} %get-tuple-element.70), channel_id=1, source_target_pairs={{0,6},{2,4},{4,2},{6,0},{8,14},{10,12},{12,10},{14,8},{16,22},{18,... | collective-permute-start | bytes 258056 | tf_op jit(solution)/shard_map/ppermute | solution.py:529
  32.5 11.9 %collective-permute-start.6 = (f32[168,128]{1,0:T(8,128)S(1)}, f32[168,128]{1,0:T(8,128)S(1)}, u32[]{:S(2)}, u32[]{:S(2)}) collective-permute-start(f32[168,128]{1,0:T(8,128)S(1)} %get-tuple-element.69), channel_id=1, source_target_pairs={{0,2},{2,0},{4,6},{6,4},{8,10},{10,8},{12,14},{14,12},{16,18},{18,... | collective-permute-start | bytes 258056 | tf_op jit(solution)/shard_map/ppermute | solution.py:529
  38.1 6.3 %collective-permute-start.10 = (f32[160,128]{1,0:T(8,128)S(1)}, f32[160,128]{1,0:T(8,128)S(1)}, u32[]{:S(2)}, u32[]{:S(2)}) collective-permute-start(f32[160,128]{1,0:T(8,128)S(1)} %add.74), channel_id=1, source_target_pairs={{0,12},{2,14},{4,8},{6,10},{8,4},{10,6},{12,0},{14,2},{16,28},{18,... | collective-permute-start | bytes 245768 | tf_op jit(solution)/shard_map/ppermute | solution.py:529
  44.4 4.9 %collective-permute-start.12 = (f32[160,128]{1,0:T(8,128)S(1)}, f32[160,128]{1,0:T(8,128)S(1)}, u32[]{:S(2)}, u32[]{:S(2)}) collective-permute-start(f32[160,128]{1,0:T(8,128)S(1)} %fusion), channel_id=1, source_target_pairs={{0,32},{2,34},{4,36},{6,38},{8,40},{10,42},{12,44},{14,46},{16,48}... | collective-permute-start | bytes 245768 | tf_op jit(solution)/shard_map/ppermute | solution.py:529
  45.3 4.8 %collective-permute-start.13 = (f32[160,128]{1,0:T(8,128)S(1)}, f32[160,128]{1,0:T(8,128)S(1)}, u32[]{:S(2)}, u32[]{:S(2)}) collective-permute-start(f32[160,128]{1,0:T(8,128)S(1)} %fusion), channel_id=1, source_target_pairs={{0,48},{2,50},{4,52},{6,54},{8,56},{10,58},{12,60},{14,62},{16,32}... | collective-permute-start | bytes 245768 | tf_op jit(solution)/shard_map/ppermute | solution.py:529
  50.3 10.6 %collective-permute-start.15 = (f32[160,128]{1,0:T(8,128)S(1)}, f32[160,128]{1,0:T(8,128)S(1)}, u32[]{:S(2)}, u32[]{:S(2)}) collective-permute-start(f32[160,128]{1,0:T(8,128)S(1)} %add_add_fusion.4), channel_id=1, source_target_pairs={{0,128},{2,130},{4,132},{6,134},{8,136},{10,138},{12,140},{14,142}... | collective-permute-start | bytes 245768 | tf_op jit(solution)/shard_map/ppermute | solution.py:529
  53.1 7.7 %collective-permute-start.16 = (f32[160,128]{1,0:T(8,128)S(1)}, f32[160,128]{1,0:T(8,128)S(1)}, u32[]{:S(2)}, u32[]{:S(2)}) collective-permute-start(f32[160,128]{1,0:T(8,128)S(1)} %add_add_fusion.4), channel_id=1, source_target_pairs={{0,192},{2,194},{4,196},{6,198},{8,200},{10,202},{12,204},{14,206}... | collective-permute-start | bytes 245768 | tf_op jit(solution)/shard_map/ppermute | solution.py:529
  54.4 6.4 %collective-permute-start.14 = (f32[160,128]{1,0:T(8,128)S(1)}, f32[160,128]{1,0:T(8,128)S(1)}, u32[]{:S(2)}, u32[]{:S(2)}) collective-permute-start(f32[160,128]{1,0:T(8,128)S(1)} %add_add_fusion.4), channel_id=1, source_target_pairs={{0,64},{2,66},{4,68},{6,70},{8,72},{10,74},{12,76},{14,78},{16,80}... | collective-permute-start | bytes 245768 | tf_op jit(solution)/shard_map/ppermute | solution.py:529
  54.9 9.1 %collective-permute-start.8 = (f32[208,128]{1,0:T(8,128)S(1)}, f32[208,128]{1,0:T(8,128)S(1)}, u32[]{:S(2)}, u32[]{:S(2)}) collective-permute-start(f32[208,128]{1,0:T(8,128)S(1)} %get-tuple-element.72), channel_id=1, source_target_pairs={{0,1},{1,0},{2,3},{3,2},{4,5},{5,4},{6,7},{7,6},{8,9},{9,8},{10,11... | collective-permute-start | bytes 319496 | tf_op jit(solution)/shard_map/ppermute | solution.py:498
  59.9 4.8 %collective-permute-start.9 = (f32[208,128]{1,0:T(8,128)S(1)}, f32[208,128]{1,0:T(8,128)S(1)}, u32[]{:S(2)}, u32[]{:S(2)}) collective-permute-start(f32[208,128]{1,0:T(8,128)S(1)} %get-tuple-element.71), channel_id=1, source_target_pairs={{0,249},{1,8},{8,1},{9,16},{16,9},{17,24},{24,17},{25,32},{32,25},... | collective-permute-start | bytes 319496 | tf_op jit(solution)/shard_map/ppermute | solution.py:497
  67.0 5.4 %collective-permute-start.18 = (f32[160,128]{1,0:T(8,128)S(1)}, f32[160,128]{1,0:T(8,128)S(1)}, u32[]{:S(2)}, u32[]{:S(2)}) collective-permute-start(f32[160,128]{1,0:T(8,128)S(1)} %get-tuple-element.54), channel_id=1, source_target_pairs={{0,1},{1,0},{2,3},{3,2},{4,5},{5,4},{6,7},{7,6},{8,9},{9,8},{10,11... | collective-permute-start | bytes 245768 | tf_op jit(solution)/shard_map/ppermute | solution.py:534
  76.2 8.2 %collective-permute-start.21 = (f32[160,128]{1,0:T(8,128)S(1)}, f32[160,128]{1,0:T(8,128)S(1)}, u32[]{:S(2)}, u32[]{:S(2)}) collective-permute-start(f32[160,128]{1,0:T(8,128)S(1)} %add.85), channel_id=1, source_target_pairs={{0,12},{2,14},{4,8},{6,10},{8,4},{10,6},{12,0},{14,2},{16,28},{18,... | collective-permute-start | bytes 245768 | tf_op jit(solution)/shard_map/ppermute | solution.py:529
  79.4 6.9 %collective-permute-start.22 = (f32[160,128]{1,0:T(8,128)S(1)}, f32[160,128]{1,0:T(8,128)S(1)}, u32[]{:S(2)}, u32[]{:S(2)}) collective-permute-start(f32[160,128]{1,0:T(8,128)S(1)} %add.85), channel_id=1, source_target_pairs={{0,6},{2,4},{4,2},{6,0},{8,14},{10,12},{12,10},{14,8},{16,22},{18,... | collective-permute-start | bytes 245768 | tf_op jit(solution)/shard_map/ppermute | solution.py:529
  79.4 8.2 %collective-permute-start.20 = (f32[160,128]{1,0:T(8,128)S(1)}, f32[160,128]{1,0:T(8,128)S(1)}, u32[]{:S(2)}, u32[]{:S(2)}) collective-permute-start(f32[160,128]{1,0:T(8,128)S(1)} %add.85), channel_id=1, source_target_pairs={{0,2},{2,0},{4,6},{6,4},{8,10},{10,8},{12,14},{14,12},{16,18},{18,... | collective-permute-start | bytes 245768 | tf_op jit(solution)/shard_map/ppermute | solution.py:529
  87.6 5.0 %collective-permute-start.24 = (f32[160,128]{1,0:T(8,128)S(1)}, f32[160,128]{1,0:T(8,128)S(1)}, u32[]{:S(2)}, u32[]{:S(2)}) collective-permute-start(f32[160,128]{1,0:T(8,128)S(1)} %add_add_fusion.2), channel_id=1, source_target_pairs={{0,32},{2,34},{4,36},{6,38},{8,40},{10,42},{12,44},{14,46},{16,48}... | collective-permute-start | bytes 245768 | tf_op jit(solution)/shard_map/ppermute | solution.py:529
  87.7 7.0 %collective-permute-start.25 = (f32[160,128]{1,0:T(8,128)S(1)}, f32[160,128]{1,0:T(8,128)S(1)}, u32[]{:S(2)}, u32[]{:S(2)}) collective-permute-start(f32[160,128]{1,0:T(8,128)S(1)} %add_add_fusion.2), channel_id=1, source_target_pairs={{0,48},{2,50},{4,52},{6,54},{8,56},{10,58},{12,60},{14,62},{16,32}... | collective-permute-start | bytes 245768 | tf_op jit(solution)/shard_map/ppermute | solution.py:529
  88.2 6.5 %collective-permute-start.23 = (f32[160,128]{1,0:T(8,128)S(1)}, f32[160,128]{1,0:T(8,128)S(1)}, u32[]{:S(2)}, u32[]{:S(2)}) collective-permute-start(f32[160,128]{1,0:T(8,128)S(1)} %add_add_fusion.2), channel_id=1, source_target_pairs={{0,16},{2,18},{4,20},{6,22},{8,24},{10,26},{12,28},{14,30},{16,0},... | collective-permute-start | bytes 245768 | tf_op jit(solution)/shard_map/ppermute | solution.py:529
  94.8 4.9 %collective-permute-start.27 = (f32[160,128]{1,0:T(8,128)S(1)}, f32[160,128]{1,0:T(8,128)S(1)}, u32[]{:S(2)}, u32[]{:S(2)}) collective-permute-start(f32[160,128]{1,0:T(8,128)S(1)} %add_add_fusion.1), channel_id=1, source_target_pairs={{0,128},{2,130},{4,132},{6,134},{8,136},{10,138},{12,140},{14,142}... | collective-permute-start | bytes 245768 | tf_op jit(solution)/shard_map/ppermute | solution.py:529
  96.5 5.3 %collective-permute-start.28 = (f32[160,128]{1,0:T(8,128)S(1)}, f32[160,128]{1,0:T(8,128)S(1)}, u32[]{:S(2)}, u32[]{:S(2)}) collective-permute-start(f32[160,128]{1,0:T(8,128)S(1)} %add_add_fusion.1), channel_id=1, source_target_pairs={{0,192},{2,194},{4,196},{6,198},{8,200},{10,202},{12,204},{14,206}... | collective-permute-start | bytes 245768 | tf_op jit(solution)/shard_map/ppermute | solution.py:529
  (11 other events, 44.2 us)

commit v4 on v3

--- a/solution.py
+++ b/solution.py
@@ -21,8 +21,6 @@
 OUT_AT = 576
 AREA_AT = 624
 PACKED = 640
-COLUMNS_AT = 96
-EDGE_AT = 112
 FINE = 512
 COARSE = 128
 VMEM_LIMIT = 48 * 1024 * 1024
@@ -32,15 +30,14 @@
     return jax.ShapeDtypeStruct(shape, f32)
 
 
-def call(kernel, outs, *args, scratch=(), smem=0, remote=0, flops=0, bytes_accessed=0):
-    first, last = smem, smem + remote
+def call(kernel, outs, *args, scratch=(), remote=0, flops=0, bytes_accessed=0):
     args = [
-        pltpu.with_memory_space_constraint(arg, pltpu.HBM) if first <= at < last else arg
+        pltpu.with_memory_space_constraint(arg, pltpu.HBM) if at < remote else arg
         for at, arg in enumerate(args)
     ]
-    specs = [pl.BlockSpec(memory_space=pltpu.SMEM)] * smem
+    specs = []
     specs += [pl.BlockSpec(memory_space=pltpu.HBM)] * remote
-    specs += [pl.BlockSpec(memory_space=pltpu.VMEM)] * (len(args) - smem - remote)
+    specs += [pl.BlockSpec(memory_space=pltpu.VMEM)] * (len(args) - remote)
     return pl.pallas_call(
         kernel,
         out_shape=outs,
@@ -133,24 +130,29 @@
         return jnp.where(self.flag, self.one[at], self.other[at])
 
 
-def sides(place, inner, outer):
-    first = place[0] == 0
+def sides(inner, outer):
+    first = lax.axis_index("grp") == 0
     return Either(first, outer, inner), Either(first, inner, outer)
 
 
-def fill_edges(place, blocks, fields, column_fields, mask_ref, x_ref, inner_ref, outer_ref, near_ref, far_ref):
-    core_first = place[0] == 0
-    depth = (inner_ref.shape[0] - EDGE_AT) // 4
+def edge_layout(ref):
+    first = 2 * CHANNELS
+    return first, (ref.shape[0] - first) // 4
+
+
+def fill_edges(blocks, fields, mask_ref, x_ref, inner_ref, outer_ref):
+    core_first = lax.axis_index("grp") == 0
+    first_row, depth = edge_layout(inner_ref)
     for out in (inner_ref, outer_ref):
-        out[0:COLUMNS_AT, :] = x_ref[...]
-        out[COLUMNS_AT:, :] = jnp.zeros((out.shape[0] - COLUMNS_AT, COARSE), f32)
+        out[0:first_row, :] = x_ref[...]
+        out[first_row:, :] = jnp.zeros((out.shape[0] - first_row, COARSE), f32)
 
     def put(rows, first, last):
         inner_ref[rows, :] = jnp.where(core_first, last, first)
         outer_ref[rows, :] = jnp.where(core_first, first, last)
 
     for block in range(4):
-        start = EDGE_AT + block * depth
+        start = first_row + block * depth
         for which in range(fields):
             at = start + which * LEVELS
             put(
@@ -162,43 +164,66 @@
             at = start + fields * LEVELS
             lanes = slice(128 * block, 128 * (block + 1))
             put(slice(at, at + 1), mask_ref[0:1, lanes], mask_ref[7:8, lanes])
-    odd = place[3] == 1
+
+
+def put_columns(near_ref, far_ref, at, low, high):
+    odd = lax.axis_index("lat") % 2 == 1
+    near_ref[at : at + 1, 0 : low.shape[1]] = jnp.where(odd, low, high)
+    far_ref[at : at + 1, 0 : low.shape[1]] = jnp.where(odd, high, low)
+
+
+def fill_columns(blocks, column_fields, mask_ref, near_ref, far_ref):
     near_ref[...] = jnp.zeros(near_ref.shape, f32)
     far_ref[...] = jnp.zeros(far_ref.shape, f32)
-
-    def put_columns(at, low, high, low_column, high_column):
-        low, high = low.T[low_column : low_column + 1], high.T[high_column : high_column + 1]
-        near_ref[at : at + 1, 0 : low.shape[1]] = jnp.where(odd, low, high)
-        far_ref[at : at + 1, 0 : low.shape[1]] = jnp.where(odd, high, low)
-
     for at, which in enumerate(column_fields):
-        put_columns(at, blocks[block_rows(which, 0), :], blocks[block_rows(which, 3), :], 0, 127)
+        low, high = (blocks[block_rows(which, block), :].T for block in (0, 3))
+        put_columns(near_ref, far_ref, at, low[0:1], high[127:128])
     if mask_ref is not None:
-        put_columns(3, mask_ref[:, 0:128], mask_ref[:, FINE - 128 : FINE], 0, 127)
-    put_columns(4, x_ref[...], x_ref[...], 0, COARSE - 1)
-    put_columns(5, x_ref[...], x_ref[...], 1, COARSE - 2)
+        low, high = mask_ref[:, 0:128].T[0:1], mask_ref[:, FINE - 128 : FINE].T[127:128]
+        put_columns(near_ref, far_ref, 3, low, high)
+
+
+def columns_kernel(x, x_inner, x_outer, near_fine, far_fine, near, far):
+    for fine, out in ((near_fine, near), (far_fine, far)):
+        out[0:8, :] = fine[...]
+        out[8:16, :] = jnp.zeros((8, COARSE), f32)
+    rows = slice(0, 2 * CHANNELS)
+    for at, ref in enumerate((x, *sides(x_inner, x_outer))):
+        turned = ref[rows, :].T
+        put_columns(near, far, 8 + 2 * at, turned[0:1], turned[127:128])
+        put_columns(near, far, 9 + 2 * at, turned[1:2], turned[126:127])
+
+
+def block_copies(refs, blocks):
+    return [
+        (ref.at[:, pl.ds(128 * block, 128)], blocks.at[block_rows(which, block), :])
+        for which, ref in enumerate(refs)
+        for block in range(4)
+    ]
 
 
 def prepare_kernel(
-    place, t, s, u, v, mask, x, target, weight, mask_values, inner, outer, near, far, sums, blocks, mask_here, semaphore
+    t, s, u, v, mask, x, target, weight, mask_values, inner, outer, sums, blocks, mask_here, semaphore
 ):
-    pairs = [(mask, mask_here)]
-    for which, ref in enumerate((t, s, u, v)):
-        for block in range(4):
-            pairs.append((ref.at[:, pl.ds(128 * block, 128)], blocks.at[block_rows(which, block), :]))
-    copies = fetch(pairs, semaphore)
+    copies = fetch([(mask, mask_here)] + block_copies((t, s, u, v), blocks), semaphore)
     for copy in copies:
         copy.wait()
     m = mask_here[...].astype(f32)
     mask_values[...] = m
     coarsen(blocks, sums, x, target)
-    fill_edges(place, blocks, 3, (0, 1, 3), mask_values, x, inner, outer, near, far)
+    fill_edges(blocks, 3, mask_values, x, inner, outer)
     rows = jnp.concatenate(
         [jnp.sum(m[0:4], axis=0, keepdims=True), jnp.sum(m[4:8], axis=0, keepdims=True)]
         + [jnp.zeros((6, FINE), f32)],
         0,
     )
     weight[...] = jnp.dot(rows.astype(bf16), pooling_matrix(), preferred_element_type=f32)
+
+
+def fine_columns_kernel(t, s, v, mask, near, far, blocks, semaphore):
+    for copy in fetch(block_copies((t, s, v), blocks), semaphore):
+        copy.wait()
+    fill_columns(blocks, (0, 1, 2), mask, near, far)
 
 
 def parts_of(value):
@@ -215,14 +240,11 @@
     return both[:rows] + (both[rows:] + dot(a_high, b_low))
 
 
-def column_matrix(low, high, west, east):
+def column_matrix(low, high):
     rows = []
-    for at in (4, 5):
-        for ref, start in ((low, 0), (high, 0)):
-            rows.append(ref[start + at : start + at + 1, :])
-        for ref in (west, east):
-            for start in (COLUMNS_AT, COLUMNS_AT + 8):
-                rows.append(ref[start + at : start + at + 1, :])
+    for at in (8, 9):
+        for side in range(3):
+            rows += [ref[at + 2 * side : at + 2 * side + 1, :] for ref in (low, high)]
     rows.append(jnp.zeros((4, COARSE), f32))
     return jnp.concatenate(rows, 0).T
 
@@ -293,10 +315,10 @@
 
 
 def network_step(
-    place, x, inner, outer, low, high, target, weight, packed, pred, own, other, taps_high, taps_low, grads
+    x, inner, outer, low, high, target, weight, packed, pred, own, other, taps_high, taps_low, grads
 ):
-    west, east = sides(place, inner, outer)
-    columns = column_matrix(low, high, west, east)
+    west, east = sides(inner, outer)
+    columns = column_matrix(low, high)
     fill_taps((taps_high, taps_low), coarse_rows(x, west, east), columns, (2, 3))
     taps = taps_high[...], taps_low[...]
     kernel = parts_of(packed[:, 0:TAPS])
@@ -335,15 +357,16 @@
     area = jnp.sum(weight[0:2, :], axis=(0, 1), keepdims=True)
     grads[:, AREA_AT : AREA_AT + 1] = jnp.broadcast_to(area, (HIDDEN, 1))
     half = HIDDEN // 2
-    for core, out in ((place[0], own), (1 - place[0], other)):
+    here = lax.axis_index("grp")
+    for core, out in ((here, own), (1 - here, other)):
         rows = pl.ds(pl.multiple_of(core * half, half), half)
         for block in range(PACKED // 128):
             out[half * block : half * (block + 1), :] = grads[rows, 128 * block : 128 * (block + 1)]
 
 
-def descended(place, packed, part, back):
+def descended(packed, part, back):
     half = HIDDEN // 2
-    first = place[0] == 0
+    first = lax.axis_index("grp") == 0
     blocks = []
     for block in range(PACKED // 128):
         mine, theirs = (ref[half * block : half * (block + 1), :] for ref in (part, back))
@@ -355,23 +378,23 @@
     return packed[...] - step * jnp.concatenate(blocks, 1)
 
 
-def next_network_kernel(
-    place, x, inner, outer, low, high, target, weight, packed, part, back, renewed, *rest
-):
-    renewed[...] = descended(place, packed, part, back)
-    network_step(place, x, inner, outer, low, high, target, weight, renewed, *rest)
-
-
-def last_kernel(place, packed, part, back, kernel, mix, out):
-    renewed = descended(place, packed, part, back)
+def next_network_kernel(*refs):
+    *ins, packed, part, back, renewed = refs[:11]
+    renewed[...] = descended(packed, part, back)
+    network_step(*ins, renewed, *refs[11:])
+
+
+def last_kernel(packed, part, back, kernel, mix, out):
+    renewed = descended(packed, part, back)
     kernel[...] = renewed[:, 0:TAPS].T
     mix[...] = renewed[:, MIX_AT : MIX_AT + HIDDEN]
     out[...] = renewed[:, OUT_AT : OUT_AT + CHANNELS].T
 
 
-def forcing(place, x, pred, packed, west, east, low, high, taps):
+def forcing(x, pred, packed, halo, taps):
+    west, east, low, high = halo
     rows = coarse_rows(x, west, east)
-    columns = column_matrix(low, high, west, east)
+    columns = column_matrix(low, high)
     fill_taps(taps, rows, columns, (1, 4))
     fill_side_taps(taps, rows, columns, 2 * COARSE)
     inputs = tuple(ref[...] for ref in taps)
@@ -383,8 +406,9 @@
         parts_of(packed[:, OUT_AT : OUT_AT + CHANNELS].T), parts_of(hidden), 0
     )
     sides = beside[:, 2 * COARSE :]
-    sides_low = jnp.where(place[1] == 0, 0.0, sides)
-    sides_high = jnp.where(place[2] == 0, 0.0, sides)
+    lat = lax.axis_index("lat")
+    sides_low = jnp.where(lat == 0, 0.0, sides)
+    sides_high = jnp.where(lat == lax.axis_size("lat") - 1, 0.0, sides)
     before = (beside[:, 0:COARSE], pred[0:CHANNELS, :])
     after = (pred[CHANNELS : 2 * CHANNELS, :], beside[:, COARSE : 2 * COARSE])
     pieces = []
@@ -408,8 +432,8 @@
     subs = lax.broadcasted_iota(jnp.int32, shape, 0)
 
     def edge_row(ref, at):
-        depth = (ref.shape[0] - EDGE_AT) // 4
-        starts = [EDGE_AT + depth * block + at for block in range(4)]
+        first, depth = edge_layout(ref)
+        starts = [first + depth * block + at for block in range(4)]
         return jnp.concatenate([ref[start : start + 1, :] for start in starts], 1)
 
     def neighbours_lon(value, row_west, row_east):
@@ -464,29 +488,33 @@
             out[at, :] = q + pace * (push - (flux_east - flux_west) - (flux_high - flux_low))
 
 
-def first_advance_kernel(place, *refs):
-    t, s, u, v, mask, x, pred, packed, inner, outer, low, high = refs[:12]
-    t_out, s_out, x_out, target, inner_out, outer_out, near, far = refs[12:20]
+def around(inner, outer, low, high):
+    return (*sides(inner, outer), low, high)
+
+
+def first_advance_kernel(*refs):
+    t, s, u, v, mask, x, pred, packed = refs[:8]
+    halo = around(*refs[8:12])
+    t_out, s_out, x_out, target, inner, outer, near, far = refs[12:20]
     sums, blocks, *taps = refs[20:24]
     t_here, s_here, u_here, v_here, semaphore = refs[24:]
     here = (t_here, s_here, u_here, v_here)
     copies = fetch(list(zip((t, s, u, v), here)), semaphore)
-    halo = (*sides(place, inner, outer), low, high)
-    force = forcing(place, x, pred, packed, *halo, taps)
+    force = forcing(x, pred, packed, halo, taps)
     for copy in copies:
         copy.wait()
     advance(*here, mask, force, halo, halo, t_out, s_out)
     fill_blocks(blocks, (t_out, s_out, u_here, v_here))
     coarsen(blocks, sums, x_out, target)
-    fill_edges(place, blocks, 2, (0, 1), None, x_out, inner_out, outer_out, near, far)
-
-
-def next_advance_kernel(place, *refs):
+    fill_edges(blocks, 2, None, x_out, inner, outer)
+    fill_columns(blocks, (0, 1), None, near, far)
+
+
+def next_advance_kernel(*refs):
     t, s, u, v, mask, x, pred, packed = refs[:8]
-    fixed, moving, (t_out, s_out, *taps) = refs[8:12], refs[12:16], refs[16:]
-    fixed = (*sides(place, *fixed[:2]), *fixed[2:])
-    moving = (*sides(place, *moving[:2]), *moving[2:])
-    force = forcing(place, x, pred, packed, *moving, taps)
+    fixed, moving = around(*refs[8:12]), around(*refs[12:16])
+    t_out, s_out, *taps = refs[16:]
+    force = forcing(x, pred, packed, moving, taps)
     advance(t, s, u, v, mask, force, fixed, moving, t_out, s_out)
 
 
@@ -512,14 +540,6 @@
     return south, jnp.where(lat == lax.axis_size("lat") - 1, 0.0, north)
 
 
-def halo(inner, outer, near, far):
-    south, north = south_north(near, far)
-    columns = jnp.concatenate([south, north], 0)
-    inner = lax.dynamic_update_slice_in_dim(inner, columns, COLUMNS_AT, 0)
-    outer = lax.dynamic_update_slice_in_dim(outer, columns, COLUMNS_AT, 0)
-    return *swap_lon(inner, outer), south, north
-
-
 def flipped(axis, mask):
     return [(i, i ^ mask) for i in range(lax.axis_size(axis))]
 
@@ -529,21 +549,26 @@
     return lax.ppermute(value, ("lon", "lat"), [(i, i ^ mask) for i in range(count)])
 
 
-def sum_over_devices(own, other, beside):
+def sum_of_four(part, bit):
+    if lax.axis_size("lon") * lax.axis_size("lat") <= 2 * bit:
+        return part
+    one, two, three = (from_chip(part, bit * step) for step in (1, 2, 3))
+    return (part + one) + (two + three)
+
+
+def sum_over_devices(own, other, after_pair, riders):
     rows = own.shape[0]
     part = own + lax.ppermute(other, "grp", flipped("grp", 1))
-    part = part + from_chip(part, 4)
-    part, riders, extra = beside(part)
-    near = from_chip(jnp.concatenate([part, *riders[:1]], 0), 1)
+    part = after_pair(part + from_chip(part, 4))
+    for bit in (8, 32):
+        part = sum_of_four(part, bit)
+    near, far = riders()
+    near = from_chip(jnp.concatenate([part, *near], 0), 1)
     cross = from_chip(part, 6)
-    far = from_chip(jnp.concatenate([part, *riders[1:]], 0), 3)
+    far = from_chip(jnp.concatenate([part, *far], 0), 3)
     part = (part + near[:rows]) + (cross + far[:rows])
-    extra = extra(near[rows:], far[rows:])
-    if lax.axis_size("lon") > 2:
-        for bit in (8, 32):
-            one, two, three = (from_chip(part, bit * step) for step in (1, 2, 3))
-            part = (part + one) + (two + three)
-    return part, lax.ppermute(part, "grp", flipped("grp", 1)), extra
+    back = lax.ppermute(part, "grp", flipped("grp", 1))
+    return part, back, (near[rows:], far[rows:])
 
 
 def shards(
@@ -571,11 +596,6 @@
         1,
     )
     blocks = pltpu.VMEM((16 * 8 * LEVELS, 128), f32)
-    lat = lax.axis_index("lat")
-    lat_last = lax.axis_size("lat") - 1
-    place = jnp.stack(
-        [lax.axis_index("grp"), (lat != 0).astype(jnp.int32), (lat != lat_last).astype(jnp.int32), lat % 2]
-    ).astype(jnp.int32)
     field_scratch = pltpu.VMEM((8 * LEVELS, FINE), f32)
     sums = [pltpu.VMEM((4 * CHANNELS, FINE), f32), pltpu.VMEM((16 * 8 * LEVELS, 128), f32)]
     wide = struct(2 * CHANNELS, COARSE)
@@ -586,68 +606,83 @@
     network_scratch = [pltpu.VMEM((TAPS, 2 * COARSE), bf16)] * 2 + [pltpu.VMEM((HIDDEN, PACKED), f32)]
     side_taps = [pltpu.VMEM((TAPS, 3 * COARSE), bf16)] * 2
 
-    edge = struct(EDGE_AT + 160, 128)
-    x, target, weight, mask, *edges = call(
+    edge = struct(2 * CHANNELS + 160, 128)
+    x, target, weight, mask, inner, outer = call(
         prepare_kernel,
-        [wide, wide, tile, struct(8, FINE), edge, edge, tile, tile],
-        place, *fields, water_indicator,
-        scratch=sums
-        + [
-            pltpu.VMEM((8, FINE), jnp.int32),
-            pltpu.SemaphoreType.DMA((17,)),
-        ],
-        smem=1,
+        [wide, wide, tile, struct(8, FINE), edge, edge],
+        *fields, water_indicator,
+        scratch=sums + [pltpu.VMEM((8, FINE), jnp.int32), pltpu.SemaphoreType.DMA((17,))],
         remote=5,
     )
-    fixed = halo(*edges[:2], *swap_lat(*edges[2:]))
+    near, far = call(
+        fine_columns_kernel,
+        [tile, tile],
+        *fields[:2], fields[3], mask,
+        scratch=[sums[1], pltpu.SemaphoreType.DMA((12,))],
+        remote=3,
+    )
+
+    def columns(x, inner, outer, near, far):
+        return call(columns_kernel, [struct(16, 128)] * 2, x, inner, outer, near, far)
+
+    inner, outer = swap_lon(inner, outer)
+    south, north = south_north(*swap_lat(*columns(x, inner, outer, near, far)))
     pred, own, other = call(
         network_step,
         network_outs,
-        place, x, *fixed, target, weight, packed,
+        x, inner, outer, south, north, target, weight, packed,
         scratch=network_scratch,
-        smem=1,
-    )
-    edge = struct(EDGE_AT + 96, 128)
+    )
+    edge = struct(2 * CHANNELS + 96, 128)
+    later = {}
+
+    fixed = inner, outer, south, north
 
     def first_advance(part):
-        t, s, x_next, target_next, *edges = call(
+        t, s, x_next, target, inner, outer, near, far = call(
             first_advance_kernel,
             [field, field, wide, wide, edge, edge, tile, tile],
-            place, *fields, mask, x, pred, packed, *fixed,
+            *fields, mask, x, pred, packed, *fixed,
             scratch=sums + side_taps + [field_scratch] * 4 + [pltpu.SemaphoreType.DMA((4,))],
-            smem=1,
             remote=4,
         )
-        inner, outer, *riders = edges
-        state = t, s, x_next, target_next
-        return part, riders, lambda near, far: (*state, halo(inner, outer, near, far))
-
-    part, back, (t, s, x, target, moving) = sum_over_devices(own, other, first_advance)
+        part, inner, outer = lax.optimization_barrier((part, inner, outer))
+        later["state"] = t, s, x_next, target
+        later["beside"] = swap_lon(inner, outer)
+        later["columns"] = near, far
+        return part
+
+    def first_riders():
+        x_next = later["state"][2]
+        near, far = columns(x_next, *later["beside"], *later["columns"])
+        return [near], [far]
+
+    part, back, received = sum_over_devices(own, other, first_advance, first_riders)
+    moving = *later["beside"], *south_north(*received)
+    t, s, x, target = later["state"]
     packed, pred, own, other = call(
         next_network_kernel,
         [struct(HIDDEN, PACKED)] + network_outs,
-        place, x, *moving, target, weight, packed, part, back,
+        x, *moving, target, weight, packed, part, back,
         scratch=network_scratch,
-        smem=1,
     )
 
     def next_advance(part):
         fields_next = call(
             next_advance_kernel,
             [field, field],
-            place, t, s, *fields[2:], mask, x, pred, packed, *fixed, *moving,
+            t, s, *fields[2:], mask, x, pred, packed, *fixed, *moving,
             scratch=side_taps,
-            smem=1,
         )
-        part, *fields_next = lax.optimization_barrier((part, *fields_next))
-        return part, [], lambda near, far: fields_next
-
-    part, back, (t, s) = sum_over_devices(own, other, next_advance)
+        part, *later["fields"] = lax.optimization_barrier((part, *fields_next))
+        return part
+
+    part, back, _ = sum_over_devices(own, other, next_advance, lambda: ([], []))
+    t, s = later["fields"]
     kernel, mix, out = call(
         last_kernel,
         [struct(TAPS, HIDDEN), struct(HIDDEN, HIDDEN), struct(CHANNELS, HIDDEN)],
-        place, packed, part, back,
-        smem=1,
+        packed, part, back,
     )
     return (
         t.reshape(thermal_anomaly.shape),

time: 106 us -> 99.3 us (0.937)
  waiting for transfers between devices: 31 us -> 25.8 us
  Pallas kernels: 15.7 us -> 13.8 us
    ppermute x2, starting transfers between devices: 4.89 us -> 9.83 us  [sum_over_devices(): back = lax.ppermute(part, 'grp', flipped('grp', 1))]
    ppermute x20, waiting for transfers between devices: 23.9 us -> 19 us  [from_chip(): lax.ppermute(value, ('lon', 'lat'), [(i, i ^ mask) for i in range(count)])]
    ppermute x2, starting transfers between devices: 9.45 us -> 4.73 us  [sum_over_devices(): part = own + lax.ppermute(other, 'grp', flipped('grp', 1))]
    ppermute x1, starting transfers between devices: 3.9 us -> 7.76 us  [swap_lat(): lax.ppermute(near, 'lat', flipped('lat', 1))]
    ppermute x2, starting transfers between devices: 8 us -> 5.16 us  [swap_lon(): return (lax.ppermute(inner, 'grp', flipped('grp', 1)), outer)]
    pallas_call x6 -> x9, Pallas kernels: 15.7 us -> 13.8 us  [call(): pl.pallas_call(kernel, out_shape=outs, in_specs=specs, out_specs=[pl.Bloc...]
    ppermute x20, starting transfers between devices: 28.5 us -> 27.4 us  [from_chip(): lax.ppermute(value, ('lon', 'lat'), [(i, i ^ mask) for i in range(count)])]
  transfers between devices with their start and end apart: 30 -> 30, of which waited for: 18 -> 17; matrix products, arithmetic and copies ran while one was open for 0% -> 0% of each run, Pallas kernels for 7% -> 8%
where the time goes in v4:
time: 99.3 us; the launch traced here: 98.8 us
  starting transfers between devices  56.5 us (57%)
  waiting for transfers between devices  25.8 us (26%)
  Pallas kernels  13.8 us (14%)
  local copies, waits for them, and re-layouts  1.67 us (2%)
    ppermute x20, starting transfers between devices, from_chip(): lax.ppermute(value, ('lon', 'lat'), [(i, i ^ mask) for i in range(count)])  27.4 us
    ppermute x20, waiting for transfers between devices, from_chip(): lax.ppermute(value, ('lon', 'lat'), [(i, i ^ mask) for i in range(count)])  19 us
    pallas_call x9, Pallas kernels, call(): pl.pallas_call(kernel, out_shape=outs, in_specs=specs, out_specs=[pl.Bloc...  13.8 us
    ppermute x2, starting transfers between devices, sum_over_devices(): back = lax.ppermute(part, 'grp', flipped('grp', 1))  9.83 us
    ppermute x1, starting transfers between devices, swap_lat(): lax.ppermute(near, 'lat', flipped('lat', 1))  7.76 us
    ppermute x2, starting transfers between devices, swap_lon(): return (lax.ppermute(inner, 'grp', flipped('grp', 1)), outer)  5.16 us
    ppermute x2, starting transfers between devices, sum_over_devices(): part = own + lax.ppermute(other, 'grp', flipped('grp', 1))  4.73 us
    ppermute x2, waiting for transfers between devices, swap_lon(): outer = lax.ppermute(outer, axis, chips)  3.1 us
  transfers between devices with their start and end apart: 30, of which 17 were waited for; matrix products, arithmetic and copies ran while one was open for 0% of the time, Pallas kernels for 8%

profile of v4, /device:TPU:1, one launch (start us, length us, event | category | flops | bytes accessed | tf_op | source)
XLA Modules:
  0.0 98.8 jit_solution(2470377551186617564)
XLA Ops:
  0.6 1.9 %shard_map.119 = (f32[96,128]{1,0:T(8,128)S(1)}, f32[96,128]{1,0:T(8,128)S(1)}, f32[8,128]{1,0:T(8,128)S(1)}, f32[8,512]{1,0:T(8,128)S(1)}, f32[256,128]{1,0:T(8,128)S(1)}, /*index=5*/f32[256,128]{1,0:T(8,128)S(1)}) custom-call(f32[96,512]{1,0:T(8,128)} %bitcast.18, f32[96,512]{1,0:T(8,128)} %bitcast.21, f32[96,512]{1,0:T(8,128)} %bitcast.15, ...), custom_call_target="tpu_custom_call" | custom-call | tf_op jit(solution)/shard_map/pallas_call | solution.py:41
  2.5 3.3 %collective-permute-start = (f32[256,128]{1,0:T(8,128)S(1)}, f32[256,128]{1,0:T(8,128)S(1)}, u32[]{:S(2)}, u32[]{:S(2)}) collective-permute-start(f32[256,128]{1,0:T(8,128)S(1)} %get-tuple-element.45), channel_id=1, source_target_pairs={{0,1},{1,0},{2,3},{3,2},{4,5},{5,4},{6,7},{7,6},{8,9},{9,8},{10,11... | collective-permute-start | bytes 393224 | tf_op jit(solution)/shard_map/ppermute | solution.py:526
  7.2 3.1 %collective-permute-done.1.x_outer.outer.refs_9_ = f32[256,128]{1,0:T(8,128)S(1)} collective-permute-done((f32[256,128]{1,0:T(8,128)S(1)}, f32[256,128]{1,0:T(8,128)S(1)}, u32[]{:S(2)}, u32[]{:S(2)}) %collective-permute-start.1) | collective-permute-done | bytes 131104 | tf_op jit(solution)/shard_map/ppermute | solution.py:525
  11.1 7.8 %collective-permute-start.2 = (f32[16,128]{1,0:T(8,128)S(1)}, f32[16,128]{1,0:T(8,128)S(1)}, u32[]{:S(2)}, u32[]{:S(2)}) collective-permute-start(f32[16,128]{1,0:T(8,128)S(1)} %get-tuple-element.49), channel_id=1, source_target_pairs={{0,2},{2,0},{4,6},{6,4},{1,3},{3,1},{5,7},{7,5},{8,10},{10,8},{12,... | collective-permute-start | bytes 24584 | tf_op jit(solution)/shard_map/ppermute | solution.py:532
  20.6 1.5 %shard_map.122 = (f32[96,128]{1,0:T(8,128)S(1)}, f32[160,128]{1,0:T(8,128)S(1)}, f32[160,128]{1,0:T(8,128)S(1)}) custom-call(f32[96,128]{1,0:T(8,128)S(1)} %get-tuple-element.44.x.refs_5_, f32[256,128]{1,0:T(8,128)S(1)} %collective-permute-done.x_inner.inner.refs_8_, f32[256,128]{1,0:T(8,128)S(1)} %collective-permute-done.1.x_outer.outer.refs_9_, ...), custom_call_target="tpu_custom_call" | custom-call | tf_op jit(solution)/shard_map/pallas_call | solution.py:41
  22.1 4.3 %collective-permute-start.4 = (f32[160,128]{1,0:T(8,128)S(1)}, f32[160,128]{1,0:T(8,128)S(1)}, u32[]{:S(2)}, u32[]{:S(2)}) collective-permute-start(f32[160,128]{1,0:T(8,128)S(1)} %get-tuple-element.56), channel_id=1, source_target_pairs={{0,1},{1,0},{2,3},{3,2},{4,5},{5,4},{6,7},{7,6},{8,9},{9,8},{10,11... | collective-permute-start | bytes 245768 | tf_op jit(solution)/shard_map/ppermute | solution.py:561
  27.4 3.8 %shard_map.123 = (f32[96,512]{1,0:T(8,128)S(1)}, f32[96,512]{1,0:T(8,128)S(1)}, f32[96,128]{1,0:T(8,128)S(1)}, f32[96,128]{1,0:T(8,128)S(1)}, f32[192,128]{1,0:T...) custom-call(f32[96,512]{1,0:T(8,128)} %bitcast.20, f32[96,512]{1,0:T(8,128)} %bitcast.23, ...), custom_call_target="tpu_custom_call" | custom-call | tf_op jit(solution)/shard_map/pallas_call | solution.py:41
  31.6 1.4 %collective-permute-start.10 = (f32[160,128]{1,0:T(8,128)S(1)}, f32[160,128]{1,0:T(8,128)S(1)}, u32[]{:S(2)}, u32[]{:S(2)}) collective-permute-start(f32[160,128]{1,0:T(8,128)S(1)} %add.73), channel_id=1, source_target_pairs={{0,48},{2,50},{4,52},{6,54},{8,56},{10,58},{12,60},{14,62},{16,32}... | collective-permute-start | bytes 245768 | tf_op jit(solution)/shard_map/ppermute | solution.py:549
  34.0 1.8 %collective-permute-start.6 = (f32[192,128]{1,0:T(8,128)S(1)}, f32[192,128]{1,0:T(8,128)S(1)}, u32[]{:S(2)}, u32[]{:S(2)}) collective-permute-start(f32[192,128]{1,0:T(8,128)S(1)} %get-tuple-element.59), channel_id=1, source_target_pairs={{0,1},{1,0},{2,3},{3,2},{4,5},{5,4},{6,7},{7,6},{8,9},{9,8},{10,11... | collective-permute-start | bytes 294920 | tf_op jit(solution)/shard_map/ppermute | solution.py:526
  37.8 2.6 %collective-permute-start.12 = (f32[160,128]{1,0:T(8,128)S(1)}, f32[160,128]{1,0:T(8,128)S(1)}, u32[]{:S(2)}, u32[]{:S(2)}) collective-permute-start(f32[160,128]{1,0:T(8,128)S(1)} %add_add_fusion.4), channel_id=1, source_target_pairs={{0,128},{2,130},{4,132},{6,134},{8,136},{10,138},{12,140},{14,142}... | collective-permute-start | bytes 245768 | tf_op jit(solution)/shard_map/ppermute | solution.py:549
  43.0 1.9 %collective-permute-done.13 = f32[160,128]{1,0:T(8,128)S(1)} collective-permute-done((f32[160,128]{1,0:T(8,128)S(1)}, f32[160,128]{1,0:T(8,128)S(1)}, u32[]{:S(2)}, u32[]{:S(2)}) %collective-permute-start.13) | collective-permute-done | bytes 81952 | tf_op jit(solution)/shard_map/ppermute | solution.py:549
  45.7 3.4 %collective-permute-start.14 = (f32[176,128]{1,0:T(8,128)S(1)}, f32[176,128]{1,0:T(8,128)S(1)}, u32[]{:S(2)}, u32[]{:S(2)}) collective-permute-start(f32[176,128]{1,0:T(8,128)S(1)} %get-tuple-element.83), channel_id=1, source_target_pairs={{0,2},{2,0},{4,6},{6,4},{8,10},{10,8},{12,14},{14,12},{16,18},{18,... | collective-permute-start | bytes 270344 | tf_op jit(solution)/shard_map/ppermute | solution.py:549
  49.1 3.1 %collective-permute-start.16 = (f32[160,128]{1,0:T(8,128)S(1)}, f32[160,128]{1,0:T(8,128)S(1)}, u32[]{:S(2)}, u32[]{:S(2)}) collective-permute-start(f32[160,128]{1,0:T(8,128)S(1)} %add_add_fusion.3), channel_id=1, source_target_pairs={{0,12},{2,14},{4,8},{6,10},{8,4},{10,6},{12,0},{14,2},{16,28},{18,... | collective-permute-start | bytes 245768 | tf_op jit(solution)/shard_map/ppermute | solution.py:549
  52.2 3.7 %collective-permute-done.16 = f32[160,128]{1,0:T(8,128)S(1)} collective-permute-done((f32[160,128]{1,0:T(8,128)S(1)}, f32[160,128]{1,0:T(8,128)S(1)}, u32[]{:S(2)}, u32[]{:S(2)}) %collective-permute-start.16) | collective-permute-done | bytes 81952 | tf_op jit(solution)/shard_map/ppermute | solution.py:549
  55.9 4.0 %collective-permute-start.17 = (f32[160,128]{1,0:T(8,128)S(1)}, f32[160,128]{1,0:T(8,128)S(1)}, u32[]{:S(2)}, u32[]{:S(2)}) collective-permute-start(f32[160,128]{1,0:T(8,128)S(1)} %fusion.refs_8_), channel_id=1, source_target_pairs={{0,1},{1,0},{2,3},{3,2},{4,5},{5,4},{6,7},{7,6},{8,9},{9,8},{10,11... | collective-permute-start | bytes 245768 | tf_op jit(solution)/shard_map/ppermute | solution.py:570
  60.9 1.5 %shard_map.125 = (f32[64,640]{1,0:T(8,128)S(1)}, f32[96,128]{1,0:T(8,128)S(1)}, f32[160,128]{1,0:T(8,128)S(1)}, f32[160,128]{1,0:T(8,128)S(1)}) custom-call(f32[96,128]{1,0:T(8,128)S(1)} %get-tuple-element.54.x.refs_0_.refs_5_, f32[192,128]{1,0:T(8,128)S(1)} %collective-permute-done.6.x_inner.refs_1_.refs_12_, ...), custom_call_target="tpu_custom_call" | custom-call | tf_op jit(solution)/shard_map/pallas_call | solution.py:41
  65.1 2.6 %shard_map.126 = (f32[96,512]{1,0:T(8,128)}, f32[96,512]{1,0:T(8,128)}) custom-call(f32[96,512]{1,0:T(8,128)S(1)} %get-tuple-element.69.refs_0_, f32[96,512]{1,0:T(8,128)S(1)} %get-tuple-element.70.refs_1_, f32[96,512]{1,0:T(8,128)S(1)} %bitcast.17, f32[96,512]{1,0:T(8,128)S(1)} %bitcast.14, f32[8,512]{1,0:T(8,128)S(1)} %get-tuple-element.43.mask.refs_4_, ...), custom_call_target="tpu_custom_call" | custom-call | tf_op jit(solution)/shard_map/pallas_call | solution.py:41
  68.7 2.7 %collective-permute-start.22 = (f32[160,128]{1,0:T(8,128)S(1)}, f32[160,128]{1,0:T(8,128)S(1)}, u32[]{:S(2)}, u32[]{:S(2)}) collective-permute-start(f32[160,128]{1,0:T(8,128)S(1)} %add.84), channel_id=1, source_target_pairs={{0,48},{2,50},{4,52},{6,54},{8,56},{10,58},{12,60},{14,62},{16,32}... | collective-permute-start | bytes 245768 | tf_op jit(solution)/shard_map/ppermute | solution.py:549
  72.6 1.8 %collective-permute-done.22 = f32[160,128]{1,0:T(8,128)S(1)} collective-permute-done((f32[160,128]{1,0:T(8,128)S(1)}, f32[160,128]{1,0:T(8,128)S(1)}, u32[]{:S(2)}, u32[]{:S(2)}) %collective-permute-start.22) | collective-permute-done | bytes 81952 | tf_op jit(solution)/shard_map/ppermute | solution.py:549
  75.0 1.6 %collective-permute-start.24 = (f32[160,128]{1,0:T(8,128)S(1)}, f32[160,128]{1,0:T(8,128)S(1)}, u32[]{:S(2)}, u32[]{:S(2)}) collective-permute-start(f32[160,128]{1,0:T(8,128)S(1)} %add_add_fusion.2), channel_id=1, source_target_pairs={{0,128},{2,130},{4,132},{6,134},{8,136},{10,138},{12,140},{14,142}... | collective-permute-start | bytes 245768 | tf_op jit(solution)/shard_map/ppermute | solution.py:549
  77.8 2.1 %collective-permute-done.24 = f32[160,128]{1,0:T(8,128)S(1)} collective-permute-done((f32[160,128]{1,0:T(8,128)S(1)}, f32[160,128]{1,0:T(8,128)S(1)}, u32[]{:S(2)}, u32[]{:S(2)}) %collective-permute-start.24) | collective-permute-done | bytes 81952 | tf_op jit(solution)/shard_map/ppermute | solution.py:549
  81.2 4.2 %collective-permute-start.27 = (f32[160,128]{1,0:T(8,128)S(1)}, f32[160,128]{1,0:T(8,128)S(1)}, u32[]{:S(2)}, u32[]{:S(2)}) collective-permute-start(f32[160,128]{1,0:T(8,128)S(1)} %add_add_fusion.1), channel_id=1, source_target_pairs={{0,12},{2,14},{4,8},{6,10},{8,4},{10,6},{12,0},{14,2},{16,28},{18,... | collective-permute-start | bytes 245768 | tf_op jit(solution)/shard_map/ppermute | solution.py:549
  87.6 3.3 %collective-permute-done.28 = f32[160,128]{1,0:T(8,128)S(1)} collective-permute-done((f32[160,128]{1,0:T(8,128)S(1)}, f32[160,128]{1,0:T(8,128)S(1)}, u32[]{:S(2)}, u32[]{:S(2)}) %collective-permute-start.28) | collective-permute-done | bytes 81952 | tf_op jit(solution)/shard_map/ppermute | solution.py:549
  91.2 5.8 %collective-permute-start.29 = (f32[160,128]{1,0:T(8,128)S(1)}, f32[160,128]{1,0:T(8,128)S(1)}, u32[]{:S(2)}, u32[]{:S(2)}) collective-permute-start(f32[160,128]{1,0:T(8,128)S(1)} %add_add_fusion.part), channel_id=1, source_target_pairs={{0,1},{1,0},{2,3},{3,2},{4,5},{5,4},{6,7},{7,6},{8,9},{9,8},{10,11... | collective-permute-start | bytes 245768 | tf_op jit(solution)/shard_map/ppermute | solution.py:570
  (73 shorter events, 24.7 us)
Async XLA Ops:
  2.5 4.7 %collective-permute-start = (f32[256,128]{1,0:T(8,128)S(1)}, f32[256,128]{1,0:T(8,128)S(1)}, u32[]{:S(2)}, u32[]{:S(2)}) collective-permute-start(f32[256,128]{1,0:T(8,128)S(1)} %get-tuple-element.45), channel_id=1, source_target_pairs={{0,1},{1,0},{2,3},{3,2},{4,5},{5,4},{6,7},{7,6},{8,9},{9,8},{10,11... | collective-permute-start | bytes 393224 | tf_op jit(solution)/shard_map/ppermute | solution.py:526
  5.8 4.5 %collective-permute-start.1 = (f32[256,128]{1,0:T(8,128)S(1)}, f32[256,128]{1,0:T(8,128)S(1)}, u32[]{:S(2)}, u32[]{:S(2)}) collective-permute-start(f32[256,128]{1,0:T(8,128)S(1)} %get-tuple-element.46), channel_id=1, source_target_pairs={{0,249},{1,8},{8,1},{9,16},{16,9},{17,24},{24,17},{25,32},{32,25},... | collective-permute-start | bytes 393224 | tf_op jit(solution)/shard_map/ppermute | solution.py:525
  10.4 10.1 %collective-permute-start.3 = (f32[16,128]{1,0:T(8,128)S(1)}, f32[16,128]{1,0:T(8,128)S(1)}, u32[]{:S(2)}, u32[]{:S(2)}) collective-permute-start(f32[16,128]{1,0:T(8,128)S(1)} %get-tuple-element.50), channel_id=1, source_target_pairs={{2,4},{4,2},{3,5},{5,3},{10,12},{12,10},{11,13},{13,11},{18,20},{2... | collective-permute-start | bytes 24584 | tf_op jit(solution)/shard_map/ppermute | solution.py:532
  11.1 9.5 %collective-permute-start.2 = (f32[16,128]{1,0:T(8,128)S(1)}, f32[16,128]{1,0:T(8,128)S(1)}, u32[]{:S(2)}, u32[]{:S(2)}) collective-permute-start(f32[16,128]{1,0:T(8,128)S(1)} %get-tuple-element.49), channel_id=1, source_target_pairs={{0,2},{2,0},{4,6},{6,4},{1,3},{3,1},{5,7},{7,5},{8,10},{10,8},{12,... | collective-permute-start | bytes 24584 | tf_op jit(solution)/shard_map/ppermute | solution.py:532
  22.1 5.2 %collective-permute-start.4 = (f32[160,128]{1,0:T(8,128)S(1)}, f32[160,128]{1,0:T(8,128)S(1)}, u32[]{:S(2)}, u32[]{:S(2)}) collective-permute-start(f32[160,128]{1,0:T(8,128)S(1)} %get-tuple-element.56), channel_id=1, source_target_pairs={{0,1},{1,0},{2,3},{3,2},{4,5},{5,4},{6,7},{7,6},{8,9},{9,8},{10,11... | collective-permute-start | bytes 245768 | tf_op jit(solution)/shard_map/ppermute | solution.py:561
  31.3 5.6 %collective-permute-start.9 = (f32[160,128]{1,0:T(8,128)S(1)}, f32[160,128]{1,0:T(8,128)S(1)}, u32[]{:S(2)}, u32[]{:S(2)}) collective-permute-start(f32[160,128]{1,0:T(8,128)S(1)} %add.73), channel_id=1, source_target_pairs={{0,32},{2,34},{4,36},{6,38},{8,40},{10,42},{12,44},{14,46},{16,48}... | collective-permute-start | bytes 245768 | tf_op jit(solution)/shard_map/ppermute | solution.py:549
  31.6 6.2 %collective-permute-start.10 = (f32[160,128]{1,0:T(8,128)S(1)}, f32[160,128]{1,0:T(8,128)S(1)}, u32[]{:S(2)}, u32[]{:S(2)}) collective-permute-start(f32[160,128]{1,0:T(8,128)S(1)} %add.73), channel_id=1, source_target_pairs={{0,48},{2,50},{4,52},{6,54},{8,56},{10,58},{12,60},{14,62},{16,32}... | collective-permute-start | bytes 245768 | tf_op jit(solution)/shard_map/ppermute | solution.py:549
  33.0 4.8 %collective-permute-start.8 = (f32[160,128]{1,0:T(8,128)S(1)}, f32[160,128]{1,0:T(8,128)S(1)}, u32[]{:S(2)}, u32[]{:S(2)}) collective-permute-start(f32[160,128]{1,0:T(8,128)S(1)} %add.73), channel_id=1, source_target_pairs={{0,16},{2,18},{4,20},{6,22},{8,24},{10,26},{12,28},{14,30},{16,0},... | collective-permute-start | bytes 245768 | tf_op jit(solution)/shard_map/ppermute | solution.py:549
  34.0 7.9 %collective-permute-start.6 = (f32[192,128]{1,0:T(8,128)S(1)}, f32[192,128]{1,0:T(8,128)S(1)}, u32[]{:S(2)}, u32[]{:S(2)}) collective-permute-start(f32[192,128]{1,0:T(8,128)S(1)} %get-tuple-element.59), channel_id=1, source_target_pairs={{0,1},{1,0},{2,3},{3,2},{4,5},{5,4},{6,7},{7,6},{8,9},{9,8},{10,11... | collective-permute-start | bytes 294920 | tf_op jit(solution)/shard_map/ppermute | solution.py:526
  35.8 6.0 %collective-permute-start.7 = (f32[192,128]{1,0:T(8,128)S(1)}, f32[192,128]{1,0:T(8,128)S(1)}, u32[]{:S(2)}, u32[]{:S(2)}) collective-permute-start(f32[192,128]{1,0:T(8,128)S(1)} %get-tuple-element.60), channel_id=1, source_target_pairs={{0,249},{1,8},{8,1},{9,16},{16,9},{17,24},{24,17},{25,32},{32,25},... | collective-permute-start | bytes 294920 | tf_op jit(solution)/shard_map/ppermute | solution.py:525
  37.8 5.2 %collective-permute-start.12 = (f32[160,128]{1,0:T(8,128)S(1)}, f32[160,128]{1,0:T(8,128)S(1)}, u32[]{:S(2)}, u32[]{:S(2)}) collective-permute-start(f32[160,128]{1,0:T(8,128)S(1)} %add_add_fusion.4), channel_id=1, source_target_pairs={{0,128},{2,130},{4,132},{6,134},{8,136},{10,138},{12,140},{14,142}... | collective-permute-start | bytes 245768 | tf_op jit(solution)/shard_map/ppermute | solution.py:549
  40.4 4.5 %collective-permute-start.13 = (f32[160,128]{1,0:T(8,128)S(1)}, f32[160,128]{1,0:T(8,128)S(1)}, u32[]{:S(2)}, u32[]{:S(2)}) collective-permute-start(f32[160,128]{1,0:T(8,128)S(1)} %add_add_fusion.4), channel_id=1, source_target_pairs={{0,192},{2,194},{4,196},{6,198},{8,200},{10,202},{12,204},{14,206}... | collective-permute-start | bytes 245768 | tf_op jit(solution)/shard_map/ppermute | solution.py:549
  45.0 10.9 %collective-permute-start.15 = (f32[176,128]{1,0:T(8,128)S(1)}, f32[176,128]{1,0:T(8,128)S(1)}, u32[]{:S(2)}, u32[]{:S(2)}) collective-permute-start(f32[176,128]{1,0:T(8,128)S(1)} %get-tuple-element.84), channel_id=1, source_target_pairs={{0,6},{2,4},{4,2},{6,0},{8,14},{10,12},{12,10},{14,8},{16,22},{18,... | collective-permute-start | bytes 270344 | tf_op jit(solution)/shard_map/ppermute | solution.py:549
  45.7 10.2 %collective-permute-start.14 = (f32[176,128]{1,0:T(8,128)S(1)}, f32[176,128]{1,0:T(8,128)S(1)}, u32[]{:S(2)}, u32[]{:S(2)}) collective-permute-start(f32[176,128]{1,0:T(8,128)S(1)} %get-tuple-element.83), channel_id=1, source_target_pairs={{0,2},{2,0},{4,6},{6,4},{8,10},{10,8},{12,14},{14,12},{16,18},{18,... | collective-permute-start | bytes 270344 | tf_op jit(solution)/shard_map/ppermute | solution.py:549
  49.1 6.8 %collective-permute-start.16 = (f32[160,128]{1,0:T(8,128)S(1)}, f32[160,128]{1,0:T(8,128)S(1)}, u32[]{:S(2)}, u32[]{:S(2)}) collective-permute-start(f32[160,128]{1,0:T(8,128)S(1)} %add_add_fusion.3), channel_id=1, source_target_pairs={{0,12},{2,14},{4,8},{6,10},{8,4},{10,6},{12,0},{14,2},{16,28},{18,... | collective-permute-start | bytes 245768 | tf_op jit(solution)/shard_map/ppermute | solution.py:549
  55.9 5.0 %collective-permute-start.17 = (f32[160,128]{1,0:T(8,128)S(1)}, f32[160,128]{1,0:T(8,128)S(1)}, u32[]{:S(2)}, u32[]{:S(2)}) collective-permute-start(f32[160,128]{1,0:T(8,128)S(1)} %fusion.refs_8_), channel_id=1, source_target_pairs={{0,1},{1,0},{2,3},{3,2},{4,5},{5,4},{6,7},{7,6},{8,9},{9,8},{10,11... | collective-permute-start | bytes 245768 | tf_op jit(solution)/shard_map/ppermute | solution.py:570
  67.7 4.9 %collective-permute-start.21 = (f32[160,128]{1,0:T(8,128)S(1)}, f32[160,128]{1,0:T(8,128)S(1)}, u32[]{:S(2)}, u32[]{:S(2)}) collective-permute-start(f32[160,128]{1,0:T(8,128)S(1)} %add.84), channel_id=1, source_target_pairs={{0,32},{2,34},{4,36},{6,38},{8,40},{10,42},{12,44},{14,46},{16,48}... | collective-permute-start | bytes 245768 | tf_op jit(solution)/shard_map/ppermute | solution.py:549
  68.7 5.8 %collective-permute-start.22 = (f32[160,128]{1,0:T(8,128)S(1)}, f32[160,128]{1,0:T(8,128)S(1)}, u32[]{:S(2)}, u32[]{:S(2)}) collective-permute-start(f32[160,128]{1,0:T(8,128)S(1)} %add.84), channel_id=1, source_target_pairs={{0,48},{2,50},{4,52},{6,54},{8,56},{10,58},{12,60},{14,62},{16,32}... | collective-permute-start | bytes 245768 | tf_op jit(solution)/shard_map/ppermute | solution.py:549
  75.0 4.9 %collective-permute-start.24 = (f32[160,128]{1,0:T(8,128)S(1)}, f32[160,128]{1,0:T(8,128)S(1)}, u32[]{:S(2)}, u32[]{:S(2)}) collective-permute-start(f32[160,128]{1,0:T(8,128)S(1)} %add_add_fusion.2), channel_id=1, source_target_pairs={{0,128},{2,130},{4,132},{6,134},{8,136},{10,138},{12,140},{14,142}... | collective-permute-start | bytes 245768 | tf_op jit(solution)/shard_map/ppermute | solution.py:549
  76.6 4.5 %collective-permute-start.25 = (f32[160,128]{1,0:T(8,128)S(1)}, f32[160,128]{1,0:T(8,128)S(1)}, u32[]{:S(2)}, u32[]{:S(2)}) collective-permute-start(f32[160,128]{1,0:T(8,128)S(1)} %add_add_fusion.2), channel_id=1, source_target_pairs={{0,192},{2,194},{4,196},{6,198},{8,200},{10,202},{12,204},{14,206}... | collective-permute-start | bytes 245768 | tf_op jit(solution)/shard_map/ppermute | solution.py:549
  81.2 6.4 %collective-permute-start.27 = (f32[160,128]{1,0:T(8,128)S(1)}, f32[160,128]{1,0:T(8,128)S(1)}, u32[]{:S(2)}, u32[]{:S(2)}) collective-permute-start(f32[160,128]{1,0:T(8,128)S(1)} %add_add_fusion.1), channel_id=1, source_target_pairs={{0,12},{2,14},{4,8},{6,10},{8,4},{10,6},{12,0},{14,2},{16,28},{18,... | collective-permute-start | bytes 245768 | tf_op jit(solution)/shard_map/ppermute | solution.py:549
  85.3 5.5 %collective-permute-start.28 = (f32[160,128]{1,0:T(8,128)S(1)}, f32[160,128]{1,0:T(8,128)S(1)}, u32[]{:S(2)}, u32[]{:S(2)}) collective-permute-start(f32[160,128]{1,0:T(8,128)S(1)} %add_add_fusion.1), channel_id=1, source_target_pairs={{0,6},{2,4},{4,2},{6,0},{8,14},{10,12},{12,10},{14,8},{16,22},{18,... | collective-permute-start | bytes 245768 | tf_op jit(solution)/shard_map/ppermute | solution.py:549
  86.7 4.5 %collective-permute-start.26 = (f32[160,128]{1,0:T(8,128)S(1)}, f32[160,128]{1,0:T(8,128)S(1)}, u32[]{:S(2)}, u32[]{:S(2)}) collective-permute-start(f32[160,128]{1,0:T(8,128)S(1)} %add_add_fusion.1), channel_id=1, source_target_pairs={{0,2},{2,0},{4,6},{6,4},{8,10},{10,8},{12,14},{14,12},{16,18},{18,... | collective-permute-start | bytes 245768 | tf_op jit(solution)/shard_map/ppermute | solution.py:549
  91.2 6.7 %collective-permute-start.29 = (f32[160,128]{1,0:T(8,128)S(1)}, f32[160,128]{1,0:T(8,128)S(1)}, u32[]{:S(2)}, u32[]{:S(2)}) collective-permute-start(f32[160,128]{1,0:T(8,128)S(1)} %add_add_fusion.part), channel_id=1, source_target_pairs={{0,1},{1,0},{2,3},{3,2},{4,5},{5,4},{6,7},{7,6},{8,9},{9,8},{10,11... | collective-permute-start | bytes 245768 | tf_op jit(solution)/shard_map/ppermute | solution.py:570
  (11 other events, 40.5 us)

commit v5 on v4

--- a/solution.py
+++ b/solution.py
@@ -17,10 +17,13 @@
 CHANNELS = 4 * LEVELS
 HIDDEN = 64
 TAPS = 9 * CHANNELS
-MIX_AT = 512
-OUT_AT = 576
-AREA_AT = 624
+MIX_AT = 432
+OUT_AT = 496
+REST_AT = 512
+USED = 544
 PACKED = 640
+HALF = HIDDEN // 2
+SUMMED = 4 * HALF + 8
 FINE = 512
 COARSE = 128
 VMEM_LIMIT = 48 * 1024 * 1024
@@ -350,42 +353,50 @@
     back_one = parts_of(
         dot_parts(parts_of(mix.T), back_two, 0) * (1.0 - hidden_one * hidden_one)
     )
-    grads[:, MIX_AT - 128 : PACKED] = jnp.zeros((HIDDEN, PACKED - MIX_AT + 128), f32)
     grads[:, 0:TAPS] = dot_parts(back_one, taps, 1)
     grads[:, MIX_AT : MIX_AT + HIDDEN] = dot_parts(back_two, one, 1)
     grads[:, OUT_AT : OUT_AT + CHANNELS] = dot_parts(two, back_out, 1)
-    area = jnp.sum(weight[0:2, :], axis=(0, 1), keepdims=True)
-    grads[:, AREA_AT : AREA_AT + 1] = jnp.broadcast_to(area, (HIDDEN, 1))
-    half = HIDDEN // 2
     here = lax.axis_index("grp")
     for core, out in ((here, own), (1 - here, other)):
-        rows = pl.ds(pl.multiple_of(core * half, half), half)
-        for block in range(PACKED // 128):
-            out[half * block : half * (block + 1), :] = grads[rows, 128 * block : 128 * (block + 1)]
-
-
-def descended(packed, part, back):
-    half = HIDDEN // 2
+        start = core * HALF
+        rows = pl.ds(pl.multiple_of(start, HALF), HALF)
+        for block in range(4):
+            out[HALF * block : HALF * (block + 1), :] = grads[rows, 128 * block : 128 * (block + 1)]
+        for part in range(4):
+            rows = pl.ds(pl.multiple_of(start + 8 * part, 8), 8)
+            out[4 * HALF : SUMMED, 32 * part : 32 * (part + 1)] = grads[rows, REST_AT:USED]
+        if out.shape[0] > SUMMED:
+            area = jnp.sum(weight[0:2, :], axis=(0, 1), keepdims=True)
+            out[SUMMED:, :] = jnp.broadcast_to(area, (8, 128))
+
+
+def descended(packed, part, back, with_area):
     first = lax.axis_index("grp") == 0
+
+    def whole(mine, theirs):
+        return jnp.concatenate([jnp.where(first, mine, theirs), jnp.where(first, theirs, mine)], 0)
+
     blocks = []
-    for block in range(PACKED // 128):
-        mine, theirs = (ref[half * block : half * (block + 1), :] for ref in (part, back))
-        blocks.append(
-            jnp.concatenate([jnp.where(first, mine, theirs), jnp.where(first, theirs, mine)], 0)
-        )
-    area = blocks[AREA_AT // 128][0:1, AREA_AT % 128 : AREA_AT % 128 + 1]
-    step = (learn_rate * 2.0 / CHANNELS) / area
+    for block in range(4):
+        rows = slice(HALF * block, HALF * (block + 1))
+        blocks.append(whole(part[rows, :], back[rows, :]))
+    rest = [
+        jnp.concatenate([ref[4 * HALF : SUMMED, 32 * at : 32 * (at + 1)] for at in range(4)], 0)
+        for ref in (part, back)
+    ]
+    blocks += [whole(*rest), jnp.zeros((HIDDEN, PACKED - USED), f32)]
+    step = (learn_rate * 2.0 / CHANNELS) / with_area[SUMMED : SUMMED + 1, 0:1]
     return packed[...] - step * jnp.concatenate(blocks, 1)
 
 
 def next_network_kernel(*refs):
     *ins, packed, part, back, renewed = refs[:11]
-    renewed[...] = descended(packed, part, back)
+    renewed[...] = descended(packed, part, back, part)
     network_step(*ins, renewed, *refs[11:])
 
 
-def last_kernel(packed, part, back, kernel, mix, out):
-    renewed = descended(packed, part, back)
+def last_kernel(packed, part, back, with_area, kernel, mix, out):
+    renewed = descended(packed, part, back, with_area)
     kernel[...] = renewed[:, 0:TAPS].T
     mix[...] = renewed[:, MIX_AT : MIX_AT + HIDDEN]
     out[...] = renewed[:, OUT_AT : OUT_AT + CHANNELS].T
@@ -588,10 +599,9 @@
     packed = jnp.concatenate(
         [
             kernel_factors.reshape(HIDDEN, TAPS),
-            jnp.zeros((HIDDEN, MIX_AT - TAPS), f32),
             hidden_pointwise_factors,
             final_pointwise_factors.T,
-            jnp.zeros((HIDDEN, PACKED - AREA_AT), f32),
+            jnp.zeros((HIDDEN, PACKED - USED), f32),
         ],
         1,
     )
@@ -600,9 +610,8 @@
     sums = [pltpu.VMEM((4 * CHANNELS, FINE), f32), pltpu.VMEM((16 * 8 * LEVELS, 128), f32)]
     wide = struct(2 * CHANNELS, COARSE)
     tile = struct(8, 128)
-    half = struct(HIDDEN // 2 * PACKED // 128, 128)
+    with_area, without = struct(SUMMED + 8, 128), struct(SUMMED, 128)
     field = struct(8 * LEVELS, FINE)
-    network_outs = [wide, half, half]
     network_scratch = [pltpu.VMEM((TAPS, 2 * COARSE), bf16)] * 2 + [pltpu.VMEM((HIDDEN, PACKED), f32)]
     side_taps = [pltpu.VMEM((TAPS, 3 * COARSE), bf16)] * 2
 
@@ -625,11 +634,11 @@
     def columns(x, inner, outer, near, far):
         return call(columns_kernel, [struct(16, 128)] * 2, x, inner, outer, near, far)
 
-    inner, outer = swap_lon(inner, outer)
+    (inner, outer), packed = lax.optimization_barrier((swap_lon(inner, outer), packed))
     south, north = south_north(*swap_lat(*columns(x, inner, outer, near, far)))
     pred, own, other = call(
         network_step,
-        network_outs,
+        [wide, with_area, with_area],
         x, inner, outer, south, north, target, weight, packed,
         scratch=network_scratch,
     )
@@ -662,7 +671,7 @@
     t, s, x, target = later["state"]
     packed, pred, own, other = call(
         next_network_kernel,
-        [struct(HIDDEN, PACKED)] + network_outs,
+        [struct(HIDDEN, PACKED), wide, without, without],
         x, *moving, target, weight, packed, part, back,
         scratch=network_scratch,
     )
@@ -677,12 +686,19 @@
         part, *later["fields"] = lax.optimization_barrier((part, *fields_next))
         return part
 
-    part, back, _ = sum_over_devices(own, other, next_advance, lambda: ([], []))
+    first_part = part
+    part = own + lax.ppermute(other, "grp", flipped("grp", 1))
+    part = next_advance(part + from_chip(part, 3))
+    for bit in (8, 32):
+        part = sum_of_four(part, bit)
+    one, two, three = (from_chip(part, mask) for mask in (4, 1, 5))
+    part = (part + one) + (two + three)
+    back = lax.ppermute(part, "grp", flipped("grp", 1))
     t, s = later["fields"]
     kernel, mix, out = call(
         last_kernel,
         [struct(TAPS, HIDDEN), struct(HIDDEN, HIDDEN), struct(CHANNELS, HIDDEN)],
-        packed, part, back,
+        packed, part, back, first_part,
     )
     return (
         t.reshape(thermal_anomaly.shape),

time: 99.3 us -> 97 us (0.977)
  starting transfers between devices: 56.5 us -> 55.1 us
  local copies, waits for them, and re-layouts: 1.67 us -> 0.29 us
    ppermute x2 -> x1, starting transfers between devices: 9.83 us -> 4.19 us  [sum_over_devices(): back = lax.ppermute(part, 'grp', flipped('grp', 1))]
    ppermute x0 -> x2, starting transfers between devices: none -> 4.68 us  [the longest x1 4.26 us: shards(): back = lax.ppermute(part, 'grp', flipped('grp', 1))]
    ppermute x0 -> x2, waiting for transfers between devices: none -> 1.81 us  [the longest x1 0.91 us: shards(): back = lax.ppermute(part, 'grp', flipped('grp', 1))]
    unnamed x11, local copies, waits for them, and re-layouts: 1.45 us -> 0.1 us
    ppermute x1, waiting for transfers between devices: 0.01 us -> 1.04 us  [swap_lat(): lax.ppermute(near, 'lat', flipped('lat', 1))]
    ppermute x2 -> x1, starting transfers between devices: 4.73 us -> 4.88 us  [sum_over_devices(): part = own + lax.ppermute(other, 'grp', flipped('grp', 1))]
  transfers between devices with their start and end apart: 30 -> 30, of which waited for: 17 -> 18; matrix products, arithmetic and copies ran while one was open for 0% -> 0% of each run, Pallas kernels for 8% -> 8%
where the time goes in v5:
time: 97 us; the launch traced here: 96.8 us
  starting transfers between devices  55.1 us (57%)
  waiting for transfers between devices  26.3 us (27%)
  Pallas kernels  14 us (14%)
    ppermute x20, starting transfers between devices, from_chip(): lax.ppermute(value, ('lon', 'lat'), [(i, i ^ mask) for i in range(count)])  26.8 us
    ppermute x20, waiting for transfers between devices, from_chip(): lax.ppermute(value, ('lon', 'lat'), [(i, i ^ mask) for i in range(count)])  18.9 us
    pallas_call x9, Pallas kernels, call(): pl.pallas_call(kernel, out_shape=outs, in_specs=specs, out_specs=[pl.Bloc...  14 us
    ppermute x1, starting transfers between devices, swap_lat(): lax.ppermute(near, 'lat', flipped('lat', 1))  7.76 us
    ppermute x2, starting transfers between devices, swap_lon(): return (lax.ppermute(inner, 'grp', flipped('grp', 1)), outer)  5 us
    ppermute x1, starting transfers between devices, sum_over_devices(): part = own + lax.ppermute(other, 'grp', flipped('grp', 1))  4.88 us
    ppermute x1, starting transfers between devices, shards(): back = lax.ppermute(part, 'grp', flipped('grp', 1))  4.26 us
    ppermute x1, starting transfers between devices, sum_over_devices(): back = lax.ppermute(part, 'grp', flipped('grp', 1))  4.19 us
  transfers between devices with their start and end apart: 30, of which 18 were waited for; matrix products, arithmetic and copies ran while one was open for 0% of the time, Pallas kernels for 8%

profile of v5, /device:TPU:1, one launch (start us, length us, event | category | flops | bytes accessed | tf_op | source)
XLA Modules:
  0.0 96.8 jit_solution(7263208084763979146)
XLA Ops:
  0.7 1.9 %shard_map.119 = (f32[96,128]{1,0:T(8,128)S(1)}, f32[96,128]{1,0:T(8,128)S(1)}, f32[8,128]{1,0:T(8,128)S(1)}, f32[8,512]{1,0:T(8,128)S(1)}, f32[256,128]{1,0:T(8,128)S(1)}, /*index=5*/f32[256,128]{1,0:T(8,128)S(1)}) custom-call(f32[96,512]{1,0:T(8,128)} %bitcast.18, f32[96,512]{1,0:T(8,128)} %bitcast.21, f32[96,512]{1,0:T(8,128)} %bitcast.15, ...), custom_call_target="tpu_custom_call" | custom-call | tf_op jit(solution)/shard_map/pallas_call | solution.py:44
  2.6 3.3 %collective-permute-start = (f32[256,128]{1,0:T(8,128)S(1)}, f32[256,128]{1,0:T(8,128)S(1)}, u32[]{:S(2)}, u32[]{:S(2)}) collective-permute-start(f32[256,128]{1,0:T(8,128)S(1)} %get-tuple-element.48), channel_id=1, source_target_pairs={{0,1},{1,0},{2,3},{3,2},{4,5},{5,4},{6,7},{7,6},{8,9},{9,8},{10,11... | collective-permute-start | bytes 393224 | tf_op jit(solution)/shard_map/ppermute | solution.py:537
  7.7 2.7 %collective-permute-done.1.x_outer.outer.refs_9_ = f32[256,128]{1,0:T(8,128)S(1)} collective-permute-done((f32[256,128]{1,0:T(8,128)S(1)}, f32[256,128]{1,0:T(8,128)S(1)}, u32[]{:S(2)}, u32[]{:S(2)}) %collective-permute-start.1) | collective-permute-done | bytes 131104 | tf_op jit(solution)/shard_map/ppermute | solution.py:536
  11.2 7.8 %collective-permute-start.2 = (f32[16,128]{1,0:T(8,128)S(1)}, f32[16,128]{1,0:T(8,128)S(1)}, u32[]{:S(2)}, u32[]{:S(2)}) collective-permute-start(f32[16,128]{1,0:T(8,128)S(1)} %get-tuple-element.54), channel_id=1, source_target_pairs={{0,2},{2,0},{4,6},{6,4},{1,3},{3,1},{5,7},{7,5},{8,10},{10,8},{12,... | collective-permute-start | bytes 24584 | tf_op jit(solution)/shard_map/ppermute | solution.py:543
  21.5 4.9 %collective-permute-start.4 = (f32[144,128]{1,0:T(8,128)S(1)}, f32[144,128]{1,0:T(8,128)S(1)}, u32[]{:S(2)}, u32[]{:S(2)}) collective-permute-start(f32[144,128]{1,0:T(8,128)S(1)} %get-tuple-element.62), channel_id=1, source_target_pairs={{0,1},{1,0},{2,3},{3,2},{4,5},{5,4},{6,7},{7,6},{8,9},{9,8},{10,11... | collective-permute-start | bytes 221192 | tf_op jit(solution)/shard_map/ppermute | solution.py:572
  27.4 3.8 %shard_map.123 = (f32[96,512]{1,0:T(8,128)S(1)}, f32[96,512]{1,0:T(8,128)S(1)}, f32[96,128]{1,0:T(8,128)S(1)}, f32[96,128]{1,0:T(8,128)S(1)}, f32[192,128]{1,0:T...) custom-call(f32[96,512]{1,0:T(8,128)} %bitcast.20, f32[96,512]{1,0:T(8,128)} %bitcast.23, ...), custom_call_target="tpu_custom_call" | custom-call | tf_op jit(solution)/shard_map/pallas_call | solution.py:44
  32.4 1.6 %collective-permute-start.8 = (f32[144,128]{1,0:T(8,128)S(1)}, f32[144,128]{1,0:T(8,128)S(1)}, u32[]{:S(2)}, u32[]{:S(2)}) collective-permute-start(f32[144,128]{1,0:T(8,128)S(1)} %add.73), channel_id=1, source_target_pairs={{0,16},{2,18},{4,20},{6,22},{8,24},{10,26},{12,28},{14,30},{16,0},... | collective-permute-start | bytes 221192 | tf_op jit(solution)/shard_map/ppermute | solution.py:560
  34.0 1.7 %collective-permute-start.6 = (f32[192,128]{1,0:T(8,128)S(1)}, f32[192,128]{1,0:T(8,128)S(1)}, u32[]{:S(2)}, u32[]{:S(2)}) collective-permute-start(f32[192,128]{1,0:T(8,128)S(1)} %get-tuple-element.65), channel_id=1, source_target_pairs={{0,1},{1,0},{2,3},{3,2},{4,5},{5,4},{6,7},{7,6},{8,9},{9,8},{10,11... | collective-permute-start | bytes 294920 | tf_op jit(solution)/shard_map/ppermute | solution.py:537
  37.4 2.8 %collective-permute-start.12 = (f32[144,128]{1,0:T(8,128)S(1)}, f32[144,128]{1,0:T(8,128)S(1)}, u32[]{:S(2)}, u32[]{:S(2)}) collective-permute-start(f32[144,128]{1,0:T(8,128)S(1)} %add_add_fusion.1), channel_id=1, source_target_pairs={{0,128},{2,130},{4,132},{6,134},{8,136},{10,138},{12,140},{14,142}... | collective-permute-start | bytes 221192 | tf_op jit(solution)/shard_map/ppermute | solution.py:560
  42.2 2.5 %collective-permute-done.13 = f32[144,128]{1,0:T(8,128)S(1)} collective-permute-done((f32[144,128]{1,0:T(8,128)S(1)}, f32[144,128]{1,0:T(8,128)S(1)}, u32[]{:S(2)}, u32[]{:S(2)}) %collective-permute-start.13) | collective-permute-done | bytes 73760 | tf_op jit(solution)/shard_map/ppermute | solution.py:560
  45.8 2.9 %collective-permute-start.14 = (f32[160,128]{1,0:T(8,128)S(1)}, f32[160,128]{1,0:T(8,128)S(1)}, u32[]{:S(2)}, u32[]{:S(2)}) collective-permute-start(f32[160,128]{1,0:T(8,128)S(1)} %get-tuple-element.89), channel_id=1, source_target_pairs={{0,2},{2,0},{4,6},{6,4},{8,10},{10,8},{12,14},{14,12},{16,18},{18,... | collective-permute-start | bytes 245768 | tf_op jit(solution)/shard_map/ppermute | solution.py:560
  48.7 3.0 %collective-permute-start.16 = (f32[144,128]{1,0:T(8,128)S(1)}, f32[144,128]{1,0:T(8,128)S(1)}, u32[]{:S(2)}, u32[]{:S(2)}) collective-permute-start(f32[144,128]{1,0:T(8,128)S(1)} %add_add_fusion), channel_id=1, source_target_pairs={{0,12},{2,14},{4,8},{6,10},{8,4},{10,6},{12,0},{14,2},{16,28},{18,... | collective-permute-start | bytes 221192 | tf_op jit(solution)/shard_map/ppermute | solution.py:560
  51.7 3.6 %collective-permute-done.16 = f32[144,128]{1,0:T(8,128)S(1)} collective-permute-done((f32[144,128]{1,0:T(8,128)S(1)}, f32[144,128]{1,0:T(8,128)S(1)}, u32[]{:S(2)}, u32[]{:S(2)}) %collective-permute-start.16) | collective-permute-done | bytes 73760 | tf_op jit(solution)/shard_map/ppermute | solution.py:560
  55.3 4.2 %collective-permute-start.17 = (f32[144,128]{1,0:T(8,128)S(1)}, f32[144,128]{1,0:T(8,128)S(1)}, u32[]{:S(2)}, u32[]{:S(2)}) collective-permute-start(f32[144,128]{1,0:T(8,128)S(1)} %fusion.refs_8_.with_area), channel_id=1, source_target_pairs={{0,1},{1,0},{2,3},{3,2},{4,5},{5,4},{6,7},{7,6},{8,9},{9,8},{10,11... | collective-permute-start | bytes 221192 | tf_op jit(solution)/shard_map/ppermute | solution.py:581
  60.4 1.6 %shard_map.125 = (f32[64,640]{1,0:T(8,128)S(1)}, f32[96,128]{1,0:T(8,128)S(1)}, f32[136,128]{1,0:T(8,128)S(1)}, f32[136,128]{1,0:T(8,128)S(1)}) custom-call(f32[96,128]{1,0:T(8,128)S(1)} %get-tuple-element.60.x.refs_0_.refs_5_, f32[192,128]{1,0:T(8,128)S(1)} %collective-permute-done.6.x_inner.refs_1_.refs_12_, ...), custom_call_target="tpu_custom_call" | custom-call | tf_op jit(solution)/shard_map/pallas_call | solution.py:44
  63.3 3.0 %collective-permute-start.19 = (f32[136,128]{1,0:T(8,128)S(1)}, f32[136,128]{1,0:T(8,128)S(1)}, u32[]{:S(2)}, u32[]{:S(2)}) collective-permute-start(f32[136,128]{1,0:T(8,128)S(1)} %add.83), channel_id=1, source_target_pairs={{0,6},{2,4},{4,2},{6,0},{8,14},{10,12},{12,10},{14,8},{16,22},{18,... | collective-permute-start | bytes 208904 | tf_op jit(solution)/shard_map/ppermute | solution.py:560
  66.3 2.6 %shard_map.126 = (f32[96,512]{1,0:T(8,128)}, f32[96,512]{1,0:T(8,128)}) custom-call(f32[96,512]{1,0:T(8,128)S(1)} %get-tuple-element.75.refs_0_, f32[96,512]{1,0:T(8,128)S(1)} %get-tuple-element.76.refs_1_, f32[96,512]{1,0:T(8,128)S(1)} %bitcast.17, f32[96,512]{1,0:T(8,128)S(1)} %bitcast.14, f32[8,512]{1,0:T(8,128)S(1)} %get-tuple-element.46.mask.refs_4_, ...), custom_call_target="tpu_custom_call" | custom-call | tf_op jit(solution)/shard_map/pallas_call | solution.py:44
  70.4 2.1 %collective-permute-start.22 = (f32[136,128]{1,0:T(8,128)S(1)}, f32[136,128]{1,0:T(8,128)S(1)}, u32[]{:S(2)}, u32[]{:S(2)}) collective-permute-start(f32[136,128]{1,0:T(8,128)S(1)} %add.84), channel_id=1, source_target_pairs={{0,48},{2,50},{4,52},{6,54},{8,56},{10,58},{12,60},{14,62},{16,32}... | collective-permute-start | bytes 208904 | tf_op jit(solution)/shard_map/ppermute | solution.py:560
  73.7 2.0 %collective-permute-done.22 = f32[136,128]{1,0:T(8,128)S(1)} collective-permute-done((f32[136,128]{1,0:T(8,128)S(1)}, f32[136,128]{1,0:T(8,128)S(1)}, u32[]{:S(2)}, u32[]{:S(2)}) %collective-permute-start.22) | collective-permute-done | bytes 69664 | tf_op jit(solution)/shard_map/ppermute | solution.py:560
  76.0 1.9 %collective-permute-start.24 = (f32[136,128]{1,0:T(8,128)S(1)}, f32[136,128]{1,0:T(8,128)S(1)}, u32[]{:S(2)}, u32[]{:S(2)}) collective-permute-start(f32[136,128]{1,0:T(8,128)S(1)} %add_add_fusion.4), channel_id=1, source_target_pairs={{0,128},{2,130},{4,132},{6,134},{8,136},{10,138},{12,140},{14,142}... | collective-permute-start | bytes 208904 | tf_op jit(solution)/shard_map/ppermute | solution.py:560
  78.7 2.0 %collective-permute-done.24 = f32[136,128]{1,0:T(8,128)S(1)} collective-permute-done((f32[136,128]{1,0:T(8,128)S(1)}, f32[136,128]{1,0:T(8,128)S(1)}, u32[]{:S(2)}, u32[]{:S(2)}) %collective-permute-start.24) | collective-permute-done | bytes 69664 | tf_op jit(solution)/shard_map/ppermute | solution.py:560
  82.4 4.4 %collective-permute-start.28 = (f32[136,128]{1,0:T(8,128)S(1)}, f32[136,128]{1,0:T(8,128)S(1)}, u32[]{:S(2)}, u32[]{:S(2)}) collective-permute-start(f32[136,128]{1,0:T(8,128)S(1)} %add_add_fusion.3), channel_id=1, source_target_pairs={{0,10},{2,8},{4,14},{6,12},{8,2},{10,0},{12,6},{14,4},{16,26},{18,... | collective-permute-start | bytes 208904 | tf_op jit(solution)/shard_map/ppermute | solution.py:560
  86.8 2.4 %collective-permute-done.28 = f32[136,128]{1,0:T(8,128)S(1)} collective-permute-done((f32[136,128]{1,0:T(8,128)S(1)}, f32[136,128]{1,0:T(8,128)S(1)}, u32[]{:S(2)}, u32[]{:S(2)}) %collective-permute-start.28) | collective-permute-done | bytes 69664 | tf_op jit(solution)/shard_map/ppermute | solution.py:560
  90.7 4.3 %collective-permute-start.29 = (f32[136,128]{1,0:T(8,128)S(1)}, f32[136,128]{1,0:T(8,128)S(1)}, u32[]{:S(2)}, u32[]{:S(2)}) collective-permute-start(f32[136,128]{1,0:T(8,128)S(1)} %add_add_fusion.2.part), channel_id=1, source_target_pairs={{0,1},{1,0},{2,3},{3,2},{4,5},{5,4},{6,7},{7,6},{8,9},{9,8},{10,11... | collective-permute-start | bytes 208904 | tf_op jit(solution)/shard_map/ppermute | solution.py:696
  (73 shorter events, 23.1 us)
Async XLA Ops:
  2.6 5.1 %collective-permute-start = (f32[256,128]{1,0:T(8,128)S(1)}, f32[256,128]{1,0:T(8,128)S(1)}, u32[]{:S(2)}, u32[]{:S(2)}) collective-permute-start(f32[256,128]{1,0:T(8,128)S(1)} %get-tuple-element.48), channel_id=1, source_target_pairs={{0,1},{1,0},{2,3},{3,2},{4,5},{5,4},{6,7},{7,6},{8,9},{9,8},{10,11... | collective-permute-start | bytes 393224 | tf_op jit(solution)/shard_map/ppermute | solution.py:537
  5.9 4.5 %collective-permute-start.1 = (f32[256,128]{1,0:T(8,128)S(1)}, f32[256,128]{1,0:T(8,128)S(1)}, u32[]{:S(2)}, u32[]{:S(2)}) collective-permute-start(f32[256,128]{1,0:T(8,128)S(1)} %get-tuple-element.49), channel_id=1, source_target_pairs={{0,249},{1,8},{8,1},{9,16},{16,9},{17,24},{24,17},{25,32},{32,25},... | collective-permute-start | bytes 393224 | tf_op jit(solution)/shard_map/ppermute | solution.py:536
  10.5 8.4 %collective-permute-start.3 = (f32[16,128]{1,0:T(8,128)S(1)}, f32[16,128]{1,0:T(8,128)S(1)}, u32[]{:S(2)}, u32[]{:S(2)}) collective-permute-start(f32[16,128]{1,0:T(8,128)S(1)} %get-tuple-element.55), channel_id=1, source_target_pairs={{2,4},{4,2},{3,5},{5,3},{10,12},{12,10},{11,13},{13,11},{18,20},{2... | collective-permute-start | bytes 24584 | tf_op jit(solution)/shard_map/ppermute | solution.py:543
  11.2 8.8 %collective-permute-start.2 = (f32[16,128]{1,0:T(8,128)S(1)}, f32[16,128]{1,0:T(8,128)S(1)}, u32[]{:S(2)}, u32[]{:S(2)}) collective-permute-start(f32[16,128]{1,0:T(8,128)S(1)} %get-tuple-element.54), channel_id=1, source_target_pairs={{0,2},{2,0},{4,6},{6,4},{1,3},{3,1},{5,7},{7,5},{8,10},{10,8},{12,... | collective-permute-start | bytes 24584 | tf_op jit(solution)/shard_map/ppermute | solution.py:543
  21.5 5.8 %collective-permute-start.4 = (f32[144,128]{1,0:T(8,128)S(1)}, f32[144,128]{1,0:T(8,128)S(1)}, u32[]{:S(2)}, u32[]{:S(2)}) collective-permute-start(f32[144,128]{1,0:T(8,128)S(1)} %get-tuple-element.62), channel_id=1, source_target_pairs={{0,1},{1,0},{2,3},{3,2},{4,5},{5,4},{6,7},{7,6},{8,9},{9,8},{10,11... | collective-permute-start | bytes 221192 | tf_op jit(solution)/shard_map/ppermute | solution.py:572
  31.3 5.5 %collective-permute-start.9 = (f32[144,128]{1,0:T(8,128)S(1)}, f32[144,128]{1,0:T(8,128)S(1)}, u32[]{:S(2)}, u32[]{:S(2)}) collective-permute-start(f32[144,128]{1,0:T(8,128)S(1)} %add.73), channel_id=1, source_target_pairs={{0,32},{2,34},{4,36},{6,38},{8,40},{10,42},{12,44},{14,46},{16,48}... | collective-permute-start | bytes 221192 | tf_op jit(solution)/shard_map/ppermute | solution.py:560
  31.6 5.8 %collective-permute-start.10 = (f32[144,128]{1,0:T(8,128)S(1)}, f32[144,128]{1,0:T(8,128)S(1)}, u32[]{:S(2)}, u32[]{:S(2)}) collective-permute-start(f32[144,128]{1,0:T(8,128)S(1)} %add.73), channel_id=1, source_target_pairs={{0,48},{2,50},{4,52},{6,54},{8,56},{10,58},{12,60},{14,62},{16,32}... | collective-permute-start | bytes 221192 | tf_op jit(solution)/shard_map/ppermute | solution.py:560
  32.4 4.9 %collective-permute-start.8 = (f32[144,128]{1,0:T(8,128)S(1)}, f32[144,128]{1,0:T(8,128)S(1)}, u32[]{:S(2)}, u32[]{:S(2)}) collective-permute-start(f32[144,128]{1,0:T(8,128)S(1)} %add.73), channel_id=1, source_target_pairs={{0,16},{2,18},{4,20},{6,22},{8,24},{10,26},{12,28},{14,30},{16,0},... | collective-permute-start | bytes 221192 | tf_op jit(solution)/shard_map/ppermute | solution.py:560
  34.0 7.1 %collective-permute-start.6 = (f32[192,128]{1,0:T(8,128)S(1)}, f32[192,128]{1,0:T(8,128)S(1)}, u32[]{:S(2)}, u32[]{:S(2)}) collective-permute-start(f32[192,128]{1,0:T(8,128)S(1)} %get-tuple-element.65), channel_id=1, source_target_pairs={{0,1},{1,0},{2,3},{3,2},{4,5},{5,4},{6,7},{7,6},{8,9},{9,8},{10,11... | collective-permute-start | bytes 294920 | tf_op jit(solution)/shard_map/ppermute | solution.py:537
  35.7 5.4 %collective-permute-start.7 = (f32[192,128]{1,0:T(8,128)S(1)}, f32[192,128]{1,0:T(8,128)S(1)}, u32[]{:S(2)}, u32[]{:S(2)}) collective-permute-start(f32[192,128]{1,0:T(8,128)S(1)} %get-tuple-element.66), channel_id=1, source_target_pairs={{0,249},{1,8},{8,1},{9,16},{16,9},{17,24},{24,17},{25,32},{32,25},... | collective-permute-start | bytes 294920 | tf_op jit(solution)/shard_map/ppermute | solution.py:536
  37.4 4.8 %collective-permute-start.12 = (f32[144,128]{1,0:T(8,128)S(1)}, f32[144,128]{1,0:T(8,128)S(1)}, u32[]{:S(2)}, u32[]{:S(2)}) collective-permute-start(f32[144,128]{1,0:T(8,128)S(1)} %add_add_fusion.1), channel_id=1, source_target_pairs={{0,128},{2,130},{4,132},{6,134},{8,136},{10,138},{12,140},{14,142}... | collective-permute-start | bytes 221192 | tf_op jit(solution)/shard_map/ppermute | solution.py:560
  40.2 4.4 %collective-permute-start.13 = (f32[144,128]{1,0:T(8,128)S(1)}, f32[144,128]{1,0:T(8,128)S(1)}, u32[]{:S(2)}, u32[]{:S(2)}) collective-permute-start(f32[144,128]{1,0:T(8,128)S(1)} %add_add_fusion.1), channel_id=1, source_target_pairs={{0,192},{2,194},{4,196},{6,198},{8,200},{10,202},{12,204},{14,206}... | collective-permute-start | bytes 221192 | tf_op jit(solution)/shard_map/ppermute | solution.py:560
  45.2 10.1 %collective-permute-start.15 = (f32[160,128]{1,0:T(8,128)S(1)}, f32[160,128]{1,0:T(8,128)S(1)}, u32[]{:S(2)}, u32[]{:S(2)}) collective-permute-start(f32[160,128]{1,0:T(8,128)S(1)} %get-tuple-element.90), channel_id=1, source_target_pairs={{0,6},{2,4},{4,2},{6,0},{8,14},{10,12},{12,10},{14,8},{16,22},{18,... | collective-permute-start | bytes 245768 | tf_op jit(solution)/shard_map/ppermute | solution.py:560
  45.8 9.5 %collective-permute-start.14 = (f32[160,128]{1,0:T(8,128)S(1)}, f32[160,128]{1,0:T(8,128)S(1)}, u32[]{:S(2)}, u32[]{:S(2)}) collective-permute-start(f32[160,128]{1,0:T(8,128)S(1)} %get-tuple-element.89), channel_id=1, source_target_pairs={{0,2},{2,0},{4,6},{6,4},{8,10},{10,8},{12,14},{14,12},{16,18},{18,... | collective-permute-start | bytes 245768 | tf_op jit(solution)/shard_map/ppermute | solution.py:560
  48.7 6.5 %collective-permute-start.16 = (f32[144,128]{1,0:T(8,128)S(1)}, f32[144,128]{1,0:T(8,128)S(1)}, u32[]{:S(2)}, u32[]{:S(2)}) collective-permute-start(f32[144,128]{1,0:T(8,128)S(1)} %add_add_fusion), channel_id=1, source_target_pairs={{0,12},{2,14},{4,8},{6,10},{8,4},{10,6},{12,0},{14,2},{16,28},{18,... | collective-permute-start | bytes 221192 | tf_op jit(solution)/shard_map/ppermute | solution.py:560
  55.3 5.1 %collective-permute-start.17 = (f32[144,128]{1,0:T(8,128)S(1)}, f32[144,128]{1,0:T(8,128)S(1)}, u32[]{:S(2)}, u32[]{:S(2)}) collective-permute-start(f32[144,128]{1,0:T(8,128)S(1)} %fusion.refs_8_.with_area), channel_id=1, source_target_pairs={{0,1},{1,0},{2,3},{3,2},{4,5},{5,4},{6,7},{7,6},{8,9},{9,8},{10,11... | collective-permute-start | bytes 221192 | tf_op jit(solution)/shard_map/ppermute | solution.py:581
  63.3 5.7 %collective-permute-start.19 = (f32[136,128]{1,0:T(8,128)S(1)}, f32[136,128]{1,0:T(8,128)S(1)}, u32[]{:S(2)}, u32[]{:S(2)}) collective-permute-start(f32[136,128]{1,0:T(8,128)S(1)} %add.83), channel_id=1, source_target_pairs={{0,6},{2,4},{4,2},{6,0},{8,14},{10,12},{12,10},{14,8},{16,22},{18,... | collective-permute-start | bytes 208904 | tf_op jit(solution)/shard_map/ppermute | solution.py:560
  69.0 4.8 %collective-permute-start.21 = (f32[136,128]{1,0:T(8,128)S(1)}, f32[136,128]{1,0:T(8,128)S(1)}, u32[]{:S(2)}, u32[]{:S(2)}) collective-permute-start(f32[136,128]{1,0:T(8,128)S(1)} %add.84), channel_id=1, source_target_pairs={{0,32},{2,34},{4,36},{6,38},{8,40},{10,42},{12,44},{14,46},{16,48}... | collective-permute-start | bytes 208904 | tf_op jit(solution)/shard_map/ppermute | solution.py:560
  70.4 5.3 %collective-permute-start.22 = (f32[136,128]{1,0:T(8,128)S(1)}, f32[136,128]{1,0:T(8,128)S(1)}, u32[]{:S(2)}, u32[]{:S(2)}) collective-permute-start(f32[136,128]{1,0:T(8,128)S(1)} %add.84), channel_id=1, source_target_pairs={{0,48},{2,50},{4,52},{6,54},{8,56},{10,58},{12,60},{14,62},{16,32}... | collective-permute-start | bytes 208904 | tf_op jit(solution)/shard_map/ppermute | solution.py:560
  76.0 4.8 %collective-permute-start.24 = (f32[136,128]{1,0:T(8,128)S(1)}, f32[136,128]{1,0:T(8,128)S(1)}, u32[]{:S(2)}, u32[]{:S(2)}) collective-permute-start(f32[136,128]{1,0:T(8,128)S(1)} %add_add_fusion.4), channel_id=1, source_target_pairs={{0,128},{2,130},{4,132},{6,134},{8,136},{10,138},{12,140},{14,142}... | collective-permute-start | bytes 208904 | tf_op jit(solution)/shard_map/ppermute | solution.py:560
  77.9 4.4 %collective-permute-start.25 = (f32[136,128]{1,0:T(8,128)S(1)}, f32[136,128]{1,0:T(8,128)S(1)}, u32[]{:S(2)}, u32[]{:S(2)}) collective-permute-start(f32[136,128]{1,0:T(8,128)S(1)} %add_add_fusion.4), channel_id=1, source_target_pairs={{0,192},{2,194},{4,196},{6,198},{8,200},{10,202},{12,204},{14,206}... | collective-permute-start | bytes 208904 | tf_op jit(solution)/shard_map/ppermute | solution.py:560
  82.3 4.5 %collective-permute-start.27 = (f32[136,128]{1,0:T(8,128)S(1)}, f32[136,128]{1,0:T(8,128)S(1)}, u32[]{:S(2)}, u32[]{:S(2)}) collective-permute-start(f32[136,128]{1,0:T(8,128)S(1)} %add_add_fusion.3), channel_id=1, source_target_pairs={{0,2},{2,0},{4,6},{6,4},{8,10},{10,8},{12,14},{14,12},{16,18},{18,... | collective-permute-start | bytes 208904 | tf_op jit(solution)/shard_map/ppermute | solution.py:560
  82.4 6.8 %collective-permute-start.28 = (f32[136,128]{1,0:T(8,128)S(1)}, f32[136,128]{1,0:T(8,128)S(1)}, u32[]{:S(2)}, u32[]{:S(2)}) collective-permute-start(f32[136,128]{1,0:T(8,128)S(1)} %add_add_fusion.3), channel_id=1, source_target_pairs={{0,10},{2,8},{4,14},{6,12},{8,2},{10,0},{12,6},{14,4},{16,26},{18,... | collective-permute-start | bytes 208904 | tf_op jit(solution)/shard_map/ppermute | solution.py:560
  90.7 5.2 %collective-permute-start.29 = (f32[136,128]{1,0:T(8,128)S(1)}, f32[136,128]{1,0:T(8,128)S(1)}, u32[]{:S(2)}, u32[]{:S(2)}) collective-permute-start(f32[136,128]{1,0:T(8,128)S(1)} %add_add_fusion.2.part), channel_id=1, source_target_pairs={{0,1},{1,0},{2,3},{3,2},{4,5},{5,4},{6,7},{7,6},{8,9},{9,8},{10,11... | collective-permute-start | bytes 208904 | tf_op jit(solution)/shard_map/ppermute | solution.py:696
  (11 other events, 42.9 us)

commit v6 on v5

--- a/solution.py
+++ b/solution.py
@@ -688,11 +688,11 @@
 
     first_part = part
     part = own + lax.ppermute(other, "grp", flipped("grp", 1))
-    part = next_advance(part + from_chip(part, 3))
-    for bit in (8, 32):
-        part = sum_of_four(part, bit)
+    part = sum_of_four(part, 32)
+    part = next_advance(sum_of_four(part, 8))
     one, two, three = (from_chip(part, mask) for mask in (4, 1, 5))
     part = (part + one) + (two + three)
+    part = part + from_chip(part, 3)
     back = lax.ppermute(part, "grp", flipped("grp", 1))
     t, s = later["fields"]
     kernel, mix, out = call(

time: 97 us -> 96 us (0.990)
  no operation moved by 1% of the time
where the time goes in v6:
time: 96 us; the launch traced here: 95.8 us
  starting transfers between devices  54.5 us (57%)
  waiting for transfers between devices  25.9 us (27%)
  Pallas kernels  14 us (15%)
    ppermute x20, starting transfers between devices, from_chip(): lax.ppermute(value, ('lon', 'lat'), [(i, i ^ mask) for i in range(count)])  26.1 us
    ppermute x20, waiting for transfers between devices, from_chip(): lax.ppermute(value, ('lon', 'lat'), [(i, i ^ mask) for i in range(count)])  18.5 us
    pallas_call x9, Pallas kernels, call(): pl.pallas_call(kernel, out_shape=outs, in_specs=specs, out_specs=[pl.Bloc...  14 us
    ppermute x1, starting transfers between devices, swap_lat(): lax.ppermute(near, 'lat', flipped('lat', 1))  7.76 us
    ppermute x2, starting transfers between devices, swap_lon(): return (lax.ppermute(inner, 'grp', flipped('grp', 1)), outer)  5 us
    ppermute x1, starting transfers between devices, sum_over_devices(): part = own + lax.ppermute(other, 'grp', flipped('grp', 1))  4.88 us
    ppermute x1, starting transfers between devices, shards(): back = lax.ppermute(part, 'grp', flipped('grp', 1))  4.29 us
    ppermute x1, starting transfers between devices, sum_over_devices(): back = lax.ppermute(part, 'grp', flipped('grp', 1))  4.26 us
  transfers between devices with their start and end apart: 30, of which 18 were waited for; matrix products, arithmetic and copies ran while one was open for 0% of the time, Pallas kernels for 8%

profile of v6, /device:TPU:1, one launch (start us, length us, event | category | flops | bytes accessed | tf_op | source)
XLA Modules:
  0.0 95.8 jit_solution(11678360380595758973)
XLA Ops:
  0.7 1.9 %shard_map.119 = (f32[96,128]{1,0:T(8,128)S(1)}, f32[96,128]{1,0:T(8,128)S(1)}, f32[8,128]{1,0:T(8,128)S(1)}, f32[8,512]{1,0:T(8,128)S(1)}, f32[256,128]{1,0:T(8,128)S(1)}, /*index=5*/f32[256,128]{1,0:T(8,128)S(1)}) custom-call(f32[96,512]{1,0:T(8,128)} %bitcast.18, f32[96,512]{1,0:T(8,128)} %bitcast.21, f32[96,512]{1,0:T(8,128)} %bitcast.15, ...), custom_call_target="tpu_custom_call" | custom-call | tf_op jit(solution)/shard_map/pallas_call | solution.py:44
  2.6 3.3 %collective-permute-start = (f32[256,128]{1,0:T(8,128)S(1)}, f32[256,128]{1,0:T(8,128)S(1)}, u32[]{:S(2)}, u32[]{:S(2)}) collective-permute-start(f32[256,128]{1,0:T(8,128)S(1)} %get-tuple-element.48), channel_id=1, source_target_pairs={{0,1},{1,0},{2,3},{3,2},{4,5},{5,4},{6,7},{7,6},{8,9},{9,8},{10,11... | collective-permute-start | bytes 393224 | tf_op jit(solution)/shard_map/ppermute | solution.py:537
  7.7 2.7 %collective-permute-done.1.x_outer.outer.refs_9_ = f32[256,128]{1,0:T(8,128)S(1)} collective-permute-done((f32[256,128]{1,0:T(8,128)S(1)}, f32[256,128]{1,0:T(8,128)S(1)}, u32[]{:S(2)}, u32[]{:S(2)}) %collective-permute-start.1) | collective-permute-done | bytes 131104 | tf_op jit(solution)/shard_map/ppermute | solution.py:536
  11.2 7.8 %collective-permute-start.2 = (f32[16,128]{1,0:T(8,128)S(1)}, f32[16,128]{1,0:T(8,128)S(1)}, u32[]{:S(2)}, u32[]{:S(2)}) collective-permute-start(f32[16,128]{1,0:T(8,128)S(1)} %get-tuple-element.54), channel_id=1, source_target_pairs={{0,2},{2,0},{4,6},{6,4},{1,3},{3,1},{5,7},{7,5},{8,10},{10,8},{12,... | collective-permute-start | bytes 24584 | tf_op jit(solution)/shard_map/ppermute | solution.py:543
  21.5 4.9 %collective-permute-start.4 = (f32[144,128]{1,0:T(8,128)S(1)}, f32[144,128]{1,0:T(8,128)S(1)}, u32[]{:S(2)}, u32[]{:S(2)}) collective-permute-start(f32[144,128]{1,0:T(8,128)S(1)} %get-tuple-element.62), channel_id=1, source_target_pairs={{0,1},{1,0},{2,3},{3,2},{4,5},{5,4},{6,7},{7,6},{8,9},{9,8},{10,11... | collective-permute-start | bytes 221192 | tf_op jit(solution)/shard_map/ppermute | solution.py:572
  27.4 3.8 %shard_map.123 = (f32[96,512]{1,0:T(8,128)S(1)}, f32[96,512]{1,0:T(8,128)S(1)}, f32[96,128]{1,0:T(8,128)S(1)}, f32[96,128]{1,0:T(8,128)S(1)}, f32[192,128]{1,0:T...) custom-call(f32[96,512]{1,0:T(8,128)} %bitcast.20, f32[96,512]{1,0:T(8,128)} %bitcast.23, ...), custom_call_target="tpu_custom_call" | custom-call | tf_op jit(solution)/shard_map/pallas_call | solution.py:44
  32.4 1.6 %collective-permute-start.8 = (f32[144,128]{1,0:T(8,128)S(1)}, f32[144,128]{1,0:T(8,128)S(1)}, u32[]{:S(2)}, u32[]{:S(2)}) collective-permute-start(f32[144,128]{1,0:T(8,128)S(1)} %add.73), channel_id=1, source_target_pairs={{0,16},{2,18},{4,20},{6,22},{8,24},{10,26},{12,28},{14,30},{16,0},... | collective-permute-start | bytes 221192 | tf_op jit(solution)/shard_map/ppermute | solution.py:560
  34.0 1.7 %collective-permute-start.6 = (f32[192,128]{1,0:T(8,128)S(1)}, f32[192,128]{1,0:T(8,128)S(1)}, u32[]{:S(2)}, u32[]{:S(2)}) collective-permute-start(f32[192,128]{1,0:T(8,128)S(1)} %get-tuple-element.65), channel_id=1, source_target_pairs={{0,1},{1,0},{2,3},{3,2},{4,5},{5,4},{6,7},{7,6},{8,9},{9,8},{10,11... | collective-permute-start | bytes 294920 | tf_op jit(solution)/shard_map/ppermute | solution.py:537
  37.3 2.8 %collective-permute-start.12 = (f32[144,128]{1,0:T(8,128)S(1)}, f32[144,128]{1,0:T(8,128)S(1)}, u32[]{:S(2)}, u32[]{:S(2)}) collective-permute-start(f32[144,128]{1,0:T(8,128)S(1)} %add_add_fusion.1), channel_id=1, source_target_pairs={{0,128},{2,130},{4,132},{6,134},{8,136},{10,138},{12,140},{14,142}... | collective-permute-start | bytes 221192 | tf_op jit(solution)/shard_map/ppermute | solution.py:560
  42.1 2.5 %collective-permute-done.13 = f32[144,128]{1,0:T(8,128)S(1)} collective-permute-done((f32[144,128]{1,0:T(8,128)S(1)}, f32[144,128]{1,0:T(8,128)S(1)}, u32[]{:S(2)}, u32[]{:S(2)}) %collective-permute-start.13) | collective-permute-done | bytes 73760 | tf_op jit(solution)/shard_map/ppermute | solution.py:560
  45.9 2.9 %collective-permute-start.14 = (f32[160,128]{1,0:T(8,128)S(1)}, f32[160,128]{1,0:T(8,128)S(1)}, u32[]{:S(2)}, u32[]{:S(2)}) collective-permute-start(f32[160,128]{1,0:T(8,128)S(1)} %get-tuple-element.89), channel_id=1, source_target_pairs={{0,2},{2,0},{4,6},{6,4},{8,10},{10,8},{12,14},{14,12},{16,18},{18,... | collective-permute-start | bytes 245768 | tf_op jit(solution)/shard_map/ppermute | solution.py:560
  48.8 2.9 %collective-permute-start.16 = (f32[144,128]{1,0:T(8,128)S(1)}, f32[144,128]{1,0:T(8,128)S(1)}, u32[]{:S(2)}, u32[]{:S(2)}) collective-permute-start(f32[144,128]{1,0:T(8,128)S(1)} %add_add_fusion), channel_id=1, source_target_pairs={{0,12},{2,14},{4,8},{6,10},{8,4},{10,6},{12,0},{14,2},{16,28},{18,... | collective-permute-start | bytes 221192 | tf_op jit(solution)/shard_map/ppermute | solution.py:560
  51.7 3.5 %collective-permute-done.16 = f32[144,128]{1,0:T(8,128)S(1)} collective-permute-done((f32[144,128]{1,0:T(8,128)S(1)}, f32[144,128]{1,0:T(8,128)S(1)}, u32[]{:S(2)}, u32[]{:S(2)}) %collective-permute-start.16) | collective-permute-done | bytes 73760 | tf_op jit(solution)/shard_map/ppermute | solution.py:560
  55.2 4.3 %collective-permute-start.17 = (f32[144,128]{1,0:T(8,128)S(1)}, f32[144,128]{1,0:T(8,128)S(1)}, u32[]{:S(2)}, u32[]{:S(2)}) collective-permute-start(f32[144,128]{1,0:T(8,128)S(1)} %fusion.refs_8_.with_area), channel_id=1, source_target_pairs={{0,1},{1,0},{2,3},{3,2},{4,5},{5,4},{6,7},{7,6},{8,9},{9,8},{10,11... | collective-permute-start | bytes 221192 | tf_op jit(solution)/shard_map/ppermute | solution.py:581
  63.3 1.8 %collective-permute-start.20 = (f32[136,128]{1,0:T(8,128)S(1)}, f32[136,128]{1,0:T(8,128)S(1)}, u32[]{:S(2)}, u32[]{:S(2)}) collective-permute-start(f32[136,128]{1,0:T(8,128)S(1)} %add.83), channel_id=1, source_target_pairs={{0,128},{2,130},{4,132},{6,134},{8,136},{10,138},{12,140},{14,142}... | collective-permute-start | bytes 208904 | tf_op jit(solution)/shard_map/ppermute | solution.py:560
  66.2 1.9 %collective-permute-done.20 = f32[136,128]{1,0:T(8,128)S(1)} collective-permute-done((f32[136,128]{1,0:T(8,128)S(1)}, f32[136,128]{1,0:T(8,128)S(1)}, u32[]{:S(2)}, u32[]{:S(2)}) %collective-permute-start.20) | collective-permute-done | bytes 69664 | tf_op jit(solution)/shard_map/ppermute | solution.py:560
  69.6 2.0 %collective-permute-start.23 = (f32[136,128]{1,0:T(8,128)S(1)}, f32[136,128]{1,0:T(8,128)S(1)}, u32[]{:S(2)}, u32[]{:S(2)}) collective-permute-start(f32[136,128]{1,0:T(8,128)S(1)} %add_add_fusion.4), channel_id=1, source_target_pairs={{0,32},{2,34},{4,36},{6,38},{8,40},{10,42},{12,44},{14,46},{16,48}... | collective-permute-start | bytes 208904 | tf_op jit(solution)/shard_map/ppermute | solution.py:560
  71.6 2.5 %collective-permute-start.24 = (f32[136,128]{1,0:T(8,128)S(1)}, f32[136,128]{1,0:T(8,128)S(1)}, u32[]{:S(2)}, u32[]{:S(2)}) collective-permute-start(f32[136,128]{1,0:T(8,128)S(1)} %add_add_fusion.4), channel_id=1, source_target_pairs={{0,48},{2,50},{4,52},{6,54},{8,56},{10,58},{12,60},{14,62},{16,32}... | collective-permute-start | bytes 208904 | tf_op jit(solution)/shard_map/ppermute | solution.py:560
  74.1 2.6 %shard_map.126 = (f32[96,512]{1,0:T(8,128)}, f32[96,512]{1,0:T(8,128)}) custom-call(f32[96,512]{1,0:T(8,128)S(1)} %get-tuple-element.75.refs_0_, f32[96,512]{1,0:T(8,128)S(1)} %get-tuple-element.76.refs_1_, f32[96,512]{1,0:T(8,128)S(1)} %bitcast.17, f32[96,512]{1,0:T(8,128)S(1)} %bitcast.14, f32[8,512]{1,0:T(8,128)S(1)} %get-tuple-element.46.mask.refs_4_, ...), custom_call_target="tpu_custom_call" | custom-call | tf_op jit(solution)/shard_map/pallas_call | solution.py:44
  77.4 2.7 %collective-permute-start.27 = (f32[136,128]{1,0:T(8,128)S(1)}, f32[136,128]{1,0:T(8,128)S(1)}, u32[]{:S(2)}, u32[]{:S(2)}) collective-permute-start(f32[136,128]{1,0:T(8,128)S(1)} %add_add_fusion.3), channel_id=1, source_target_pairs={{0,10},{2,8},{4,14},{6,12},{8,2},{10,0},{12,6},{14,4},{16,26},{18,... | collective-permute-start | bytes 208904 | tf_op jit(solution)/shard_map/ppermute | solution.py:560
  80.2 2.8 %collective-permute-done.26 = f32[136,128]{1,0:T(8,128)S(1)} collective-permute-done((f32[136,128]{1,0:T(8,128)S(1)}, f32[136,128]{1,0:T(8,128)S(1)}, u32[]{:S(2)}, u32[]{:S(2)}) %collective-permute-start.26) | collective-permute-done | bytes 69664 | tf_op jit(solution)/shard_map/ppermute | solution.py:560
  84.2 2.9 %collective-permute-start.28 = (f32[136,128]{1,0:T(8,128)S(1)}, f32[136,128]{1,0:T(8,128)S(1)}, u32[]{:S(2)}, u32[]{:S(2)}) collective-permute-start(f32[136,128]{1,0:T(8,128)S(1)} %add_add_fusion.2), channel_id=1, source_target_pairs={{0,6},{2,4},{4,2},{6,0},{8,14},{10,12},{12,10},{14,8},{16,22},{18,... | collective-permute-start | bytes 208904 | tf_op jit(solution)/shard_map/ppermute | solution.py:560
  87.0 2.7 %collective-permute-done.28 = f32[136,128]{1,0:T(8,128)S(1)} collective-permute-done((f32[136,128]{1,0:T(8,128)S(1)}, f32[136,128]{1,0:T(8,128)S(1)}, u32[]{:S(2)}, u32[]{:S(2)}) %collective-permute-start.28) | collective-permute-done | bytes 69664 | tf_op jit(solution)/shard_map/ppermute | solution.py:560
  89.7 4.3 %collective-permute-start.29 = (f32[136,128]{1,0:T(8,128)S(1)}, f32[136,128]{1,0:T(8,128)S(1)}, u32[]{:S(2)}, u32[]{:S(2)}) collective-permute-start(f32[136,128]{1,0:T(8,128)S(1)} %add.93.part), channel_id=1, source_target_pairs={{0,1},{1,0},{2,3},{3,2},{4,5},{5,4},{6,7},{7,6},{8,9},{9,8},{10,11... | collective-permute-start | bytes 208904 | tf_op jit(solution)/shard_map/ppermute | solution.py:696
  (73 shorter events, 22.2 us)
Async XLA Ops:
  2.6 5.1 %collective-permute-start = (f32[256,128]{1,0:T(8,128)S(1)}, f32[256,128]{1,0:T(8,128)S(1)}, u32[]{:S(2)}, u32[]{:S(2)}) collective-permute-start(f32[256,128]{1,0:T(8,128)S(1)} %get-tuple-element.48), channel_id=1, source_target_pairs={{0,1},{1,0},{2,3},{3,2},{4,5},{5,4},{6,7},{7,6},{8,9},{9,8},{10,11... | collective-permute-start | bytes 393224 | tf_op jit(solution)/shard_map/ppermute | solution.py:537
  5.9 4.5 %collective-permute-start.1 = (f32[256,128]{1,0:T(8,128)S(1)}, f32[256,128]{1,0:T(8,128)S(1)}, u32[]{:S(2)}, u32[]{:S(2)}) collective-permute-start(f32[256,128]{1,0:T(8,128)S(1)} %get-tuple-element.49), channel_id=1, source_target_pairs={{0,249},{1,8},{8,1},{9,16},{16,9},{17,24},{24,17},{25,32},{32,25},... | collective-permute-start | bytes 393224 | tf_op jit(solution)/shard_map/ppermute | solution.py:536
  10.5 8.4 %collective-permute-start.3 = (f32[16,128]{1,0:T(8,128)S(1)}, f32[16,128]{1,0:T(8,128)S(1)}, u32[]{:S(2)}, u32[]{:S(2)}) collective-permute-start(f32[16,128]{1,0:T(8,128)S(1)} %get-tuple-element.55), channel_id=1, source_target_pairs={{2,4},{4,2},{3,5},{5,3},{10,12},{12,10},{11,13},{13,11},{18,20},{2... | collective-permute-start | bytes 24584 | tf_op jit(solution)/shard_map/ppermute | solution.py:543
  11.2 8.8 %collective-permute-start.2 = (f32[16,128]{1,0:T(8,128)S(1)}, f32[16,128]{1,0:T(8,128)S(1)}, u32[]{:S(2)}, u32[]{:S(2)}) collective-permute-start(f32[16,128]{1,0:T(8,128)S(1)} %get-tuple-element.54), channel_id=1, source_target_pairs={{0,2},{2,0},{4,6},{6,4},{1,3},{3,1},{5,7},{7,5},{8,10},{10,8},{12,... | collective-permute-start | bytes 24584 | tf_op jit(solution)/shard_map/ppermute | solution.py:543
  21.5 5.8 %collective-permute-start.4 = (f32[144,128]{1,0:T(8,128)S(1)}, f32[144,128]{1,0:T(8,128)S(1)}, u32[]{:S(2)}, u32[]{:S(2)}) collective-permute-start(f32[144,128]{1,0:T(8,128)S(1)} %get-tuple-element.62), channel_id=1, source_target_pairs={{0,1},{1,0},{2,3},{3,2},{4,5},{5,4},{6,7},{7,6},{8,9},{9,8},{10,11... | collective-permute-start | bytes 221192 | tf_op jit(solution)/shard_map/ppermute | solution.py:572
  31.3 5.6 %collective-permute-start.9 = (f32[144,128]{1,0:T(8,128)S(1)}, f32[144,128]{1,0:T(8,128)S(1)}, u32[]{:S(2)}, u32[]{:S(2)}) collective-permute-start(f32[144,128]{1,0:T(8,128)S(1)} %add.73), channel_id=1, source_target_pairs={{0,32},{2,34},{4,36},{6,38},{8,40},{10,42},{12,44},{14,46},{16,48}... | collective-permute-start | bytes 221192 | tf_op jit(solution)/shard_map/ppermute | solution.py:560
  31.6 5.7 %collective-permute-start.10 = (f32[144,128]{1,0:T(8,128)S(1)}, f32[144,128]{1,0:T(8,128)S(1)}, u32[]{:S(2)}, u32[]{:S(2)}) collective-permute-start(f32[144,128]{1,0:T(8,128)S(1)} %add.73), channel_id=1, source_target_pairs={{0,48},{2,50},{4,52},{6,54},{8,56},{10,58},{12,60},{14,62},{16,32}... | collective-permute-start | bytes 221192 | tf_op jit(solution)/shard_map/ppermute | solution.py:560
  32.4 4.9 %collective-permute-start.8 = (f32[144,128]{1,0:T(8,128)S(1)}, f32[144,128]{1,0:T(8,128)S(1)}, u32[]{:S(2)}, u32[]{:S(2)}) collective-permute-start(f32[144,128]{1,0:T(8,128)S(1)} %add.73), channel_id=1, source_target_pairs={{0,16},{2,18},{4,20},{6,22},{8,24},{10,26},{12,28},{14,30},{16,0},... | collective-permute-start | bytes 221192 | tf_op jit(solution)/shard_map/ppermute | solution.py:560
  34.0 7.1 %collective-permute-start.6 = (f32[192,128]{1,0:T(8,128)S(1)}, f32[192,128]{1,0:T(8,128)S(1)}, u32[]{:S(2)}, u32[]{:S(2)}) collective-permute-start(f32[192,128]{1,0:T(8,128)S(1)} %get-tuple-element.65), channel_id=1, source_target_pairs={{0,1},{1,0},{2,3},{3,2},{4,5},{5,4},{6,7},{7,6},{8,9},{9,8},{10,11... | collective-permute-start | bytes 294920 | tf_op jit(solution)/shard_map/ppermute | solution.py:537
  35.7 5.4 %collective-permute-start.7 = (f32[192,128]{1,0:T(8,128)S(1)}, f32[192,128]{1,0:T(8,128)S(1)}, u32[]{:S(2)}, u32[]{:S(2)}) collective-permute-start(f32[192,128]{1,0:T(8,128)S(1)} %get-tuple-element.66), channel_id=1, source_target_pairs={{0,249},{1,8},{8,1},{9,16},{16,9},{17,24},{24,17},{25,32},{32,25},... | collective-permute-start | bytes 294920 | tf_op jit(solution)/shard_map/ppermute | solution.py:536
  37.3 4.8 %collective-permute-start.12 = (f32[144,128]{1,0:T(8,128)S(1)}, f32[144,128]{1,0:T(8,128)S(1)}, u32[]{:S(2)}, u32[]{:S(2)}) collective-permute-start(f32[144,128]{1,0:T(8,128)S(1)} %add_add_fusion.1), channel_id=1, source_target_pairs={{0,128},{2,130},{4,132},{6,134},{8,136},{10,138},{12,140},{14,142}... | collective-permute-start | bytes 221192 | tf_op jit(solution)/shard_map/ppermute | solution.py:560
  40.2 4.4 %collective-permute-start.13 = (f32[144,128]{1,0:T(8,128)S(1)}, f32[144,128]{1,0:T(8,128)S(1)}, u32[]{:S(2)}, u32[]{:S(2)}) collective-permute-start(f32[144,128]{1,0:T(8,128)S(1)} %add_add_fusion.1), channel_id=1, source_target_pairs={{0,192},{2,194},{4,196},{6,198},{8,200},{10,202},{12,204},{14,206}... | collective-permute-start | bytes 221192 | tf_op jit(solution)/shard_map/ppermute | solution.py:560
  45.2 10.0 %collective-permute-start.15 = (f32[160,128]{1,0:T(8,128)S(1)}, f32[160,128]{1,0:T(8,128)S(1)}, u32[]{:S(2)}, u32[]{:S(2)}) collective-permute-start(f32[160,128]{1,0:T(8,128)S(1)} %get-tuple-element.90), channel_id=1, source_target_pairs={{0,6},{2,4},{4,2},{6,0},{8,14},{10,12},{12,10},{14,8},{16,22},{18,... | collective-permute-start | bytes 245768 | tf_op jit(solution)/shard_map/ppermute | solution.py:560
  45.9 9.3 %collective-permute-start.14 = (f32[160,128]{1,0:T(8,128)S(1)}, f32[160,128]{1,0:T(8,128)S(1)}, u32[]{:S(2)}, u32[]{:S(2)}) collective-permute-start(f32[160,128]{1,0:T(8,128)S(1)} %get-tuple-element.89), channel_id=1, source_target_pairs={{0,2},{2,0},{4,6},{6,4},{8,10},{10,8},{12,14},{14,12},{16,18},{18,... | collective-permute-start | bytes 245768 | tf_op jit(solution)/shard_map/ppermute | solution.py:560
  48.8 6.5 %collective-permute-start.16 = (f32[144,128]{1,0:T(8,128)S(1)}, f32[144,128]{1,0:T(8,128)S(1)}, u32[]{:S(2)}, u32[]{:S(2)}) collective-permute-start(f32[144,128]{1,0:T(8,128)S(1)} %add_add_fusion), channel_id=1, source_target_pairs={{0,12},{2,14},{4,8},{6,10},{8,4},{10,6},{12,0},{14,2},{16,28},{18,... | collective-permute-start | bytes 221192 | tf_op jit(solution)/shard_map/ppermute | solution.py:560
  55.2 5.2 %collective-permute-start.17 = (f32[144,128]{1,0:T(8,128)S(1)}, f32[144,128]{1,0:T(8,128)S(1)}, u32[]{:S(2)}, u32[]{:S(2)}) collective-permute-start(f32[144,128]{1,0:T(8,128)S(1)} %fusion.refs_8_.with_area), channel_id=1, source_target_pairs={{0,1},{1,0},{2,3},{3,2},{4,5},{5,4},{6,7},{7,6},{8,9},{9,8},{10,11... | collective-permute-start | bytes 221192 | tf_op jit(solution)/shard_map/ppermute | solution.py:581
  63.3 4.8 %collective-permute-start.20 = (f32[136,128]{1,0:T(8,128)S(1)}, f32[136,128]{1,0:T(8,128)S(1)}, u32[]{:S(2)}, u32[]{:S(2)}) collective-permute-start(f32[136,128]{1,0:T(8,128)S(1)} %add.83), channel_id=1, source_target_pairs={{0,128},{2,130},{4,132},{6,134},{8,136},{10,138},{12,140},{14,142}... | collective-permute-start | bytes 208904 | tf_op jit(solution)/shard_map/ppermute | solution.py:560
  65.1 4.5 %collective-permute-start.21 = (f32[136,128]{1,0:T(8,128)S(1)}, f32[136,128]{1,0:T(8,128)S(1)}, u32[]{:S(2)}, u32[]{:S(2)}) collective-permute-start(f32[136,128]{1,0:T(8,128)S(1)} %add.83), channel_id=1, source_target_pairs={{0,192},{2,194},{4,196},{6,198},{8,200},{10,202},{12,204},{14,206}... | collective-permute-start | bytes 208904 | tf_op jit(solution)/shard_map/ppermute | solution.py:560
  69.6 7.1 %collective-permute-start.23 = (f32[136,128]{1,0:T(8,128)S(1)}, f32[136,128]{1,0:T(8,128)S(1)}, u32[]{:S(2)}, u32[]{:S(2)}) collective-permute-start(f32[136,128]{1,0:T(8,128)S(1)} %add_add_fusion.4), channel_id=1, source_target_pairs={{0,32},{2,34},{4,36},{6,38},{8,40},{10,42},{12,44},{14,46},{16,48}... | collective-permute-start | bytes 208904 | tf_op jit(solution)/shard_map/ppermute | solution.py:560
  71.6 5.3 %collective-permute-start.24 = (f32[136,128]{1,0:T(8,128)S(1)}, f32[136,128]{1,0:T(8,128)S(1)}, u32[]{:S(2)}, u32[]{:S(2)}) collective-permute-start(f32[136,128]{1,0:T(8,128)S(1)} %add_add_fusion.4), channel_id=1, source_target_pairs={{0,48},{2,50},{4,52},{6,54},{8,56},{10,58},{12,60},{14,62},{16,32}... | collective-permute-start | bytes 208904 | tf_op jit(solution)/shard_map/ppermute | solution.py:560
  77.3 5.7 %collective-permute-start.26 = (f32[136,128]{1,0:T(8,128)S(1)}, f32[136,128]{1,0:T(8,128)S(1)}, u32[]{:S(2)}, u32[]{:S(2)}) collective-permute-start(f32[136,128]{1,0:T(8,128)S(1)} %add_add_fusion.3), channel_id=1, source_target_pairs={{0,2},{2,0},{4,6},{6,4},{8,10},{10,8},{12,14},{14,12},{16,18},{18,... | collective-permute-start | bytes 208904 | tf_op jit(solution)/shard_map/ppermute | solution.py:560
  77.4 5.6 %collective-permute-start.27 = (f32[136,128]{1,0:T(8,128)S(1)}, f32[136,128]{1,0:T(8,128)S(1)}, u32[]{:S(2)}, u32[]{:S(2)}) collective-permute-start(f32[136,128]{1,0:T(8,128)S(1)} %add_add_fusion.3), channel_id=1, source_target_pairs={{0,10},{2,8},{4,14},{6,12},{8,2},{10,0},{12,6},{14,4},{16,26},{18,... | collective-permute-start | bytes 208904 | tf_op jit(solution)/shard_map/ppermute | solution.py:560
  84.2 5.5 %collective-permute-start.28 = (f32[136,128]{1,0:T(8,128)S(1)}, f32[136,128]{1,0:T(8,128)S(1)}, u32[]{:S(2)}, u32[]{:S(2)}) collective-permute-start(f32[136,128]{1,0:T(8,128)S(1)} %add_add_fusion.2), channel_id=1, source_target_pairs={{0,6},{2,4},{4,2},{6,0},{8,14},{10,12},{12,10},{14,8},{16,22},{18,... | collective-permute-start | bytes 208904 | tf_op jit(solution)/shard_map/ppermute | solution.py:560
  89.7 5.2 %collective-permute-start.29 = (f32[136,128]{1,0:T(8,128)S(1)}, f32[136,128]{1,0:T(8,128)S(1)}, u32[]{:S(2)}, u32[]{:S(2)}) collective-permute-start(f32[136,128]{1,0:T(8,128)S(1)} %add.93.part), channel_id=1, source_target_pairs={{0,1},{1,0},{2,3},{3,2},{4,5},{5,4},{6,7},{7,6},{8,9},{9,8},{10,11... | collective-permute-start | bytes 208904 | tf_op jit(solution)/shard_map/ppermute | solution.py:696
  (11 other events, 53.7 us)

commit v7 on v6

--- a/solution.py
+++ b/solution.py
@@ -607,7 +607,7 @@
     )
     blocks = pltpu.VMEM((16 * 8 * LEVELS, 128), f32)
     field_scratch = pltpu.VMEM((8 * LEVELS, FINE), f32)
-    sums = [pltpu.VMEM((4 * CHANNELS, FINE), f32), pltpu.VMEM((16 * 8 * LEVELS, 128), f32)]
+    sums = [pltpu.VMEM((4 * CHANNELS, FINE), f32), pltpu.VMEM((16 * 8 * LEVELS + 64, 128), f32)]
     wide = struct(2 * CHANNELS, COARSE)
     tile = struct(8, 128)
     with_area, without = struct(SUMMED + 8, 128), struct(SUMMED, 128)

time: 96 us -> 96 us (level)
  no operation moved by 1% of the time
where the time goes in v7:
time: 96 us; the launch traced here: 95.8 us
  starting transfers between devices  54.5 us (57%)
  waiting for transfers between devices  25.9 us (27%)
  Pallas kernels  14 us (15%)
    ppermute x20, starting transfers between devices, from_chip(): lax.ppermute(value, ('lon', 'lat'), [(i, i ^ mask) for i in range(count)])  26.1 us
    ppermute x20, waiting for transfers between devices, from_chip(): lax.ppermute(value, ('lon', 'lat'), [(i, i ^ mask) for i in range(count)])  18.5 us
    pallas_call x9, Pallas kernels, call(): pl.pallas_call(kernel, out_shape=outs, in_specs=specs, out_specs=[pl.Bloc...  14 us
    ppermute x1, starting transfers between devices, swap_lat(): lax.ppermute(near, 'lat', flipped('lat', 1))  7.76 us
    ppermute x2, starting transfers between devices, swap_lon(): return (lax.ppermute(inner, 'grp', flipped('grp', 1)), outer)  5 us
    ppermute x1, starting transfers between devices, sum_over_devices(): part = own + lax.ppermute(other, 'grp', flipped('grp', 1))  4.88 us
    ppermute x1, starting transfers between devices, shards(): back = lax.ppermute(part, 'grp', flipped('grp', 1))  4.29 us
    ppermute x1, starting transfers between devices, sum_over_devices(): back = lax.ppermute(part, 'grp', flipped('grp', 1))  4.26 us
  transfers between devices with their start and end apart: 30, of which 18 were waited for; matrix products, arithmetic and copies ran while one was open for 0% of the time, Pallas kernels for 8%

profile of v7, /device:TPU:1, one launch (start us, length us, event | category | flops | bytes accessed | tf_op | source)
XLA Modules:
  0.0 95.8 jit_solution(17923886185591647741)
XLA Ops:
  0.7 1.9 %shard_map.119 = (f32[96,128]{1,0:T(8,128)S(1)}, f32[96,128]{1,0:T(8,128)S(1)}, f32[8,128]{1,0:T(8,128)S(1)}, f32[8,512]{1,0:T(8,128)S(1)}, f32[256,128]{1,0:T(8,128)S(1)}, /*index=5*/f32[256,128]{1,0:T(8,128)S(1)}) custom-call(f32[96,512]{1,0:T(8,128)} %bitcast.18, f32[96,512]{1,0:T(8,128)} %bitcast.21, f32[96,512]{1,0:T(8,128)} %bitcast.15, ...), custom_call_target="tpu_custom_call" | custom-call | tf_op jit(solution)/shard_map/pallas_call | solution.py:44
  2.6 3.3 %collective-permute-start = (f32[256,128]{1,0:T(8,128)S(1)}, f32[256,128]{1,0:T(8,128)S(1)}, u32[]{:S(2)}, u32[]{:S(2)}) collective-permute-start(f32[256,128]{1,0:T(8,128)S(1)} %get-tuple-element.48), channel_id=1, source_target_pairs={{0,1},{1,0},{2,3},{3,2},{4,5},{5,4},{6,7},{7,6},{8,9},{9,8},{10,11... | collective-permute-start | bytes 393224 | tf_op jit(solution)/shard_map/ppermute | solution.py:537
  7.7 2.7 %collective-permute-done.1.x_outer.outer.refs_9_ = f32[256,128]{1,0:T(8,128)S(1)} collective-permute-done((f32[256,128]{1,0:T(8,128)S(1)}, f32[256,128]{1,0:T(8,128)S(1)}, u32[]{:S(2)}, u32[]{:S(2)}) %collective-permute-start.1) | collective-permute-done | bytes 131104 | tf_op jit(solution)/shard_map/ppermute | solution.py:536
  11.2 7.8 %collective-permute-start.2 = (f32[16,128]{1,0:T(8,128)S(1)}, f32[16,128]{1,0:T(8,128)S(1)}, u32[]{:S(2)}, u32[]{:S(2)}) collective-permute-start(f32[16,128]{1,0:T(8,128)S(1)} %get-tuple-element.54), channel_id=1, source_target_pairs={{0,2},{2,0},{4,6},{6,4},{1,3},{3,1},{5,7},{7,5},{8,10},{10,8},{12,... | collective-permute-start | bytes 24584 | tf_op jit(solution)/shard_map/ppermute | solution.py:543
  21.5 4.9 %collective-permute-start.4 = (f32[144,128]{1,0:T(8,128)S(1)}, f32[144,128]{1,0:T(8,128)S(1)}, u32[]{:S(2)}, u32[]{:S(2)}) collective-permute-start(f32[144,128]{1,0:T(8,128)S(1)} %get-tuple-element.62), channel_id=1, source_target_pairs={{0,1},{1,0},{2,3},{3,2},{4,5},{5,4},{6,7},{7,6},{8,9},{9,8},{10,11... | collective-permute-start | bytes 221192 | tf_op jit(solution)/shard_map/ppermute | solution.py:572
  27.4 3.8 %shard_map.123 = (f32[96,512]{1,0:T(8,128)S(1)}, f32[96,512]{1,0:T(8,128)S(1)}, f32[96,128]{1,0:T(8,128)S(1)}, f32[96,128]{1,0:T(8,128)S(1)}, f32[192,128]{1,0:T...) custom-call(f32[96,512]{1,0:T(8,128)} %bitcast.20, f32[96,512]{1,0:T(8,128)} %bitcast.23, ...), custom_call_target="tpu_custom_call" | custom-call | tf_op jit(solution)/shard_map/pallas_call | solution.py:44
  32.4 1.6 %collective-permute-start.8 = (f32[144,128]{1,0:T(8,128)S(1)}, f32[144,128]{1,0:T(8,128)S(1)}, u32[]{:S(2)}, u32[]{:S(2)}) collective-permute-start(f32[144,128]{1,0:T(8,128)S(1)} %add.73), channel_id=1, source_target_pairs={{0,16},{2,18},{4,20},{6,22},{8,24},{10,26},{12,28},{14,30},{16,0},... | collective-permute-start | bytes 221192 | tf_op jit(solution)/shard_map/ppermute | solution.py:560
  34.0 1.7 %collective-permute-start.6 = (f32[192,128]{1,0:T(8,128)S(1)}, f32[192,128]{1,0:T(8,128)S(1)}, u32[]{:S(2)}, u32[]{:S(2)}) collective-permute-start(f32[192,128]{1,0:T(8,128)S(1)} %get-tuple-element.65), channel_id=1, source_target_pairs={{0,1},{1,0},{2,3},{3,2},{4,5},{5,4},{6,7},{7,6},{8,9},{9,8},{10,11... | collective-permute-start | bytes 294920 | tf_op jit(solution)/shard_map/ppermute | solution.py:537
  37.3 2.8 %collective-permute-start.12 = (f32[144,128]{1,0:T(8,128)S(1)}, f32[144,128]{1,0:T(8,128)S(1)}, u32[]{:S(2)}, u32[]{:S(2)}) collective-permute-start(f32[144,128]{1,0:T(8,128)S(1)} %add_add_fusion.1), channel_id=1, source_target_pairs={{0,128},{2,130},{4,132},{6,134},{8,136},{10,138},{12,140},{14,142}... | collective-permute-start | bytes 221192 | tf_op jit(solution)/shard_map/ppermute | solution.py:560
  42.1 2.5 %collective-permute-done.13 = f32[144,128]{1,0:T(8,128)S(1)} collective-permute-done((f32[144,128]{1,0:T(8,128)S(1)}, f32[144,128]{1,0:T(8,128)S(1)}, u32[]{:S(2)}, u32[]{:S(2)}) %collective-permute-start.13) | collective-permute-done | bytes 73760 | tf_op jit(solution)/shard_map/ppermute | solution.py:560
  45.9 2.9 %collective-permute-start.14 = (f32[160,128]{1,0:T(8,128)S(1)}, f32[160,128]{1,0:T(8,128)S(1)}, u32[]{:S(2)}, u32[]{:S(2)}) collective-permute-start(f32[160,128]{1,0:T(8,128)S(1)} %get-tuple-element.89), channel_id=1, source_target_pairs={{0,2},{2,0},{4,6},{6,4},{8,10},{10,8},{12,14},{14,12},{16,18},{18,... | collective-permute-start | bytes 245768 | tf_op jit(solution)/shard_map/ppermute | solution.py:560
  48.8 2.9 %collective-permute-start.16 = (f32[144,128]{1,0:T(8,128)S(1)}, f32[144,128]{1,0:T(8,128)S(1)}, u32[]{:S(2)}, u32[]{:S(2)}) collective-permute-start(f32[144,128]{1,0:T(8,128)S(1)} %add_add_fusion), channel_id=1, source_target_pairs={{0,12},{2,14},{4,8},{6,10},{8,4},{10,6},{12,0},{14,2},{16,28},{18,... | collective-permute-start | bytes 221192 | tf_op jit(solution)/shard_map/ppermute | solution.py:560
  51.7 3.5 %collective-permute-done.16 = f32[144,128]{1,0:T(8,128)S(1)} collective-permute-done((f32[144,128]{1,0:T(8,128)S(1)}, f32[144,128]{1,0:T(8,128)S(1)}, u32[]{:S(2)}, u32[]{:S(2)}) %collective-permute-start.16) | collective-permute-done | bytes 73760 | tf_op jit(solution)/shard_map/ppermute | solution.py:560
  55.2 4.3 %collective-permute-start.17 = (f32[144,128]{1,0:T(8,128)S(1)}, f32[144,128]{1,0:T(8,128)S(1)}, u32[]{:S(2)}, u32[]{:S(2)}) collective-permute-start(f32[144,128]{1,0:T(8,128)S(1)} %fusion.refs_8_.with_area), channel_id=1, source_target_pairs={{0,1},{1,0},{2,3},{3,2},{4,5},{5,4},{6,7},{7,6},{8,9},{9,8},{10,11... | collective-permute-start | bytes 221192 | tf_op jit(solution)/shard_map/ppermute | solution.py:581
  63.3 1.8 %collective-permute-start.20 = (f32[136,128]{1,0:T(8,128)S(1)}, f32[136,128]{1,0:T(8,128)S(1)}, u32[]{:S(2)}, u32[]{:S(2)}) collective-permute-start(f32[136,128]{1,0:T(8,128)S(1)} %add.83), channel_id=1, source_target_pairs={{0,128},{2,130},{4,132},{6,134},{8,136},{10,138},{12,140},{14,142}... | collective-permute-start | bytes 208904 | tf_op jit(solution)/shard_map/ppermute | solution.py:560
  66.2 1.9 %collective-permute-done.20 = f32[136,128]{1,0:T(8,128)S(1)} collective-permute-done((f32[136,128]{1,0:T(8,128)S(1)}, f32[136,128]{1,0:T(8,128)S(1)}, u32[]{:S(2)}, u32[]{:S(2)}) %collective-permute-start.20) | collective-permute-done | bytes 69664 | tf_op jit(solution)/shard_map/ppermute | solution.py:560
  69.6 2.0 %collective-permute-start.23 = (f32[136,128]{1,0:T(8,128)S(1)}, f32[136,128]{1,0:T(8,128)S(1)}, u32[]{:S(2)}, u32[]{:S(2)}) collective-permute-start(f32[136,128]{1,0:T(8,128)S(1)} %add_add_fusion.4), channel_id=1, source_target_pairs={{0,32},{2,34},{4,36},{6,38},{8,40},{10,42},{12,44},{14,46},{16,48}... | collective-permute-start | bytes 208904 | tf_op jit(solution)/shard_map/ppermute | solution.py:560
  71.6 2.5 %collective-permute-start.24 = (f32[136,128]{1,0:T(8,128)S(1)}, f32[136,128]{1,0:T(8,128)S(1)}, u32[]{:S(2)}, u32[]{:S(2)}) collective-permute-start(f32[136,128]{1,0:T(8,128)S(1)} %add_add_fusion.4), channel_id=1, source_target_pairs={{0,48},{2,50},{4,52},{6,54},{8,56},{10,58},{12,60},{14,62},{16,32}... | collective-permute-start | bytes 208904 | tf_op jit(solution)/shard_map/ppermute | solution.py:560
  74.1 2.6 %shard_map.126 = (f32[96,512]{1,0:T(8,128)}, f32[96,512]{1,0:T(8,128)}) custom-call(f32[96,512]{1,0:T(8,128)S(1)} %get-tuple-element.75.refs_0_, f32[96,512]{1,0:T(8,128)S(1)} %get-tuple-element.76.refs_1_, f32[96,512]{1,0:T(8,128)S(1)} %bitcast.17, f32[96,512]{1,0:T(8,128)S(1)} %bitcast.14, f32[8,512]{1,0:T(8,128)S(1)} %get-tuple-element.46.mask.refs_4_, ...), custom_call_target="tpu_custom_call" | custom-call | tf_op jit(solution)/shard_map/pallas_call | solution.py:44
  77.4 2.7 %collective-permute-start.27 = (f32[136,128]{1,0:T(8,128)S(1)}, f32[136,128]{1,0:T(8,128)S(1)}, u32[]{:S(2)}, u32[]{:S(2)}) collective-permute-start(f32[136,128]{1,0:T(8,128)S(1)} %add_add_fusion.3), channel_id=1, source_target_pairs={{0,10},{2,8},{4,14},{6,12},{8,2},{10,0},{12,6},{14,4},{16,26},{18,... | collective-permute-start | bytes 208904 | tf_op jit(solution)/shard_map/ppermute | solution.py:560
  80.2 2.8 %collective-permute-done.26 = f32[136,128]{1,0:T(8,128)S(1)} collective-permute-done((f32[136,128]{1,0:T(8,128)S(1)}, f32[136,128]{1,0:T(8,128)S(1)}, u32[]{:S(2)}, u32[]{:S(2)}) %collective-permute-start.26) | collective-permute-done | bytes 69664 | tf_op jit(solution)/shard_map/ppermute | solution.py:560
  84.2 2.9 %collective-permute-start.28 = (f32[136,128]{1,0:T(8,128)S(1)}, f32[136,128]{1,0:T(8,128)S(1)}, u32[]{:S(2)}, u32[]{:S(2)}) collective-permute-start(f32[136,128]{1,0:T(8,128)S(1)} %add_add_fusion.2), channel_id=1, source_target_pairs={{0,6},{2,4},{4,2},{6,0},{8,14},{10,12},{12,10},{14,8},{16,22},{18,... | collective-permute-start | bytes 208904 | tf_op jit(solution)/shard_map/ppermute | solution.py:560
  87.0 2.7 %collective-permute-done.28 = f32[136,128]{1,0:T(8,128)S(1)} collective-permute-done((f32[136,128]{1,0:T(8,128)S(1)}, f32[136,128]{1,0:T(8,128)S(1)}, u32[]{:S(2)}, u32[]{:S(2)}) %collective-permute-start.28) | collective-permute-done | bytes 69664 | tf_op jit(solution)/shard_map/ppermute | solution.py:560
  89.7 4.3 %collective-permute-start.29 = (f32[136,128]{1,0:T(8,128)S(1)}, f32[136,128]{1,0:T(8,128)S(1)}, u32[]{:S(2)}, u32[]{:S(2)}) collective-permute-start(f32[136,128]{1,0:T(8,128)S(1)} %add.93.part), channel_id=1, source_target_pairs={{0,1},{1,0},{2,3},{3,2},{4,5},{5,4},{6,7},{7,6},{8,9},{9,8},{10,11... | collective-permute-start | bytes 208904 | tf_op jit(solution)/shard_map/ppermute | solution.py:696
  (73 shorter events, 22.2 us)
Async XLA Ops:
  2.6 5.1 %collective-permute-start = (f32[256,128]{1,0:T(8,128)S(1)}, f32[256,128]{1,0:T(8,128)S(1)}, u32[]{:S(2)}, u32[]{:S(2)}) collective-permute-start(f32[256,128]{1,0:T(8,128)S(1)} %get-tuple-element.48), channel_id=1, source_target_pairs={{0,1},{1,0},{2,3},{3,2},{4,5},{5,4},{6,7},{7,6},{8,9},{9,8},{10,11... | collective-permute-start | bytes 393224 | tf_op jit(solution)/shard_map/ppermute | solution.py:537
  5.9 4.5 %collective-permute-start.1 = (f32[256,128]{1,0:T(8,128)S(1)}, f32[256,128]{1,0:T(8,128)S(1)}, u32[]{:S(2)}, u32[]{:S(2)}) collective-permute-start(f32[256,128]{1,0:T(8,128)S(1)} %get-tuple-element.49), channel_id=1, source_target_pairs={{0,249},{1,8},{8,1},{9,16},{16,9},{17,24},{24,17},{25,32},{32,25},... | collective-permute-start | bytes 393224 | tf_op jit(solution)/shard_map/ppermute | solution.py:536
  10.5 8.4 %collective-permute-start.3 = (f32[16,128]{1,0:T(8,128)S(1)}, f32[16,128]{1,0:T(8,128)S(1)}, u32[]{:S(2)}, u32[]{:S(2)}) collective-permute-start(f32[16,128]{1,0:T(8,128)S(1)} %get-tuple-element.55), channel_id=1, source_target_pairs={{2,4},{4,2},{3,5},{5,3},{10,12},{12,10},{11,13},{13,11},{18,20},{2... | collective-permute-start | bytes 24584 | tf_op jit(solution)/shard_map/ppermute | solution.py:543
  11.2 8.8 %collective-permute-start.2 = (f32[16,128]{1,0:T(8,128)S(1)}, f32[16,128]{1,0:T(8,128)S(1)}, u32[]{:S(2)}, u32[]{:S(2)}) collective-permute-start(f32[16,128]{1,0:T(8,128)S(1)} %get-tuple-element.54), channel_id=1, source_target_pairs={{0,2},{2,0},{4,6},{6,4},{1,3},{3,1},{5,7},{7,5},{8,10},{10,8},{12,... | collective-permute-start | bytes 24584 | tf_op jit(solution)/shard_map/ppermute | solution.py:543
  21.5 5.8 %collective-permute-start.4 = (f32[144,128]{1,0:T(8,128)S(1)}, f32[144,128]{1,0:T(8,128)S(1)}, u32[]{:S(2)}, u32[]{:S(2)}) collective-permute-start(f32[144,128]{1,0:T(8,128)S(1)} %get-tuple-element.62), channel_id=1, source_target_pairs={{0,1},{1,0},{2,3},{3,2},{4,5},{5,4},{6,7},{7,6},{8,9},{9,8},{10,11... | collective-permute-start | bytes 221192 | tf_op jit(solution)/shard_map/ppermute | solution.py:572
  31.3 5.6 %collective-permute-start.9 = (f32[144,128]{1,0:T(8,128)S(1)}, f32[144,128]{1,0:T(8,128)S(1)}, u32[]{:S(2)}, u32[]{:S(2)}) collective-permute-start(f32[144,128]{1,0:T(8,128)S(1)} %add.73), channel_id=1, source_target_pairs={{0,32},{2,34},{4,36},{6,38},{8,40},{10,42},{12,44},{14,46},{16,48}... | collective-permute-start | bytes 221192 | tf_op jit(solution)/shard_map/ppermute | solution.py:560
  31.6 5.7 %collective-permute-start.10 = (f32[144,128]{1,0:T(8,128)S(1)}, f32[144,128]{1,0:T(8,128)S(1)}, u32[]{:S(2)}, u32[]{:S(2)}) collective-permute-start(f32[144,128]{1,0:T(8,128)S(1)} %add.73), channel_id=1, source_target_pairs={{0,48},{2,50},{4,52},{6,54},{8,56},{10,58},{12,60},{14,62},{16,32}... | collective-permute-start | bytes 221192 | tf_op jit(solution)/shard_map/ppermute | solution.py:560
  32.4 4.9 %collective-permute-start.8 = (f32[144,128]{1,0:T(8,128)S(1)}, f32[144,128]{1,0:T(8,128)S(1)}, u32[]{:S(2)}, u32[]{:S(2)}) collective-permute-start(f32[144,128]{1,0:T(8,128)S(1)} %add.73), channel_id=1, source_target_pairs={{0,16},{2,18},{4,20},{6,22},{8,24},{10,26},{12,28},{14,30},{16,0},... | collective-permute-start | bytes 221192 | tf_op jit(solution)/shard_map/ppermute | solution.py:560
  34.0 7.1 %collective-permute-start.6 = (f32[192,128]{1,0:T(8,128)S(1)}, f32[192,128]{1,0:T(8,128)S(1)}, u32[]{:S(2)}, u32[]{:S(2)}) collective-permute-start(f32[192,128]{1,0:T(8,128)S(1)} %get-tuple-element.65), channel_id=1, source_target_pairs={{0,1},{1,0},{2,3},{3,2},{4,5},{5,4},{6,7},{7,6},{8,9},{9,8},{10,11... | collective-permute-start | bytes 294920 | tf_op jit(solution)/shard_map/ppermute | solution.py:537
  35.7 5.4 %collective-permute-start.7 = (f32[192,128]{1,0:T(8,128)S(1)}, f32[192,128]{1,0:T(8,128)S(1)}, u32[]{:S(2)}, u32[]{:S(2)}) collective-permute-start(f32[192,128]{1,0:T(8,128)S(1)} %get-tuple-element.66), channel_id=1, source_target_pairs={{0,249},{1,8},{8,1},{9,16},{16,9},{17,24},{24,17},{25,32},{32,25},... | collective-permute-start | bytes 294920 | tf_op jit(solution)/shard_map/ppermute | solution.py:536
  37.3 4.8 %collective-permute-start.12 = (f32[144,128]{1,0:T(8,128)S(1)}, f32[144,128]{1,0:T(8,128)S(1)}, u32[]{:S(2)}, u32[]{:S(2)}) collective-permute-start(f32[144,128]{1,0:T(8,128)S(1)} %add_add_fusion.1), channel_id=1, source_target_pairs={{0,128},{2,130},{4,132},{6,134},{8,136},{10,138},{12,140},{14,142}... | collective-permute-start | bytes 221192 | tf_op jit(solution)/shard_map/ppermute | solution.py:560
  40.2 4.4 %collective-permute-start.13 = (f32[144,128]{1,0:T(8,128)S(1)}, f32[144,128]{1,0:T(8,128)S(1)}, u32[]{:S(2)}, u32[]{:S(2)}) collective-permute-start(f32[144,128]{1,0:T(8,128)S(1)} %add_add_fusion.1), channel_id=1, source_target_pairs={{0,192},{2,194},{4,196},{6,198},{8,200},{10,202},{12,204},{14,206}... | collective-permute-start | bytes 221192 | tf_op jit(solution)/shard_map/ppermute | solution.py:560
  45.2 10.0 %collective-permute-start.15 = (f32[160,128]{1,0:T(8,128)S(1)}, f32[160,128]{1,0:T(8,128)S(1)}, u32[]{:S(2)}, u32[]{:S(2)}) collective-permute-start(f32[160,128]{1,0:T(8,128)S(1)} %get-tuple-element.90), channel_id=1, source_target_pairs={{0,6},{2,4},{4,2},{6,0},{8,14},{10,12},{12,10},{14,8},{16,22},{18,... | collective-permute-start | bytes 245768 | tf_op jit(solution)/shard_map/ppermute | solution.py:560
  45.9 9.3 %collective-permute-start.14 = (f32[160,128]{1,0:T(8,128)S(1)}, f32[160,128]{1,0:T(8,128)S(1)}, u32[]{:S(2)}, u32[]{:S(2)}) collective-permute-start(f32[160,128]{1,0:T(8,128)S(1)} %get-tuple-element.89), channel_id=1, source_target_pairs={{0,2},{2,0},{4,6},{6,4},{8,10},{10,8},{12,14},{14,12},{16,18},{18,... | collective-permute-start | bytes 245768 | tf_op jit(solution)/shard_map/ppermute | solution.py:560
  48.8 6.5 %collective-permute-start.16 = (f32[144,128]{1,0:T(8,128)S(1)}, f32[144,128]{1,0:T(8,128)S(1)}, u32[]{:S(2)}, u32[]{:S(2)}) collective-permute-start(f32[144,128]{1,0:T(8,128)S(1)} %add_add_fusion), channel_id=1, source_target_pairs={{0,12},{2,14},{4,8},{6,10},{8,4},{10,6},{12,0},{14,2},{16,28},{18,... | collective-permute-start | bytes 221192 | tf_op jit(solution)/shard_map/ppermute | solution.py:560
  55.2 5.2 %collective-permute-start.17 = (f32[144,128]{1,0:T(8,128)S(1)}, f32[144,128]{1,0:T(8,128)S(1)}, u32[]{:S(2)}, u32[]{:S(2)}) collective-permute-start(f32[144,128]{1,0:T(8,128)S(1)} %fusion.refs_8_.with_area), channel_id=1, source_target_pairs={{0,1},{1,0},{2,3},{3,2},{4,5},{5,4},{6,7},{7,6},{8,9},{9,8},{10,11... | collective-permute-start | bytes 221192 | tf_op jit(solution)/shard_map/ppermute | solution.py:581
  63.3 4.8 %collective-permute-start.20 = (f32[136,128]{1,0:T(8,128)S(1)}, f32[136,128]{1,0:T(8,128)S(1)}, u32[]{:S(2)}, u32[]{:S(2)}) collective-permute-start(f32[136,128]{1,0:T(8,128)S(1)} %add.83), channel_id=1, source_target_pairs={{0,128},{2,130},{4,132},{6,134},{8,136},{10,138},{12,140},{14,142}... | collective-permute-start | bytes 208904 | tf_op jit(solution)/shard_map/ppermute | solution.py:560
  65.1 4.5 %collective-permute-start.21 = (f32[136,128]{1,0:T(8,128)S(1)}, f32[136,128]{1,0:T(8,128)S(1)}, u32[]{:S(2)}, u32[]{:S(2)}) collective-permute-start(f32[136,128]{1,0:T(8,128)S(1)} %add.83), channel_id=1, source_target_pairs={{0,192},{2,194},{4,196},{6,198},{8,200},{10,202},{12,204},{14,206}... | collective-permute-start | bytes 208904 | tf_op jit(solution)/shard_map/ppermute | solution.py:560
  69.6 7.1 %collective-permute-start.23 = (f32[136,128]{1,0:T(8,128)S(1)}, f32[136,128]{1,0:T(8,128)S(1)}, u32[]{:S(2)}, u32[]{:S(2)}) collective-permute-start(f32[136,128]{1,0:T(8,128)S(1)} %add_add_fusion.4), channel_id=1, source_target_pairs={{0,32},{2,34},{4,36},{6,38},{8,40},{10,42},{12,44},{14,46},{16,48}... | collective-permute-start | bytes 208904 | tf_op jit(solution)/shard_map/ppermute | solution.py:560
  71.6 5.3 %collective-permute-start.24 = (f32[136,128]{1,0:T(8,128)S(1)}, f32[136,128]{1,0:T(8,128)S(1)}, u32[]{:S(2)}, u32[]{:S(2)}) collective-permute-start(f32[136,128]{1,0:T(8,128)S(1)} %add_add_fusion.4), channel_id=1, source_target_pairs={{0,48},{2,50},{4,52},{6,54},{8,56},{10,58},{12,60},{14,62},{16,32}... | collective-permute-start | bytes 208904 | tf_op jit(solution)/shard_map/ppermute | solution.py:560
  77.3 5.7 %collective-permute-start.26 = (f32[136,128]{1,0:T(8,128)S(1)}, f32[136,128]{1,0:T(8,128)S(1)}, u32[]{:S(2)}, u32[]{:S(2)}) collective-permute-start(f32[136,128]{1,0:T(8,128)S(1)} %add_add_fusion.3), channel_id=1, source_target_pairs={{0,2},{2,0},{4,6},{6,4},{8,10},{10,8},{12,14},{14,12},{16,18},{18,... | collective-permute-start | bytes 208904 | tf_op jit(solution)/shard_map/ppermute | solution.py:560
  77.4 5.6 %collective-permute-start.27 = (f32[136,128]{1,0:T(8,128)S(1)}, f32[136,128]{1,0:T(8,128)S(1)}, u32[]{:S(2)}, u32[]{:S(2)}) collective-permute-start(f32[136,128]{1,0:T(8,128)S(1)} %add_add_fusion.3), channel_id=1, source_target_pairs={{0,10},{2,8},{4,14},{6,12},{8,2},{10,0},{12,6},{14,4},{16,26},{18,... | collective-permute-start | bytes 208904 | tf_op jit(solution)/shard_map/ppermute | solution.py:560
  84.2 5.5 %collective-permute-start.28 = (f32[136,128]{1,0:T(8,128)S(1)}, f32[136,128]{1,0:T(8,128)S(1)}, u32[]{:S(2)}, u32[]{:S(2)}) collective-permute-start(f32[136,128]{1,0:T(8,128)S(1)} %add_add_fusion.2), channel_id=1, source_target_pairs={{0,6},{2,4},{4,2},{6,0},{8,14},{10,12},{12,10},{14,8},{16,22},{18,... | collective-permute-start | bytes 208904 | tf_op jit(solution)/shard_map/ppermute | solution.py:560
  89.7 5.2 %collective-permute-start.29 = (f32[136,128]{1,0:T(8,128)S(1)}, f32[136,128]{1,0:T(8,128)S(1)}, u32[]{:S(2)}, u32[]{:S(2)}) collective-permute-start(f32[136,128]{1,0:T(8,128)S(1)} %add.93.part), channel_id=1, source_target_pairs={{0,1},{1,0},{2,3},{3,2},{4,5},{5,4},{6,7},{7,6},{8,9},{9,8},{10,11... | collective-permute-start | bytes 208904 | tf_op jit(solution)/shard_map/ppermute | solution.py:696
  (11 other events, 53.7 us)
